TPU v7x, 512 devices: a whole 4x8x8 slice. The times are simulated.
512 devices in a mesh: dp: 32 (over z, x), vocab: 16 (over y, core).
Axes of the slice: x: 4, y: 8, z: 8, core: 2. Of those that a mesh axis runs over, the one named last changes fastest.
Arguments:
- student_hidden: bfloat16 [16384, 4096], P(('dp', 'vocab')), may hold values from -16 to 16
- teacher_hidden: bfloat16 [16384, 4096], P(('dp', 'vocab')), may hold values from -16 to 16
- packing: int32 [16384], P(('dp', 'vocab')), may hold values from 0 to 16383, as said below
- token_mask: int32 [16384], P(('dp', 'vocab')), may hold values from 0 to 1
- student_head: bfloat16 [4096, 4096], P(None, 'vocab'), may hold values from -3 to 3
- teacher_head: bfloat16 [4096, 4096], P(None, 'vocab'), may hold values from -3 to 3
- loss_scale: float32 [], replicated, may hold values from 32768 to 131072
Outputs:
- hidden_grad: bfloat16 [16384, 4096], P(('dp', 'vocab'))
- loss: float32 [], replicated
Inputs may be any that keep to these rules, and one draw needn't show every extreme that they name: At least one slot has token_mask 1. A permutation of the slots. Rollout row t and slot packing[t] lie on devices with the same vocab index (device of a row or slot: its index // 32, in dp-major order). Each device's rows go at most 2 to the devices of one dp index, and exactly 2 to one of them.
All inputs are finite; a program needn't handle non-finite values.
Results may differ from a plain program's by a relative error of at most 0.022.
Values may be sent and summed in bfloat16 or wider, within the bound.
No kernel may reach another device: no remote copies, remote signals or barrier semaphores. Data moves between devices by JAX's collectives and lax.ppermute only.
A program may use at most 64 MiB of HBM per device.

v0:
```python
import jax
import jax.numpy as jnp
from jax import lax
from jax.sharding import PartitionSpec as P


def body(
    student_hidden, teacher_hidden, packing, token_mask, student_head, teacher_head, loss_scale
):
    tok_rows = student_hidden.shape[0]
    width = student_hidden.shape[1]
    dp_count = lax.axis_size("dp")
    vocab_count = lax.axis_size("vocab")
    capacity = max(2, 2 * tok_rows // dp_count)
    destination = packing // (vocab_count * tok_rows)
    slot_local = packing % tok_rows
    one_hot = (destination[:, None] == jnp.arange(dp_count, dtype=jnp.int32)[None, :]).astype(
        jnp.int32
    )
    order_rank = jnp.sum(jnp.cumsum(one_hot, axis=0) * one_hot, axis=1) - 1
    position = destination * capacity + order_rank
    send_rows = (
        jnp.zeros((dp_count * capacity, width), jnp.bfloat16).at[position].set(teacher_hidden)
    )
    send_slots = jnp.full((dp_count * capacity,), tok_rows, jnp.int32).at[position].set(slot_local)
    got_rows, got_slots = (
        lax.all_to_all(
            send_rows.reshape(dp_count, capacity, width),
            "dp",
            split_axis=0,
            concat_axis=0,
            tiled=True,
        ),
        lax.all_to_all(
            send_slots.reshape(dp_count, capacity), "dp", split_axis=0, concat_axis=0, tiled=True
        ),
    )
    placed = (
        jnp.zeros((tok_rows + 1, width), jnp.bfloat16)
        .at[got_slots.reshape(-1)]
        .set(got_rows.reshape(dp_count * capacity, width))[:tok_rows]
    )
    group_student, group_teacher, group_mask = (
        lax.all_gather(student_hidden, "vocab", axis=0, tiled=True),
        lax.all_gather(placed, "vocab", axis=0, tiled=True),
        lax.all_gather(token_mask, "vocab", axis=0, tiled=True),
    )
    student_logits = jnp.dot(group_student, student_head, preferred_element_type=jnp.float32)
    teacher_logits = jnp.dot(group_teacher, teacher_head, preferred_element_type=jnp.float32)
    difference = student_logits - teacher_logits
    student_top, teacher_top = lax.pmax(
        (jnp.max(student_logits, axis=1), jnp.max(teacher_logits, axis=1)), "vocab"
    )
    student_exp = jnp.exp(student_logits - student_top[:, None])
    teacher_exp = jnp.exp(teacher_logits - teacher_top[:, None])
    student_sum, teacher_sum, cross_sum = lax.psum(
        (
            jnp.sum(student_exp, axis=1),
            jnp.sum(teacher_exp, axis=1),
            jnp.sum(student_exp * difference, axis=1),
        ),
        "vocab",
    )
    student_lse = student_top + jnp.log(student_sum)
    teacher_lse = teacher_top + jnp.log(teacher_sum)
    row_kl = cross_sum / student_sum - student_lse + teacher_lse
    weights = group_mask.astype(jnp.float32)
    counted = lax.psum(jnp.sum(token_mask.astype(jnp.float32)), ("dp", "vocab"))
    kl_total = lax.psum(jnp.sum(weights * row_kl), "dp")
    loss = kl_total / counted
    log_ps = student_logits - student_lse[:, None]
    log_pt = teacher_logits - teacher_lse[:, None]
    factor = loss_scale * weights / counted
    logit_grad = (factor[:, None] * jnp.exp(log_ps) * (log_ps - log_pt - row_kl[:, None])).astype(
        jnp.bfloat16
    )
    summed = lax.psum_scatter(
        lax.dot_general(
            logit_grad, student_head, (((1,), (1,)), ((), ())), preferred_element_type=jnp.float32
        ).astype(jnp.bfloat16),
        "vocab",
        scatter_dimension=0,
        tiled=True,
    )
    return (summed, loss)


def solution(mesh):
    return jax.shard_map(
        body,
        mesh=mesh,
        in_specs=(
            P(("dp", "vocab"), None),
            P(("dp", "vocab"), None),
            P(("dp", "vocab")),
            P(("dp", "vocab")),
            P(None, "vocab"),
            P(None, "vocab"),
            P(),
        ),
        out_specs=(P(("dp", "vocab"), None), P()),
        check_vma=False,
    )
```

profile of v0, /device:TPU:6, one launch (start us, length us, event | category | flops | bytes accessed | tf_op | source)
XLA Modules:
  0.0 303.5 jit_solution(2940728268002782816)
XLA Ops:
  7.2 0.0 copy-start
  7.2 0.0 copy-start.1
  7.2 0.0 all-gather.3.cloned.1.call-start
  7.2 0.7 all-gather.3.cloned.1.call-update
  7.9 0.7 and_select_fusion
  8.6 0.1 fusion.9
  8.7 0.1 reduce_window_sum.11
  8.7 0.2 select_reduce_fusion
  8.9 0.7 scatter_custom_fusion
  9.6 0.7 all_to_all.9
  10.3 13.4 %all-to-all-start = ((s32[32,1,2]{2,1,0:T(1,128)}), s32[32,1,2]{2,1,0:T(1,128)S(1)}, u32[]{:S(2)}, u32[]{:S(2)}) async-start(s32[32,1,2]{2,1,0:T(1,128)} %bitcast.1), calls=%async_computation | async-start | bytes 32768 | tf_op jit(solution)/shard_map/all_to_all | solution.py:34
  23.7 1.6 scatter_custom_fusion.1
  25.3 1.1 reshape.54
  26.4 5.2 %all-to-all-done = s32[32,1,2]{2,1,0:T(1,128)S(1)} async-done(((s32[32,1,2]{2,1,0:T(1,128)}), s32[32,1,2]{2,1,0:T(1,128)S(1)}, u32[]{:S(2)}, u32[]{:S(2)}) %all-to-all-start) | async-done | bytes 288 | tf_op jit(solution)/shard_map/all_to_all | solution.py:34
  31.6 5.6 %all-to-all-start.1 = ((bf16[32,2,4096]{2,1,0:T(2,128)(2,1)}), bf16[32,2,4096]{2,1,0:T(2,128)(2,1)S(1)}, u32[]{:S(2)}, u32[]{:S(2)}) async-start(bf16[32,2,4096]{2,1,0:T(2,128)(2,1)} %reshape.54), calls=%async_computation.1 | async-start | bytes 1048576 | tf_op jit(solution)/shard_map/all_to_all | solution.py:27
  37.2 0.0 all-gather.5.cloned.1.call-start
  37.2 0.5 broadcast.57
  37.7 0.7 reduce.3
  38.4 0.1 reshape.53
  38.6 14.4 %all-to-all-done.1 = bf16[32,2,4096]{2,1,0:T(2,128)(2,1)S(1)} async-done(((bf16[32,2,4096]{2,1,0:T(2,128)(2,1)}), bf16[32,2,4096]{2,1,0:T(2,128)(2,1)S(1)}, u32[]{:S(2)}, u32[]{:S(2)}) %all-to-all-start.1) | async-done | bytes 524320 | tf_op jit(solution)/shard_map/all_to_all | solution.py:27
  52.9 0.2 reshape.76
  53.1 1.4 scatter_custom_fusion.2
  54.5 0.7 slice.4
  55.2 0.0 all-gather.5.cloned.1.call-update
  55.3 0.0 reduce-scatter.2.cloned.1.call-start
  55.3 0.0 copy-done.1
  55.3 0.6 convert_reduce_fusion
  55.9 96.0 %psum.35 = f32[]{:T(128)} all-reduce(f32[]{:T(128)} %convert_reduce_fusion), channel_id=1, replica_groups=mesh['dp'=32,'vocab'=16] {'dp','vocab'}, use_global_device_ids=true, to_apply=%region_1.2 | all-reduce | flops 1 | bytes 8 | tf_op jit(solution)/shard_map/psum | solution.py:68
  152.6 1.3 dynamic-slice
  154.5 0.2 dynamic-update-slice
  154.7 11.9 %all-reduce = s32[512]{0:T(512)S(1)} all-reduce(s32[512]{0:T(512)S(1)} %dynamic-update-slice), channel_id=1, replica_groups=mesh['dp'=32,'vocab'=16] {'vocab'}, use_global_device_ids=true, to_apply=%add | all-reduce | flops 512 | bytes 4096
  166.7 0.0 all-gather.3.cloned.1.call-done
  166.7 0.0 copy-done
  166.7 3.5 %fusion.14 = (f32[512]{0:T(512)S(1)}, f32[512,256]{0,1:T(8,128)S(1)}) fusion(bf16[512,4096]{1,0:T(8,128)(2,1)} %all-gather.3.cloned.1.call-done, bf16[4096,256]{1,0:T(8,128)(2,1)S(1)} %copy-done), kind=kOutput, calls=%fused_computation.38 | convolution fusion | flops 1073872384 | bytes 6817792 | tf_op jit(solution)/shard_map/dot_general | solution.py:48
  170.2 0.0 all-gather.5.cloned.1.call-done
  170.2 4.2 %fusion.13 = (f32[512]{0:T(512)S(1)}, f32[512,256]{0,1:T(8,128)S(1)}) fusion(bf16[512,4096]{1,0:T(8,128)(2,1)} %all-gather.5.cloned.1.call-done, bf16[4096,256]{1,0:T(8,128)(2,1)} %param.12), kind=kOutput, calls=%fused_computation.37 | convolution fusion | flops 1073872384 | bytes 6817792 | tf_op jit(solution)/shard_map/dot_general | solution.py:49
  174.4 23.5 %all-reduce.2 = (f32[512]{0:T(512)S(1)}, f32[512]{0:T(512)S(1)}) all-reduce(f32[512]{0:T(512)S(1)} %get-tuple-element.17, f32[512]{0:T(512)S(1)} %get-tuple-element.19), channel_id=1, replica_groups=mesh['dp'=32,'vocab'=16] {'vocab'}, use_global_device_ids=true, to_apply=%region_12.13 | all-reduce | flops 1024 | bytes 8192 | tf_op jit(solution)/shard_map/pmax | solution.py:51
  197.9 0.2 fusion
  198.1 24.0 %all-reduce.1 = (f32[512]{0:T(512)S(1)}, f32[512]{0:T(512)S(1)}, f32[512]{0:T(512)S(1)}) all-reduce(f32[512]{0:T(512)S(1)} %get-tuple-element.4, f32[512]{0:T(512)S(1)} %get-tuple-element.3, f32[512]{0:T(512)S(1)} %get-tuple-element.2), channel_id=1, replica_groups=mesh['dp'=32,'vocab'=16] {'vocab'}, use_global_device_ids=true, to_apply=%region_14.15 | all-reduce | flops 1536 | bytes 12288 | tf_op jit(solution)/shard_map/psum | solution.py:56
  222.2 1.2 multiply_reduce_fusion.1
  223.3 3.3 %convolution_convert_fusion = bf16[512,4096]{1,0:T(8,128)(2,1)} fusion(bf16[4096,256]{1,0:T(8,128)(2,1)S(1)} %copy-done, f32[512,256]{0,1:T(8,128)S(1)} %get-tuple-element.18, f32[512,256]{0,1:T(8,128)S(1)} %get-tuple-element.20, f32[512]{0:T(512)S(1)} %get-tuple-element.11, f32[512]{0:T(512)S(1)} %get-tuple-element.12, f32[512]{0:T(512)S(1)} %get-tuple-element.13, ...), kind=kOutput, calls=%fused_computation.3 | convolution fusion | flops 1076756480 | bytes 7348224 | tf_op jit(solution)/shard_map/dot_general | solution.py:78
  226.6 0.0 reduce-scatter.2.cloned.1.call-update
  226.6 67.9 %psum.39 = f32[]{:T(128)} all-reduce(f32[]{:T(128)} %get-tuple-element.10), channel_id=1, replica_groups=mesh['dp'=32,'vocab'=16] {'dp'}, use_global_device_ids=true, to_apply=%region_19.20 | all-reduce | flops 1 | bytes 8 | tf_op jit(solution)/shard_map/psum | solution.py:69
  295.8 0.0 reduce-scatter.2.cloned.1.call-done
  (3 shorter events, 0.0 us)
Async XLA Ops:
  7.2 159.5 %copy-start = (bf16[4096,256]{1,0:T(8,128)(2,1)S(1)}, bf16[4096,256]{1,0:T(8,128)(2,1)}, u32[]{:S(2)}) copy-start(bf16[4096,256]{1,0:T(8,128)(2,1)} %param.11) | copy-start | bytes 6291460
  7.2 48.1 %copy-start.1 = (s32[32]{0:T(128)S(1)}, s32[32]{0:T(128)}, u32[]{:S(2)}) copy-start(s32[32]{0:T(128)} %param.10) | copy-start | bytes 388
  7.2 159.5 %all-gather.3.cloned.1.call-start = ((), (), s32[]{:S(2)}) async-start(), calls=%async_computation.3 | async-start | bytes 4456448 | tf_op jit(solution)/shard_map/all_gather | solution.py:44
  10.3 21.3 %all-to-all-start = ((s32[32,1,2]{2,1,0:T(1,128)}), s32[32,1,2]{2,1,0:T(1,128)S(1)}, u32[]{:S(2)}, u32[]{:S(2)}) async-start(s32[32,1,2]{2,1,0:T(1,128)} %bitcast.1), calls=%async_computation | async-start | bytes 32768 | tf_op jit(solution)/shard_map/all_to_all | solution.py:34
  31.6 21.3 %all-to-all-start.1 = ((bf16[32,2,4096]{2,1,0:T(2,128)(2,1)}), bf16[32,2,4096]{2,1,0:T(2,128)(2,1)S(1)}, u32[]{:S(2)}, u32[]{:S(2)}) async-start(bf16[32,2,4096]{2,1,0:T(2,128)(2,1)} %reshape.54), calls=%async_computation.1 | async-start | bytes 1048576 | tf_op jit(solution)/shard_map/all_to_all | solution.py:27
  37.2 133.0 %all-gather.5.cloned.1.call-start = ((), (), s32[]{:S(2)}) async-start(), calls=%async_computation.4 | async-start | bytes 4456448 | tf_op jit(solution)/shard_map/all_gather | solution.py:45
  55.3 240.5 %reduce-scatter.2.cloned.1.call-start = ((), (), s32[]{:S(2)}) async-start(), calls=%async_computation.5 | async-start | bytes 4456448 | tf_op jit(solution)/shard_map/reduce_scatter | solution.py:77
Sparse Core Ops, SparseCore 0:
  10.1 49.1 all-gather.2
  62.0 44.3 all-gather.4
  226.7 61.6 reduce-scatter.1
where the time goes:
time: 308 us; the launch traced here: 303 us
  blocking collectives  223 us (72%)
  waiting for transfers between devices  20.3 us (7%)
  starting transfers between devices  19.1 us (6%)
  between operations  17.6 us (6%)
  matrix products  10.9 us (4%)
  local copies, waits for them, and re-layouts  8.51 us (3%)
  other arithmetic  3.67 us (1%)
    psum x1, blocking collectives, body(): counted = lax.psum(jnp.sum(token_mask.astype(jnp.float32)), ('dp', 'vocab'))  96 us
    psum x1, blocking collectives, body(): kl_total = lax.psum(jnp.sum(weights * row_kl), 'dp')  67.9 us
    psum x1, blocking collectives, body(): lax.psum((jnp.sum(student_exp, axis=1), jnp.sum(teacher_exp, axis=1), jnp...  24 us
    pmax x1, blocking collectives, body(): lax.pmax((jnp.max(student_logits, axis=1), jnp.max(teacher_logits, axis=1...  23.5 us
    all_to_all x1, waiting for transfers between devices, body(): lax.all_to_all(send_rows.reshape(dp_count, capacity, width), 'dp', split_...  14.4 us
    all_to_all x1, starting transfers between devices, body(): lax.all_to_all(send_slots.reshape(dp_count, capacity), 'dp', split_axis=0...  13.4 us
    unnamed x1, blocking collectives  11.9 us
  transfers between devices with their start and end apart: 5, of which 2 were waited for; matrix products, arithmetic and copies ran while one was open for 4% of the time, Pallas kernels for 0%

commit v1 on v0

v1 whole, which is shorter than its diff:
```python
import jax
import jax.numpy as jnp
from jax import lax
from jax.sharding import Mesh, PartitionSpec as P

BF = jnp.bfloat16
F32 = jnp.float32
CORES = 2


def dot(a, b, ca, cb):
    return lax.dot_general(a, b, (((ca,), (cb,)), ((), ())), preferred_element_type=F32)


def exchange(x, axis):
    return lax.all_to_all(x, axis, split_axis=0, concat_axis=0, tiled=True)


def body(student_hidden, teacher_hidden, packing, token_mask, student_head, teacher_head, loss_scale):
    tok, width = student_hidden.shape
    n_dp, n_y = lax.axis_size("dp"), lax.axis_size("y")
    cap = max(2, 2 * tok // n_dp)
    rows = n_y * tok
    swap = [(0, 1), (1, 0)]

    student_rows = exchange(
        jnp.broadcast_to(student_hidden[None], (n_y, tok, width)), "y"
    ).reshape(rows, width)

    destination = packing // (n_y * CORES * tok)
    local = packing % tok
    index = jnp.arange(tok, dtype=jnp.int32)
    earlier = (destination[:, None] == destination[None, :]) & (index[None, :] < index[:, None])
    rank = jnp.sum(earlier.astype(jnp.int32), axis=1)
    position = destination * cap + rank
    spread = (jnp.arange(n_dp * cap, dtype=jnp.int32)[:, None] == position[None, :]).astype(BF)
    payload = jnp.concatenate(
        [teacher_hidden, jnp.broadcast_to((local + 1).astype(BF)[:, None], (tok, 128))], axis=1
    )
    send = dot(spread, payload, 1, 0).astype(BF)
    got = exchange(send.reshape(n_dp, cap, width + 128), "dp").reshape(n_dp * cap, width + 128)
    slots = got[:, width].astype(jnp.int32) - 1
    place = (lax.rem(jnp.arange(rows, dtype=jnp.int32), tok)[:, None] == slots[None, :]).astype(BF)
    placed = dot(place, got[:, :width], 1, 0).astype(BF)
    teacher_rows = exchange(placed.reshape(n_y, tok, width), "y").reshape(rows, width)

    student_both = jnp.concatenate(
        [student_head, lax.ppermute(student_head, "core", swap)], axis=1
    )
    teacher_both = jnp.concatenate(
        [teacher_head, lax.ppermute(teacher_head, "core", swap)], axis=1
    )

    student_logits = dot(student_rows, student_both, 1, 0)
    teacher_logits = dot(teacher_rows, teacher_both, 1, 0)
    difference = student_logits - teacher_logits
    student_top = jnp.max(student_logits, axis=1)
    teacher_top = jnp.max(teacher_logits, axis=1)
    student_exp = jnp.exp(student_logits - student_top[:, None])
    teacher_exp = jnp.exp(teacher_logits - teacher_top[:, None])
    own_mask = jnp.pad(token_mask.astype(F32), (0, rows - tok))
    stats = jnp.stack(
        [
            student_top,
            teacher_top,
            jnp.sum(student_exp, axis=1),
            jnp.sum(teacher_exp, axis=1),
            jnp.sum(student_exp * difference, axis=1),
            own_mask,
        ]
    )
    stats = exchange(jnp.broadcast_to(stats[None], (n_y,) + stats.shape), "y")
    student_max = jnp.max(stats[:, 0], axis=0)
    teacher_max = jnp.max(stats[:, 1], axis=0)
    student_scale = jnp.exp(stats[:, 0] - student_max[None])
    teacher_scale = jnp.exp(stats[:, 1] - teacher_max[None])
    student_sum = jnp.sum(stats[:, 2] * student_scale, axis=0)
    teacher_sum = jnp.sum(stats[:, 3] * teacher_scale, axis=0)
    mean_difference = jnp.sum(stats[:, 4] * student_scale, axis=0) / student_sum
    row_kl = (
        mean_difference
        - (student_max + jnp.log(student_sum))
        + (teacher_max + jnp.log(teacher_sum))
    )
    weights = stats[:, 5, :tok].reshape(rows)

    parts = jnp.stack([jnp.sum(weights * row_kl), jnp.sum(weights)])
    parts = jnp.broadcast_to(jnp.pad(parts, (0, 126))[None, None], (n_dp * CORES, 1, 128))
    totals = jnp.sum(exchange(parts, ("dp", "core")), axis=(0, 1))
    counted = totals[1]
    loss = totals[0] / counted

    probs = jnp.exp(student_logits - student_max[:, None]) / student_sum[:, None]
    grad = (probs * (difference - mean_difference[:, None])).astype(BF)
    partial = dot(grad, student_both, 1, 1).astype(BF)
    blocks = exchange(partial.reshape(n_y, tok, width), "y")
    factor = loss_scale * token_mask.astype(F32) / counted
    hidden_grad = (factor[:, None] * jnp.sum(blocks.astype(F32), axis=0)).astype(BF)
    return hidden_grad, loss


def solution(mesh):
    dp, vocab = mesh.devices.shape
    grid = Mesh(mesh.devices.reshape(dp, vocab // CORES, CORES), ("dp", "y", "core"))
    every = ("dp", "y", "core")
    return jax.shard_map(
        body,
        mesh=grid,
        in_specs=(
            P(every, None),
            P(every, None),
            P(every),
            P(every),
            P(None, ("y", "core")),
            P(None, ("y", "core")),
            P(),
        ),
        out_specs=(P(every, None), P()),
        check_vma=False,
    )
```

time: 308 us -> 240 us (0.78)
  blocking collectives: 223 us -> 44.1 us
  waiting for transfers between devices: 20.3 us -> 136 us
  between operations: 17.6 us -> 3.95 us
  starting transfers between devices: 19.1 us -> 25.4 us
    psum x3 -> x0, blocking collectives: 188 us -> none  [the longest x1 96 us: body(): counted = lax.psum(jnp.sum(token_mask.astype(jnp.float32)), ('dp', 'vocab'))]
    all_to_all x2 -> x4, waiting for transfers between devices: 19.6 us -> 134 us  [exchange(): return lax.all_to_all(x, axis, split_axis=0, concat_axis=0, tiled=True)]
    all_to_all x0 -> x2, blocking collectives: none -> 44.1 us  [exchange(): return lax.all_to_all(x, axis, split_axis=0, concat_axis=0, tiled=True)]
    pmax x1 -> x0, blocking collectives: 23.5 us -> none  [body(): lax.pmax((jnp.max(student_logits, axis=1), jnp.max(teacher_logits, axis=1...]
    unnamed x1 -> x0, blocking collectives: 11.9 us -> none
    ppermute x0 -> x2, starting transfers between devices: none -> 4.33 us  [the longest x1 2.4 us: body(): lax.ppermute(teacher_head, 'core', swap)]
    scatter x3 -> x0, local copies, waits for them, and re-layouts: 3.6 us -> none  [the longest x1 1.55 us: body(): jnp.zeros((dp_count * capacity, width), jnp.bfloat16).at[position]]
    dot_general x3 -> x5, matrix products: 10.9 us -> 13.7 us  [dot(): lax.dot_general(a, b, (((ca,), (cb,)), ((), ())), preferred_element_type=...]
  transfers between devices with their start and end apart: 5 -> 6, of which waited for: 2 -> 6; matrix products, arithmetic and copies ran while one was open for 4% -> 4% of each run, Pallas kernels for 0% -> 0%
where the time goes in v1:
time: 240 us; the launch traced here: 235 us
  waiting for transfers between devices  136 us (57%)
  blocking collectives  44.1 us (18%)
  starting transfers between devices  25.4 us (11%)
  matrix products  13.7 us (6%)
  local copies, waits for them, and re-layouts  5.85 us (2%)
  other arithmetic  5.83 us (2%)
  between operations  3.95 us (2%)
    all_to_all x4, waiting for transfers between devices, exchange(): return lax.all_to_all(x, axis, split_axis=0, concat_axis=0, tiled=True)  134 us
    all_to_all x2, blocking collectives, exchange(): return lax.all_to_all(x, axis, split_axis=0, concat_axis=0, tiled=True)  44.1 us
    all_to_all x4, starting transfers between devices, exchange(): return lax.all_to_all(x, axis, split_axis=0, concat_axis=0, tiled=True)  21 us
    dot_general x5, matrix products, dot(): lax.dot_general(a, b, (((ca,), (cb,)), ((), ())), preferred_element_type=...  13.7 us
  transfers between devices with their start and end apart: 6, of which 6 were waited for; matrix products, arithmetic and copies ran while one was open for 4% of the time, Pallas kernels for 0%

profile of v1, /device:TPU:6, one launch (start us, length us, event | category | flops | bytes accessed | tf_op | source)
XLA Modules:
  0.0 235.0 jit_solution(6248684636238445199)
XLA Ops:
  0.6 0.0 copy-start.4
  0.6 0.7 and_select_fusion.1
  1.3 0.2 convert_reduce_fusion.1
  1.5 0.1 broadcast_in_dim.9
  1.6 1.2 convolution_convert_fusion
  2.8 0.2 reshape.126
  3.1 30.4 %all_to_all.30 = bf16[32,2,4224]{2,1,0:T(2,128)(2,1)S(1)} all-to-all(bf16[32,2,4224]{2,1,0:T(2,128)(2,1)S(1)} %reshape.126), channel_id=1, replica_groups=mesh['dp'=32,'y'=8,'core'=2] {'dp'}, dimensions={0} | all-to-all | bytes 1081344 | tf_op jit(solution)/shard_map/all_to_all | solution.py:16
  33.5 0.0 copy-done.4
  33.5 1.6 broadcast_in_dim.8
  35.0 7.1 %all-to-all-start = ((bf16[8,32,4096]{2,1,0:T(8,128)(2,1)}), bf16[8,32,4096]{2,1,0:T(8,128)(2,1)S(1)}, u32[]{:S(2)}, u32[]{:S(2)}) async-start(bf16[8,32,4096]{2,1,0:T(8,128)(2,1)} %broadcast_in_dim.8), calls=%async_computation | async-start | bytes 4194304 | tf_op jit(solution)/shard_map/all_to_all | solution.py:16
  42.2 0.2 reshape.127
  42.4 0.1 add_reduce_fusion
  42.5 2.1 convolution_convert_fusion.2
  44.6 47.2 %all-to-all-done = bf16[8,32,4096]{2,1,0:T(8,128)(2,1)S(1)} async-done(((bf16[8,32,4096]{2,1,0:T(8,128)(2,1)}), bf16[8,32,4096]{2,1,0:T(8,128)(2,1)S(1)}, u32[]{:S(2)}, u32[]{:S(2)}) %all-to-all-start) | async-done | bytes 2097184 | tf_op jit(solution)/shard_map/all_to_all | solution.py:16
  91.8 0.0 copy-start.1
  91.8 1.3 copy-done.1
  93.1 0.0 copy-start
  93.1 0.0 copy-start.5
  93.1 4.5 %all-to-all-start.2 = ((bf16[8,32,4096]{2,1,0:T(8,128)(2,1)}), bf16[8,32,4096]{2,1,0:T(8,128)(2,1)}, u32[]{:S(2)}, u32[]{:S(2)}) async-start(bf16[8,32,4096]{2,1,0:T(8,128)(2,1)} %bitcast.2), calls=%async_computation.2 | async-start | bytes 4194304 | tf_op jit(solution)/shard_map/all_to_all | solution.py:16
  97.6 0.0 copy-done
  97.6 1.9 collective-permute-start
  99.5 2.4 %collective-permute-start.1 = (bf16[4096,256]{1,0:T(8,128)(2,1)}, bf16[4096,256]{1,0:T(8,128)(2,1)}, u32[]{:S(2)}, u32[]{:S(2)}) collective-permute-start(bf16[4096,256]{1,0:T(8,128)(2,1)} %param.12), channel_id=1, source_target_pairs={{0,1},{1,0},{2,3},{3,2},{4,5},{5,4},{6,7},{7,6},{8,9},{9,8},{10,11... | collective-permute-start | bytes 6291464 | tf_op jit(solution)/shard_map/ppermute | solution.py:51
  101.9 0.0 copy-done.5
  102.0 0.2 constant_dynamic-update-slice_fusion.1
  102.1 0.0 copy-start.2
  102.2 1.5 collective-permute-done
  103.6 0.2 constant_dynamic-update-slice_fusion
  103.8 0.0 copy-start.3
  103.8 0.0 copy-done.2
  103.8 1.3 fusion.38
  105.2 0.6 copy-done.3
  105.7 1.2 collective-permute-done.1
  107.0 38.7 %all-to-all-done.2 = bf16[8,32,4096]{2,1,0:T(8,128)(2,1)} async-done(((bf16[8,32,4096]{2,1,0:T(8,128)(2,1)}), bf16[8,32,4096]{2,1,0:T(8,128)(2,1)}, u32[]{:S(2)}, u32[]{:S(2)}) %all-to-all-start.2) | async-done | bytes 2097184 | tf_op jit(solution)/shard_map/all_to_all | solution.py:16
  145.7 4.2 %fusion.39 = (f32[256]{0:T(256)S(1)}, f32[256,512]{1,0:T(8,128)S(1)}) fusion(bf16[256,4096]{1,0:T(8,128)(2,1)} %bitcast.3, bf16[4096,256]{1,0:T(8,128)(2,1)} %collective-permute-done.1, bf16[4096,256]{1,0:T(8,128)(2,1)} %param.12), kind=kOutput, calls=%fused_computation.73 | convolution fusion | flops 1082261248 | bytes 6816768 | tf_op jit(solution)/shard_map/dot_general | solution.py:12
  149.9 0.2 copy.23
  150.1 0.2 exponential_reduce_fusion
  150.3 0.1 multiply_reduce_fusion
  150.5 13.7 %all_to_all.31 = f32[8,6,256]{2,1,0:T(8,128)S(1)} all-to-all(f32[8,6,256]{2,1,0:T(8,128)S(1)} %broadcast_in_dim.10), channel_id=1, replica_groups=mesh['dp'=32,'y'=8,'core'=2] {'y'}, dimensions={0} | all-to-all | bytes 98304 | tf_op jit(solution)/shard_map/all_to_all | solution.py:16
  164.3 0.1 add.65
  164.4 0.6 reduce_sum.107
  165.0 0.6 reduce_sum.106
  165.6 1.4 fusion.32
  166.9 0.6 broadcast_in_dim.11
  167.6 5.8 %all-to-all-start.4 = ((f32[64,1,128]{2,1,0:T(1,128)}), f32[64,1,128]{2,1,0:T(1,128)S(1)}, u32[]{:S(2)}, u32[]{:S(2)}) async-start(f32[64,1,128]{2,1,0:T(1,128)} %broadcast_in_dim.11), calls=%async_computation.4 | async-start | bytes 65536 | tf_op jit(solution)/shard_map/all_to_all | solution.py:16
  173.4 4.9 %convolution_convert_fusion.1 = bf16[256,4096]{1,0:T(8,128)(2,1)} fusion(bf16[4096,512]{1,0:T(8,128)(2,1)} %copy-done.3, f32[512,256]{1,0:T(8,128)S(1)} %get-tuple-element.22, f32[256]{0:T(256)S(1)} %get-tuple-element.9, f32[256]{0:T(256)S(1)} %get-tuple-element.6, f32[256]{0:T(256)S(1)} %get-tuple-element.5, f32[256,512]{0,1:T(8,128)S(1)} %copy.23), kind=kOutput, calls=%fused_computation.1 | convolution fusion | flops 1075576832 | bytes 7343104 | tf_op jit(solution)/shard_map/dot_general | solution.py:12
  178.3 2.9 %all-to-all-done.4 = f32[64,1,128]{2,1,0:T(1,128)S(1)} async-done(((f32[64,1,128]{2,1,0:T(1,128)}), f32[64,1,128]{2,1,0:T(1,128)S(1)}, u32[]{:S(2)}, u32[]{:S(2)}) %all-to-all-start.4) | async-done | bytes 32800 | tf_op jit(solution)/shard_map/all_to_all | solution.py:16
  181.2 3.6 %all-to-all-start.5 = ((bf16[8,32,4096]{2,1,0:T(8,128)(2,1)}), bf16[8,32,4096]{2,1,0:T(8,128)(2,1)S(1)}, u32[]{:S(2)}, u32[]{:S(2)}) async-start(bf16[8,32,4096]{2,1,0:T(8,128)(2,1)} %bitcast.78), calls=%async_computation.5 | async-start | bytes 4194304 | tf_op jit(solution)/shard_map/all_to_all | solution.py:16
  185.5 0.6 fusion.37
  187.4 0.7 multiply_divide_fusion
  188.1 44.7 %all-to-all-done.5 = bf16[8,32,4096]{2,1,0:T(8,128)(2,1)S(1)} async-done(((bf16[8,32,4096]{2,1,0:T(8,128)(2,1)}), bf16[8,32,4096]{2,1,0:T(8,128)(2,1)S(1)}, u32[]{:S(2)}, u32[]{:S(2)}) %all-to-all-start.5) | async-done | bytes 2097184 | tf_op jit(solution)/shard_map/all_to_all | solution.py:16
  232.8 0.3 convert_reduce_fusion
  233.1 0.8 multiply_convert_fusion
  (11 shorter events, 0.2 us)
Async XLA Ops:
  0.6 32.8 %copy-start.4 = (bf16[32,4096]{1,0:T(8,128)(2,1)S(1)}, bf16[32,4096]{1,0:T(8,128)(2,1)}, u32[]{:S(2)}) copy-start(bf16[32,4096]{1,0:T(8,128)(2,1)} %param.7) | copy-start | bytes 786436
  35.0 56.7 %all-to-all-start = ((bf16[8,32,4096]{2,1,0:T(8,128)(2,1)}), bf16[8,32,4096]{2,1,0:T(8,128)(2,1)S(1)}, u32[]{:S(2)}, u32[]{:S(2)}) async-start(bf16[8,32,4096]{2,1,0:T(8,128)(2,1)} %broadcast_in_dim.8), calls=%async_computation | async-start | bytes 4194304 | tf_op jit(solution)/shard_map/all_to_all | solution.py:16
  91.8 1.3 copy-start.1
  93.1 4.5 %copy-start = (bf16[4096,256]{1,0:T(8,128)(2,1)S(1)}, bf16[4096,256]{1,0:T(8,128)(2,1)}, u32[]{:S(2)}) copy-start(bf16[4096,256]{1,0:T(8,128)(2,1)} %param.11) | copy-start | bytes 6291460
  93.1 8.9 %copy-start.5 = (s32[32]{0:T(128)S(1)}, s32[32]{0:T(128)}, u32[]{:S(2)}) copy-start(s32[32]{0:T(128)} %param.10) | copy-start | bytes 388
  93.1 52.6 %all-to-all-start.2 = ((bf16[8,32,4096]{2,1,0:T(8,128)(2,1)}), bf16[8,32,4096]{2,1,0:T(8,128)(2,1)}, u32[]{:S(2)}, u32[]{:S(2)}) async-start(bf16[8,32,4096]{2,1,0:T(8,128)(2,1)} %bitcast.2), calls=%async_computation.2 | async-start | bytes 4194304 | tf_op jit(solution)/shard_map/all_to_all | solution.py:16
  97.6 6.1 %collective-permute-start = (bf16[4096,256]{1,0:T(8,128)(2,1)S(1)}, bf16[4096,256]{1,0:T(8,128)(2,1)S(1)}, u32[]{:S(2)}, u32[]{:S(2)}) collective-permute-start(bf16[4096,256]{1,0:T(8,128)(2,1)S(1)} %copy-done), channel_id=1, source_target_pairs={{0,1},{1,0},{2,3},{3,2},{4,5},{5,4},{6,7},{7,6},{8,9},{9,8},{10,11... | collective-permute-start | bytes 6291464 | tf_op jit(solution)/shard_map/ppermute | solution.py:48
  99.5 7.5 %collective-permute-start.1 = (bf16[4096,256]{1,0:T(8,128)(2,1)}, bf16[4096,256]{1,0:T(8,128)(2,1)}, u32[]{:S(2)}, u32[]{:S(2)}) collective-permute-start(bf16[4096,256]{1,0:T(8,128)(2,1)} %param.12), channel_id=1, source_target_pairs={{0,1},{1,0},{2,3},{3,2},{4,5},{5,4},{6,7},{7,6},{8,9},{9,8},{10,11... | collective-permute-start | bytes 6291464 | tf_op jit(solution)/shard_map/ppermute | solution.py:51
  102.1 1.7 copy-start.2
  103.8 1.9 copy-start.3
  167.6 13.7 %all-to-all-start.4 = ((f32[64,1,128]{2,1,0:T(1,128)}), f32[64,1,128]{2,1,0:T(1,128)S(1)}, u32[]{:S(2)}, u32[]{:S(2)}) async-start(f32[64,1,128]{2,1,0:T(1,128)} %broadcast_in_dim.11), calls=%async_computation.4 | async-start | bytes 65536 | tf_op jit(solution)/shard_map/all_to_all | solution.py:16
  181.2 51.5 %all-to-all-start.5 = ((bf16[8,32,4096]{2,1,0:T(8,128)(2,1)}), bf16[8,32,4096]{2,1,0:T(8,128)(2,1)S(1)}, u32[]{:S(2)}, u32[]{:S(2)}) async-start(bf16[8,32,4096]{2,1,0:T(8,128)(2,1)} %bitcast.78), calls=%async_computation.5 | async-start | bytes 4194304 | tf_op jit(solution)/shard_map/all_to_all | solution.py:16

commit v2 on v1

--- a/solution.py
+++ b/solution.py
@@ -16,6 +16,30 @@
     return lax.all_to_all(x, axis, split_axis=0, concat_axis=0, tiled=True)
 
 
+def ring_gather(x, axis):
+    n = lax.axis_size(axis)
+    me = lax.axis_index(axis)
+    right = [(i, (i + 1) % n) for i in range(n)]
+    left = [(i, (i - 1) % n) for i in range(n)]
+    half = x.shape[0] // 2
+    out = jnp.zeros((n,) + x.shape, x.dtype)
+
+    def put(out, block, owner, row=0):
+        return lax.dynamic_update_slice(out, block[None], (lax.rem(owner, n), row, 0))
+
+    out = put(out, x, me)
+    r = l = x
+    for k in range(1, n // 2):
+        r = lax.ppermute(r, axis, right)
+        l = lax.ppermute(l, axis, left)
+        out = put(out, r, me + n - k)
+        out = put(out, l, me + k)
+    r = lax.ppermute(r[:half], axis, right)
+    l = lax.ppermute(l[half:], axis, left)
+    out = put(out, r, me + n // 2)
+    return put(out, l, me + n // 2, half)
+
+
 def body(student_hidden, teacher_hidden, packing, token_mask, student_head, teacher_head, loss_scale):
     tok, width = student_hidden.shape
     n_dp, n_y = lax.axis_size("dp"), lax.axis_size("y")
@@ -23,9 +47,7 @@
     rows = n_y * tok
     swap = [(0, 1), (1, 0)]
 
-    student_rows = exchange(
-        jnp.broadcast_to(student_hidden[None], (n_y, tok, width)), "y"
-    ).reshape(rows, width)
+    student_rows = lax.all_gather(student_hidden, "y", axis=0, tiled=True)
 
     destination = packing // (n_y * CORES * tok)
     local = packing % tok
@@ -40,9 +62,9 @@
     send = dot(spread, payload, 1, 0).astype(BF)
     got = exchange(send.reshape(n_dp, cap, width + 128), "dp").reshape(n_dp * cap, width + 128)
     slots = got[:, width].astype(jnp.int32) - 1
-    place = (lax.rem(jnp.arange(rows, dtype=jnp.int32), tok)[:, None] == slots[None, :]).astype(BF)
+    place = (index[:, None] == slots[None, :]).astype(BF)
     placed = dot(place, got[:, :width], 1, 0).astype(BF)
-    teacher_rows = exchange(placed.reshape(n_y, tok, width), "y").reshape(rows, width)
+    teacher_rows = ring_gather(placed, "y").reshape(rows, width)
 
     student_both = jnp.concatenate(
         [student_head, lax.ppermute(student_head, "core", swap)], axis=1
@@ -84,18 +106,18 @@
     )
     weights = stats[:, 5, :tok].reshape(rows)
 
+    probs = jnp.exp(student_logits - student_max[:, None]) / student_sum[:, None]
+    grad = (probs * (difference - mean_difference[:, None])).astype(BF)
+    partial = dot(grad, student_both, 1, 1).astype(BF)
+    summed = lax.psum_scatter(partial, "y", scatter_dimension=0, tiled=True)
+
     parts = jnp.stack([jnp.sum(weights * row_kl), jnp.sum(weights)])
     parts = jnp.broadcast_to(jnp.pad(parts, (0, 126))[None, None], (n_dp * CORES, 1, 128))
     totals = jnp.sum(exchange(parts, ("dp", "core")), axis=(0, 1))
     counted = totals[1]
     loss = totals[0] / counted
-
-    probs = jnp.exp(student_logits - student_max[:, None]) / student_sum[:, None]
-    grad = (probs * (difference - mean_difference[:, None])).astype(BF)
-    partial = dot(grad, student_both, 1, 1).astype(BF)
-    blocks = exchange(partial.reshape(n_y, tok, width), "y")
     factor = loss_scale * token_mask.astype(F32) / counted
-    hidden_grad = (factor[:, None] * jnp.sum(blocks.astype(F32), axis=0)).astype(BF)
+    hidden_grad = (factor[:, None] * summed.astype(F32)).astype(BF)
     return hidden_grad, loss
 
 

time: 240 us -> 173 us (0.72); the launches traced: 235 us -> 173 us
  waiting for transfers between devices: 136 us -> 58.5 us
  blocking collectives: 44.1 us -> 13.7 us
  starting transfers between devices: 25.4 us -> 54.9 us
  between operations: 3.95 us -> 17.6 us
    all_to_all x4 -> x2, waiting for transfers between devices: 134 us -> 19.7 us  [exchange(): return lax.all_to_all(x, axis, split_axis=0, concat_axis=0, tiled=True)]
    all_to_all x2 -> x1, blocking collectives: 44.1 us -> 13.7 us  [exchange(): return lax.all_to_all(x, axis, split_axis=0, concat_axis=0, tiled=True)]
    ppermute x0 -> x8, starting transfers between devices: none -> 28.4 us  [the longest x3 14.1 us: ring_gather(): l = lax.ppermute(l, axis, left)]
    ppermute x0 -> x8, waiting for transfers between devices: none -> 22.5 us  [the longest x3 20.1 us: ring_gather(): r = lax.ppermute(r, axis, right)]
    reduce_scatter x0 -> x1, waiting for transfers between devices: none -> 16.2 us  [body(): summed = lax.psum_scatter(partial, 'y', scatter_dimension=0, tiled=True)]
    concatenate x1, local copies, waits for them, and re-layouts: 0.16 us -> 3.11 us  [body(): jnp.concatenate([student_head, lax.ppermute(student_head, 'core', swap)],...]
    all_to_all x4 -> x2, starting transfers between devices: 21 us -> 22.1 us  [exchange(): return lax.all_to_all(x, axis, split_axis=0, concat_axis=0, tiled=True)]
  transfers between devices with their start and end apart: 6 -> 14, of which waited for: 6 -> 8; matrix products, arithmetic and copies ran while one was open for 4% -> 8% of each run, Pallas kernels for 0% -> 0%
where the time goes in v2:
time: 173 us
  waiting for transfers between devices  58.5 us (34%)
  starting transfers between devices  54.9 us (32%)
  between operations  17.6 us (10%)
  blocking collectives  13.7 us (8%)
  matrix products  13.4 us (8%)
  local copies, waits for them, and re-layouts  7.87 us (5%)
  other arithmetic  6.59 us (4%)
    all_to_all x2, starting transfers between devices, exchange(): return lax.all_to_all(x, axis, split_axis=0, concat_axis=0, tiled=True)  22.1 us
    ppermute x3, waiting for transfers between devices, ring_gather(): r = lax.ppermute(r, axis, right)  20.1 us
    all_to_all x2, waiting for transfers between devices, exchange(): return lax.all_to_all(x, axis, split_axis=0, concat_axis=0, tiled=True)  19.7 us
    reduce_scatter x1, waiting for transfers between devices, body(): summed = lax.psum_scatter(partial, 'y', scatter_dimension=0, tiled=True)  16.2 us
    ppermute x3, starting transfers between devices, ring_gather(): l = lax.ppermute(l, axis, left)  14.1 us
    all_to_all x1, blocking collectives, exchange(): return lax.all_to_all(x, axis, split_axis=0, concat_axis=0, tiled=True)  13.7 us
    dot_general x5, matrix products, dot(): lax.dot_general(a, b, (((ca,), (cb,)), ((), ())), preferred_element_type=...  13.4 us
    ppermute x3, starting transfers between devices, ring_gather(): r = lax.ppermute(r, axis, right)  7.3 us
  transfers between devices with their start and end apart: 14, of which 8 were waited for; matrix products, arithmetic and copies ran while one was open for 8% of the time, Pallas kernels for 0%

profile of v2, /device:TPU:6, one launch (start us, length us, event | category | flops | bytes accessed | tf_op | source)
XLA Modules:
  0.0 172.6 jit_solution(13261173987124349607)
XLA Ops:
  7.2 0.0 copy-start
  7.2 0.0 copy-start.1
  7.2 0.8 and_select_fusion.1
  8.0 0.2 convert_reduce_fusion
  8.2 0.1 broadcast_in_dim.27
  8.3 1.2 convolution_convert_fusion
  9.5 1.0 reshape.111
  10.5 13.4 %all-to-all-start = ((bf16[32,2,4224]{2,1,0:T(2,128)(2,1)}), bf16[32,2,4224]{2,1,0:T(2,128)(2,1)S(1)}, u32[]{:S(2)}, u32[]{:S(2)}) async-start(bf16[32,2,4224]{2,1,0:T(2,128)(2,1)} %reshape.111), calls=%async_computation | async-start | bytes 1081344 | tf_op jit(solution)/shard_map/all_to_all | solution.py:16
  23.9 0.0 all-gather.2.cloned.1.call-start
  24.0 0.0 copy-done
  24.0 1.9 %collective-permute-start = (bf16[4096,256]{1,0:T(8,128)(2,1)S(1)}, bf16[4096,256]{1,0:T(8,128)(2,1)}, u32[]{:S(2)}, u32[]{:S(2)}) collective-permute-start(bf16[4096,256]{1,0:T(8,128)(2,1)S(1)} %copy-done), channel_id=1, source_target_pairs={{0,1},{1,0},{2,3},{3,2},{4,5},{5,4},{6,7},{7,6},{8,9},{9,8},{10,11... | collective-permute-start | bytes 6291464 | tf_op jit(solution)/shard_map/ppermute | solution.py:70
  25.9 0.0 all-gather.2.cloned.1.call-update
  25.9 0.0 reduce-scatter.2.cloned.1.call-start
  26.0 2.4 %collective-permute-start.9 = (bf16[4096,256]{1,0:T(8,128)(2,1)}, bf16[4096,256]{1,0:T(8,128)(2,1)}, u32[]{:S(2)}, u32[]{:S(2)}) collective-permute-start(bf16[4096,256]{1,0:T(8,128)(2,1)} %param.12), channel_id=1, source_target_pairs={{0,1},{1,0},{2,3},{3,2},{4,5},{5,4},{6,7},{7,6},{8,9},{9,8},{10,11... | collective-permute-start | bytes 6291464 | tf_op jit(solution)/shard_map/ppermute | solution.py:73
  28.4 0.0 copy-done.1
  28.5 12.6 %all-to-all-done = bf16[32,2,4224]{2,1,0:T(2,128)(2,1)S(1)} async-done(((bf16[32,2,4224]{2,1,0:T(2,128)(2,1)}), bf16[32,2,4224]{2,1,0:T(2,128)(2,1)S(1)}, u32[]{:S(2)}, u32[]{:S(2)}) %all-to-all-start) | async-done | bytes 540704 | tf_op jit(solution)/shard_map/all_to_all | solution.py:16
  41.1 0.2 reshape.112
  41.3 0.1 add_reduce_fusion
  41.4 0.2 broadcast_in_dim.26
  41.7 0.2 bitcast_dynamic-update-slice_fusion.6
  41.9 3.5 %collective-permute-start.1 = (bf16[32,4096]{1,0:T(8,128)(2,1)S(1)}, bf16[32,4096]{1,0:T(8,128)(2,1)S(1)}, u32[]{:S(2)}, u32[]{:S(2)}) collective-permute-start(bf16[32,4096]{1,0:T(8,128)(2,1)S(1)} %get-tuple-element.24), channel_id=1, source_target_pairs={{0,2},{2,4},{4,6},{6,8},{8,10},{10,12},{12,14},{14,0},{1,3},{3,5},... | collective-permute-start | bytes 786440 | tf_op jit(solution)/shard_map/ppermute | solution.py:33
  45.4 3.8 %collective-permute-start.2 = (bf16[32,4096]{1,0:T(8,128)(2,1)S(1)}, bf16[32,4096]{1,0:T(8,128)(2,1)S(1)}, u32[]{:S(2)}, u32[]{:S(2)}) collective-permute-start(bf16[32,4096]{1,0:T(8,128)(2,1)S(1)} %get-tuple-element.24), channel_id=1, source_target_pairs={{0,14},{2,0},{4,2},{6,4},{8,6},{10,8},{12,10},{14,12},{1,15},{3,1}... | collective-permute-start | bytes 786440 | tf_op jit(solution)/shard_map/ppermute | solution.py:34
  49.2 1.5 constant_dynamic-update-slice_fusion.1
  50.7 8.4 %collective-permute-done.1 = bf16[32,4096]{1,0:T(8,128)(2,1)S(1)} collective-permute-done((bf16[32,4096]{1,0:T(8,128)(2,1)S(1)}, bf16[32,4096]{1,0:T(8,128)(2,1)S(1)}, u32[]{:S(2)}, u32[]{:S(2)}) %collective-permute-start.1) | collective-permute-done | bytes 262176 | tf_op jit(solution)/shard_map/ppermute | solution.py:33
  59.1 1.9 %collective-permute-start.3 = (bf16[32,4096]{1,0:T(8,128)(2,1)S(1)}, bf16[32,4096]{1,0:T(8,128)(2,1)S(1)}, u32[]{:S(2)}, u32[]{:S(2)}) collective-permute-start(bf16[32,4096]{1,0:T(8,128)(2,1)S(1)} %collective-permute-done.1), channel_id=1, source_target_pairs={{0,2},{2,4},{4,6},{6,8},{8,10},{10,12},{12,14},{14,0},{1,3},{3,5},... | collective-permute-start | bytes 786440 | tf_op jit(solution)/shard_map/ppermute | solution.py:33
  61.0 0.0 collective-permute-done.2
  61.0 5.1 %collective-permute-start.4 = (bf16[32,4096]{1,0:T(8,128)(2,1)S(1)}, bf16[32,4096]{1,0:T(8,128)(2,1)S(1)}, u32[]{:S(2)}, u32[]{:S(2)}) collective-permute-start(bf16[32,4096]{1,0:T(8,128)(2,1)S(1)} %collective-permute-done.2), channel_id=1, source_target_pairs={{0,14},{2,0},{4,2},{6,4},{8,6},{10,8},{12,10},{14,12},{1,15},{3,1}... | collective-permute-start | bytes 786440 | tf_op jit(solution)/shard_map/ppermute | solution.py:34
  66.1 0.0 copy-start.2
  66.2 9.4 %collective-permute-done.3 = bf16[32,4096]{1,0:T(8,128)(2,1)S(1)} collective-permute-done((bf16[32,4096]{1,0:T(8,128)(2,1)S(1)}, bf16[32,4096]{1,0:T(8,128)(2,1)S(1)}, u32[]{:S(2)}, u32[]{:S(2)}) %collective-permute-start.3) | collective-permute-done | bytes 262176 | tf_op jit(solution)/shard_map/ppermute | solution.py:33
  75.6 1.9 %collective-permute-start.5 = (bf16[32,4096]{1,0:T(8,128)(2,1)S(1)}, bf16[32,4096]{1,0:T(8,128)(2,1)S(1)}, u32[]{:S(2)}, u32[]{:S(2)}) collective-permute-start(bf16[32,4096]{1,0:T(8,128)(2,1)S(1)} %collective-permute-done.3), channel_id=1, source_target_pairs={{0,2},{2,4},{4,6},{6,8},{8,10},{10,12},{12,14},{14,0},{1,3},{3,5},... | collective-permute-start | bytes 786440 | tf_op jit(solution)/shard_map/ppermute | solution.py:33
  77.5 0.0 collective-permute-done.4
  77.5 5.1 %collective-permute-start.6 = (bf16[32,4096]{1,0:T(8,128)(2,1)S(1)}, bf16[32,4096]{1,0:T(8,128)(2,1)S(1)}, u32[]{:S(2)}, u32[]{:S(2)}) collective-permute-start(bf16[32,4096]{1,0:T(8,128)(2,1)S(1)} %collective-permute-done.4), channel_id=1, source_target_pairs={{0,14},{2,0},{4,2},{6,4},{8,6},{10,8},{12,10},{14,12},{1,15},{3,1}... | collective-permute-start | bytes 786440 | tf_op jit(solution)/shard_map/ppermute | solution.py:34
  82.7 2.3 %collective-permute-done.5 = bf16[32,4096]{1,0:T(8,128)(2,1)S(1)} collective-permute-done((bf16[32,4096]{1,0:T(8,128)(2,1)S(1)}, bf16[32,4096]{1,0:T(8,128)(2,1)S(1)}, u32[]{:S(2)}, u32[]{:S(2)}) %collective-permute-start.5) | collective-permute-done | bytes 262176 | tf_op jit(solution)/shard_map/ppermute | solution.py:33
  85.1 1.9 %collective-permute-start.7 = (bf16[16,4096]{1,0:T(8,128)(2,1)S(1)}, bf16[16,4096]{1,0:T(8,128)(2,1)S(1)}, u32[]{:S(2)}, u32[]{:S(2)}) collective-permute-start(bf16[16,4096]{1,0:T(8,128)(2,1)S(1)} %slice.52), channel_id=1, source_target_pairs={{0,2},{2,4},{4,6},{6,8},{8,10},{10,12},{12,14},{14,0},{1,3},{3,5},... | collective-permute-start | bytes 393224 | tf_op jit(solution)/shard_map/ppermute | solution.py:37
  87.0 0.0 collective-permute-done.6
  87.0 5.1 %collective-permute-start.8 = (bf16[16,4096]{1,0:T(8,128)(2,1)S(1)}, bf16[16,4096]{1,0:T(8,128)(2,1)S(1)}, u32[]{:S(2)}, u32[]{:S(2)}) collective-permute-start(bf16[16,4096]{1,0:T(8,128)(2,1)S(1)} %slice.53), channel_id=1, source_target_pairs={{0,14},{2,0},{4,2},{6,4},{8,6},{10,8},{12,10},{14,12},{1,15},{3,1}... | collective-permute-start | bytes 393224 | tf_op jit(solution)/shard_map/ppermute | solution.py:38
  92.2 0.9 collective-permute-done.7
  93.2 1.5 collective-permute-done.8
  94.7 0.0 collective-permute-done.9
  94.7 0.0 copy-done.2
  94.7 2.9 %fusion.37 = (f32[256]{0:T(256)S(1)}, f32[256,512]{1,0:T(8,128)S(1)}) fusion(bf16[256,4096]{1,0:T(8,128)(2,1)S(1)} %bitcast.92, bf16[4096,256]{1,0:T(8,128)(2,1)} %collective-permute-done.9, bf16[4096,256]{1,0:T(8,128)(2,1)S(1)} %copy-done.2), kind=kOutput, calls=%fused_computation.79 | convolution fusion | flops 1082261248 | bytes 6816768 | tf_op jit(solution)/shard_map/dot_general | solution.py:12
  97.6 0.2 copy.23
  97.8 0.2 exponential_reduce_fusion
  98.1 0.0 collective-permute-done
  98.1 3.1 %constant_dynamic-update-slice_fusion = bf16[4096,512]{1,0:T(8,128)(2,1)} fusion(bf16[4096,512]{1,0:T(8,128)(2,1)} %constant_dynamic-update-slice_fusion.1, bf16[4096,256]{1,0:T(8,128)(2,1)} %collective-permute-done), kind=kLoop, calls=%fused_computation.56 | loop fusion | bytes 4194304 | tf_op jit(solution)/shard_map/concatenate | solution.py:69
  101.2 0.0 all-gather.2.cloned.1.call-done
  101.2 4.2 %fusion.36 = (f32[256]{0:T(256)S(1)}, f32[512,256]{1,0:T(8,128)S(1)}) fusion(bf16[4096,512]{1,0:T(8,128)(2,1)} %constant_dynamic-update-slice_fusion, bf16[256,4096]{1,0:T(8,128)(2,1)} %all-gather.2.cloned.1.call-done), kind=kOutput, calls=%fused_computation.78 | convolution fusion | flops 1073872640 | bytes 6816768 | tf_op jit(solution)/shard_map/dot_general | solution.py:12
  105.3 0.1 multiply_reduce_fusion
  105.5 13.7 %all_to_all.15 = f32[8,6,256]{2,1,0:T(8,128)S(1)} all-to-all(f32[8,6,256]{2,1,0:T(8,128)S(1)} %broadcast_in_dim.37), channel_id=1, replica_groups=mesh['dp'=32,'y'=8,'core'=2] {'y'}, dimensions={0} | all-to-all | bytes 98304 | tf_op jit(solution)/shard_map/all_to_all | solution.py:16
  119.3 4.9 %convolution_convert_fusion.1 = bf16[256,4096]{1,0:T(8,128)(2,1)} fusion(bf16[4096,512]{1,0:T(8,128)(2,1)} %constant_dynamic-update-slice_fusion, f32[512,256]{1,0:T(8,128)S(1)} %get-tuple-element.22, f32[256]{0:T(256)S(1)} %get-tuple-element.9, f32[256]{0:T(256)S(1)} %get-tuple-element.6, f32[256]{0:T(256)S(1)} %get-tuple-element.5, f32[256,512]{0,1:T(8,128)S(1)} %copy.23), kind=kOutput, calls=%fused_computation.1 | convolution fusion | flops 1075576832 | bytes 7343104 | tf_op jit(solution)/shard_map/dot_general | solution.py:12
  124.2 0.0 reduce-scatter.2.cloned.1.call-update
  124.2 0.1 add.129
  124.3 0.6 reduce_sum.98
  124.9 0.6 reduce_sum.97
  125.5 1.4 fusion.30
  126.9 0.6 broadcast_in_dim.76
  127.5 8.7 %all-to-all-start.2 = ((f32[64,1,128]{2,1,0:T(1,128)}), f32[64,1,128]{2,1,0:T(1,128)S(1)}, u32[]{:S(2)}, u32[]{:S(2)}) async-start(f32[64,1,128]{2,1,0:T(1,128)} %broadcast_in_dim.76), calls=%async_computation.2 | async-start | bytes 65536 | tf_op jit(solution)/shard_map/all_to_all | solution.py:16
  136.8 7.2 %all-to-all-done.2 = f32[64,1,128]{2,1,0:T(1,128)S(1)} async-done(((f32[64,1,128]{2,1,0:T(1,128)}), f32[64,1,128]{2,1,0:T(1,128)S(1)}, u32[]{:S(2)}, u32[]{:S(2)}) %all-to-all-start.2) | async-done | bytes 32800 | tf_op jit(solution)/shard_map/all_to_all | solution.py:16
  144.0 0.6 fusion.35
  145.9 0.7 multiply_divide_fusion
  146.6 16.2 %reduce-scatter.2.cloned.1.call-done = bf16[32,4096]{1,0:T(8,128)(2,1)} async-done(((bf16[256,4096]{1,0:T(8,128)(2,1)}), bf16[32,4096]{1,0:T(8,128)(2,1)}) %reduce-scatter.2.cloned.1.call-update) | async-done | bytes 262160 | tf_op jit(solution)/shard_map/reduce_scatter | solution.py:112
  162.8 1.8 %multiply_convert_fusion = bf16[32,4096]{1,0:T(8,128)(2,1)} fusion(bf16[32,4096]{1,0:T(8,128)(2,1)} %reduce-scatter.2.cloned.1.call-done, f32[32]{0:T(128)S(1)} %multiply_divide_fusion), kind=kLoop, calls=%fused_computation.15 | loop fusion | flops 393216 | bytes 524416 | tf_op jit(solution)/shard_map/convert_element_type | solution.py:120
  (20 shorter events, 0.4 us)
Async XLA Ops:
  7.2 16.8 %copy-start = (bf16[4096,256]{1,0:T(8,128)(2,1)S(1)}, bf16[4096,256]{1,0:T(8,128)(2,1)}, u32[]{:S(2)}) copy-start(bf16[4096,256]{1,0:T(8,128)(2,1)} %param.11) | copy-start | bytes 6291460
  7.2 21.3 %copy-start.1 = (s32[32]{0:T(128)S(1)}, s32[32]{0:T(128)}, u32[]{:S(2)}) copy-start(s32[32]{0:T(128)} %param.10) | copy-start | bytes 388
  10.5 30.6 %all-to-all-start = ((bf16[32,2,4224]{2,1,0:T(2,128)(2,1)}), bf16[32,2,4224]{2,1,0:T(2,128)(2,1)S(1)}, u32[]{:S(2)}, u32[]{:S(2)}) async-start(bf16[32,2,4224]{2,1,0:T(2,128)(2,1)} %reshape.111), calls=%async_computation | async-start | bytes 1081344 | tf_op jit(solution)/shard_map/all_to_all | solution.py:16
  23.9 77.3 %all-gather.2.cloned.1.call-start = ((), (), s32[]{:S(2)}) async-start(), calls=%async_computation.4 | async-start | bytes 2359296 | tf_op jit(solution)/shard_map/all_gather | solution.py:50
  24.0 74.1 %collective-permute-start = (bf16[4096,256]{1,0:T(8,128)(2,1)S(1)}, bf16[4096,256]{1,0:T(8,128)(2,1)}, u32[]{:S(2)}, u32[]{:S(2)}) collective-permute-start(bf16[4096,256]{1,0:T(8,128)(2,1)S(1)} %copy-done), channel_id=1, source_target_pairs={{0,1},{1,0},{2,3},{3,2},{4,5},{5,4},{6,7},{7,6},{8,9},{9,8},{10,11... | collective-permute-start | bytes 6291464 | tf_op jit(solution)/shard_map/ppermute | solution.py:70
  25.9 136.9 %reduce-scatter.2.cloned.1.call-start = ((), (), s32[]{:S(2)}) async-start(), calls=%async_computation.5 | async-start | bytes 2359296 | tf_op jit(solution)/shard_map/reduce_scatter | solution.py:112
  26.0 68.7 %collective-permute-start.9 = (bf16[4096,256]{1,0:T(8,128)(2,1)}, bf16[4096,256]{1,0:T(8,128)(2,1)}, u32[]{:S(2)}, u32[]{:S(2)}) collective-permute-start(bf16[4096,256]{1,0:T(8,128)(2,1)} %param.12), channel_id=1, source_target_pairs={{0,1},{1,0},{2,3},{3,2},{4,5},{5,4},{6,7},{7,6},{8,9},{9,8},{10,11... | collective-permute-start | bytes 6291464 | tf_op jit(solution)/shard_map/ppermute | solution.py:73
  41.9 17.2 %collective-permute-start.1 = (bf16[32,4096]{1,0:T(8,128)(2,1)S(1)}, bf16[32,4096]{1,0:T(8,128)(2,1)S(1)}, u32[]{:S(2)}, u32[]{:S(2)}) collective-permute-start(bf16[32,4096]{1,0:T(8,128)(2,1)S(1)} %get-tuple-element.24), channel_id=1, source_target_pairs={{0,2},{2,4},{4,6},{6,8},{8,10},{10,12},{12,14},{14,0},{1,3},{3,5},... | collective-permute-start | bytes 786440 | tf_op jit(solution)/shard_map/ppermute | solution.py:33
  45.4 15.6 %collective-permute-start.2 = (bf16[32,4096]{1,0:T(8,128)(2,1)S(1)}, bf16[32,4096]{1,0:T(8,128)(2,1)S(1)}, u32[]{:S(2)}, u32[]{:S(2)}) collective-permute-start(bf16[32,4096]{1,0:T(8,128)(2,1)S(1)} %get-tuple-element.24), channel_id=1, source_target_pairs={{0,14},{2,0},{4,2},{6,4},{8,6},{10,8},{12,10},{14,12},{1,15},{3,1}... | collective-permute-start | bytes 786440 | tf_op jit(solution)/shard_map/ppermute | solution.py:34
  59.1 16.5 %collective-permute-start.3 = (bf16[32,4096]{1,0:T(8,128)(2,1)S(1)}, bf16[32,4096]{1,0:T(8,128)(2,1)S(1)}, u32[]{:S(2)}, u32[]{:S(2)}) collective-permute-start(bf16[32,4096]{1,0:T(8,128)(2,1)S(1)} %collective-permute-done.1), channel_id=1, source_target_pairs={{0,2},{2,4},{4,6},{6,8},{8,10},{10,12},{12,14},{14,0},{1,3},{3,5},... | collective-permute-start | bytes 786440 | tf_op jit(solution)/shard_map/ppermute | solution.py:33
  61.0 16.5 %collective-permute-start.4 = (bf16[32,4096]{1,0:T(8,128)(2,1)S(1)}, bf16[32,4096]{1,0:T(8,128)(2,1)S(1)}, u32[]{:S(2)}, u32[]{:S(2)}) collective-permute-start(bf16[32,4096]{1,0:T(8,128)(2,1)S(1)} %collective-permute-done.2), channel_id=1, source_target_pairs={{0,14},{2,0},{4,2},{6,4},{8,6},{10,8},{12,10},{14,12},{1,15},{3,1}... | collective-permute-start | bytes 786440 | tf_op jit(solution)/shard_map/ppermute | solution.py:34
  66.1 28.6 %copy-start.2 = (bf16[4096,256]{1,0:T(8,128)(2,1)S(1)}, bf16[4096,256]{1,0:T(8,128)(2,1)}, u32[]{:S(2)}) copy-start(bf16[4096,256]{1,0:T(8,128)(2,1)} %param.12) | copy-start | bytes 6291460
  75.6 9.5 %collective-permute-start.5 = (bf16[32,4096]{1,0:T(8,128)(2,1)S(1)}, bf16[32,4096]{1,0:T(8,128)(2,1)S(1)}, u32[]{:S(2)}, u32[]{:S(2)}) collective-permute-start(bf16[32,4096]{1,0:T(8,128)(2,1)S(1)} %collective-permute-done.3), channel_id=1, source_target_pairs={{0,2},{2,4},{4,6},{6,8},{8,10},{10,12},{12,14},{14,0},{1,3},{3,5},... | collective-permute-start | bytes 786440 | tf_op jit(solution)/shard_map/ppermute | solution.py:33
  77.5 9.5 %collective-permute-start.6 = (bf16[32,4096]{1,0:T(8,128)(2,1)S(1)}, bf16[32,4096]{1,0:T(8,128)(2,1)S(1)}, u32[]{:S(2)}, u32[]{:S(2)}) collective-permute-start(bf16[32,4096]{1,0:T(8,128)(2,1)S(1)} %collective-permute-done.4), channel_id=1, source_target_pairs={{0,14},{2,0},{4,2},{6,4},{8,6},{10,8},{12,10},{14,12},{1,15},{3,1}... | collective-permute-start | bytes 786440 | tf_op jit(solution)/shard_map/ppermute | solution.py:34
  85.1 8.1 %collective-permute-start.7 = (bf16[16,4096]{1,0:T(8,128)(2,1)S(1)}, bf16[16,4096]{1,0:T(8,128)(2,1)S(1)}, u32[]{:S(2)}, u32[]{:S(2)}) collective-permute-start(bf16[16,4096]{1,0:T(8,128)(2,1)S(1)} %slice.52), channel_id=1, source_target_pairs={{0,2},{2,4},{4,6},{6,8},{8,10},{10,12},{12,14},{14,0},{1,3},{3,5},... | collective-permute-start | bytes 393224 | tf_op jit(solution)/shard_map/ppermute | solution.py:37
  87.0 7.6 %collective-permute-start.8 = (bf16[16,4096]{1,0:T(8,128)(2,1)S(1)}, bf16[16,4096]{1,0:T(8,128)(2,1)S(1)}, u32[]{:S(2)}, u32[]{:S(2)}) collective-permute-start(bf16[16,4096]{1,0:T(8,128)(2,1)S(1)} %slice.53), channel_id=1, source_target_pairs={{0,14},{2,0},{4,2},{6,4},{8,6},{10,8},{12,10},{14,12},{1,15},{3,1}... | collective-permute-start | bytes 393224 | tf_op jit(solution)/shard_map/ppermute | solution.py:38
  127.5 16.5 %all-to-all-start.2 = ((f32[64,1,128]{2,1,0:T(1,128)}), f32[64,1,128]{2,1,0:T(1,128)S(1)}, u32[]{:S(2)}, u32[]{:S(2)}) async-start(f32[64,1,128]{2,1,0:T(1,128)} %broadcast_in_dim.76), calls=%async_computation.2 | async-start | bytes 65536 | tf_op jit(solution)/shard_map/all_to_all | solution.py:16
Sparse Core Ops, SparseCore 0:
  26.8 51.0 all-gather.1
  124.3 38.4 reduce-scatter.1

commit v3 on v2

v3 whole, which is shorter than its diff:
```python
import jax
import jax.experimental.pallas as pl
import jax.experimental.pallas.tpu as pltpu
import jax.numpy as jnp
from jax import lax
from jax.sharding import Mesh, PartitionSpec as P

BF = jnp.bfloat16
F32 = jnp.float32
CORES = 2
STATS = 8
STEPS = 4
GRADIENT_STEPS = 2
VMEM_LIMIT = 16 * 1024 * 1024


def dot(a, b, ca, cb):
    return lax.dot_general(a, b, (((ca,), (cb,)), ((), ())), preferred_element_type=F32)


def exchange(x, axis):
    return lax.all_to_all(x, axis, split_axis=0, concat_axis=0, tiled=True)


def ring_gather(x, out, axis, beside):
    n = lax.axis_size(axis)
    me = lax.axis_index(axis)
    right = [(i, (i + 1) % n) for i in range(n)]
    left = [(i, (i - 1) % n) for i in range(n)]
    half = x.shape[0] // 2

    def put(out, block, owner, row=0):
        return lax.dynamic_update_slice(out, block[None], (lax.rem(owner, n), row, 0))

    out = put(out, x, me)
    r = l = x
    for k in range(1, n // 2):
        r = lax.ppermute(r, axis, right)
        l = lax.ppermute(l, axis, left)
        out = put(out, r, me + n - k)
        out = put(out, l, me + k)
        if k == 2:
            r, l, beside = lax.optimization_barrier((r, l, beside))
    r = lax.ppermute(r[:half], axis, right)
    l = lax.ppermute(l[half:], axis, left)
    out = put(out, r, me + n // 2)
    return put(out, l, me + n // 2, half), beside


def buffers(*shapes):
    return pl.pallas_call(
        lambda *refs: None,
        out_specs=[pl.BlockSpec(memory_space=pl.ANY) for _ in shapes],
        out_shape=[pltpu.HBM(shape, BF) for shape in shapes],
        name="buffers",
    )()


def logits_kernel(xs_ref, xt_ref, ws0_ref, ws1_ref, wt0_ref, wt1_ref, mask_ref, s_ref, d_ref, stats_ref):
    step = pl.program_id(0)
    rows, block = s_ref.shape[0], ws0_ref.shape[1]
    xs = xs_ref[...].reshape(rows, xs_ref.shape[2])
    xt = xt_ref[...].reshape(rows, xt_ref.shape[2])

    @pl.when(step == 0)
    def _():
        s_ref[...] = jnp.zeros_like(s_ref)
        d_ref[...] = jnp.zeros_like(d_ref)

    s_ref[:, :block] += dot(xs, ws0_ref[...], 1, 0)
    s_ref[:, block:] += dot(xs, ws1_ref[...], 1, 0)
    d_ref[:, :block] += dot(xt, wt0_ref[...], 1, 0)
    d_ref[:, block:] += dot(xt, wt1_ref[...], 1, 0)

    @pl.when(step == pl.num_programs(0) - 1)
    def _():
        s, t = s_ref[...], d_ref[...]
        d = s - t
        d_ref[...] = d
        s_top = jnp.max(s, axis=1, keepdims=True)
        t_top = jnp.max(t, axis=1, keepdims=True)
        e = jnp.exp(s - s_top)
        columns = (
            s_top,
            t_top,
            jnp.sum(e, axis=1, keepdims=True),
            jnp.sum(jnp.exp(t - t_top), axis=1, keepdims=True),
            jnp.sum(e * d, axis=1, keepdims=True),
        )
        lane = lax.broadcasted_iota(jnp.int32, (rows, 128), 1)
        table = jnp.zeros((rows, 128), F32)
        for j, column in enumerate(columns):
            table = jnp.where(lane == j, column, table)
        table = table.T[:STATS]
        line = lax.broadcasted_iota(jnp.int32, (STATS, rows), 0)
        table = jnp.where(line == len(columns), mask_ref[...], table)
        stats_ref[...] = jnp.broadcast_to(table[None], stats_ref.shape)


def logits(student_rows, teacher_rows, heads, mask):
    n_y, tok, width = student_rows.shape
    rows = n_y * tok
    block = heads[0].shape[1]
    depth = width // STEPS
    head = pl.BlockSpec((depth, block), lambda k: (k, 0))
    whole = pl.BlockSpec((rows, CORES * block), lambda k: (0, 0))
    return pl.pallas_call(
        logits_kernel,
        grid=(STEPS,),
        in_specs=[
            pl.BlockSpec((n_y, tok, depth), lambda k: (0, 0, k)),
            pl.BlockSpec((n_y, tok, depth), lambda k: (0, 0, k)),
            head,
            head,
            head,
            head,
            pl.BlockSpec((1, rows), lambda k: (0, 0)),
        ],
        out_specs=[whole, whole, pl.BlockSpec((n_y, STATS, rows), lambda k: (0, 0, 0))],
        out_shape=[
            jax.ShapeDtypeStruct((rows, CORES * block), F32),
            jax.ShapeDtypeStruct((rows, CORES * block), F32),
            jax.ShapeDtypeStruct((n_y, STATS, rows), F32),
        ],
        compiler_params=pltpu.CompilerParams(vmem_limit_bytes=VMEM_LIMIT),
        cost_estimate=pl.CostEstimate(
            flops=8 * rows * width * block, bytes_accessed=12 * 2**20, transcendentals=2**18
        ),
        name="logits",
    )(student_rows, teacher_rows, *heads, mask)


def gradient_kernel(stats_ref, s_ref, d_ref, w0_ref, w1_ref, out_ref, parts_ref, grad_ref):
    rows, block = s_ref.shape[0], w0_ref.shape[1]

    @pl.when(pl.program_id(0) == 0)
    def _():
        stats = [stats_ref[:, j, :] for j in range(6)]
        s_top = jnp.max(stats[0], axis=0, keepdims=True)
        t_top = jnp.max(stats[1], axis=0, keepdims=True)
        scale = jnp.exp(stats[0] - s_top)
        s_sum = jnp.sum(stats[2] * scale, axis=0, keepdims=True)
        t_sum = jnp.sum(stats[3] * jnp.exp(stats[1] - t_top), axis=0, keepdims=True)
        mean = jnp.sum(stats[4] * scale, axis=0, keepdims=True) / s_sum
        weights = jnp.sum(stats[5], axis=0, keepdims=True)
        row_kl = mean - (s_top + jnp.log(s_sum)) + (t_top + jnp.log(t_sum))
        lane = lax.broadcasted_iota(jnp.int32, parts_ref.shape, 1)
        parts_ref[...] = jnp.where(
            lane == 0, jnp.sum(weights * row_kl), jnp.where(lane == 1, jnp.sum(weights), 0.0)
        )
        line = lax.broadcasted_iota(jnp.int32, (128, rows), 0)
        table = jnp.where(line == 0, s_top, jnp.where(line == 1, 1.0 / s_sum, mean)).T
        probs = jnp.exp(s_ref[...] - table[:, 0:1]) * table[:, 1:2]
        grad_ref[...] = (probs * (d_ref[...] - table[:, 2:3])).astype(BF)

    out_ref[...] = (
        dot(grad_ref[:, :block], w0_ref[...], 1, 1) + dot(grad_ref[:, block:], w1_ref[...], 1, 1)
    ).astype(BF)


def gradient(stats, s, d, heads, copies):
    rows, (width, block) = s.shape[0], heads[0].shape
    depth = width // GRADIENT_STEPS
    head = pl.BlockSpec((depth, block), lambda k: (k, 0))
    whole = pl.BlockSpec(s.shape, lambda k: (0, 0))
    return pl.pallas_call(
        gradient_kernel,
        grid=(GRADIENT_STEPS,),
        in_specs=[pl.BlockSpec(stats.shape, lambda k: (0, 0, 0)), whole, whole, head, head],
        out_specs=[
            pl.BlockSpec((rows, depth), lambda k: (0, k)),
            pl.BlockSpec((copies, 128), lambda k: (0, 0)),
        ],
        out_shape=[
            pltpu.HBM((rows, width), BF),
            jax.ShapeDtypeStruct((copies, 128), F32),
        ],
        scratch_shapes=[pltpu.VMEM(s.shape, BF)],
        compiler_params=pltpu.CompilerParams(vmem_limit_bytes=VMEM_LIMIT),
        cost_estimate=pl.CostEstimate(
            flops=4 * rows * width * block, bytes_accessed=7 * 2**20, transcendentals=2**17
        ),
        name="gradient",
    )(stats, s, d, *heads)


def body(student_hidden, teacher_hidden, packing, token_mask, student_head, teacher_head, loss_scale):
    tok, width = student_hidden.shape
    n_dp, n_y = lax.axis_size("dp"), lax.axis_size("y")
    cap = max(2, 2 * tok // n_dp)
    rows = n_y * tok
    swap = [(0, 1), (1, 0)]

    destination = packing // (n_y * CORES * tok)
    local = packing % tok
    index = jnp.arange(tok, dtype=jnp.int32)
    earlier = (destination[:, None] == destination[None, :]) & (index[None, :] < index[:, None])
    rank = jnp.sum(earlier.astype(jnp.int32), axis=1)
    position = destination * cap + rank
    payload = jnp.concatenate(
        [teacher_hidden, jnp.broadcast_to((local + 1).astype(BF)[:, None], (tok, 128))], axis=1
    )

    def teacher_turn(_, carry):
        position, out, *_ = carry
        spread = (jnp.arange(n_dp * cap, dtype=jnp.int32)[:, None] == position[None, :]).astype(BF)
        send = dot(spread, payload, 1, 0).astype(BF)
        got = exchange(send.reshape(n_dp, cap, width + 128), "dp").reshape(n_dp * cap, width + 128)
        slots = got[:, width].astype(jnp.int32) - 1
        place = (index[:, None] == slots[None, :]).astype(BF)
        placed = dot(place, got[:, :width], 1, 0).astype(BF)
        heads, placed = lax.optimization_barrier(((student_head, teacher_head), placed))
        other = [lax.ppermute(head, "core", swap) for head in heads]
        out, other = ring_gather(placed, out, "y", other)
        return slots[:tok], out, *other

    student_rows = lax.all_gather(student_hidden, "y", axis=0)
    once = lax.optimization_barrier(jnp.int32(1))
    empty = buffers((n_y, tok, width), student_head.shape, teacher_head.shape)
    _, teacher_rows, *other = lax.fori_loop(0, once, teacher_turn, (position, *empty))

    mine = jnp.arange(rows, dtype=jnp.int32) // tok == lax.axis_index("y")
    mask = jnp.where(mine, jnp.tile(token_mask.astype(F32), n_y), 0.0)[None]

    student_rows, teacher_rows, teacher_head = (
        pltpu.with_memory_space_constraint(x, pltpu.HBM) for x in (student_rows, teacher_rows, teacher_head)
    )
    s, d, stats = logits(student_rows, teacher_rows, (student_head, other[0], teacher_head, other[1]), mask)
    stats = exchange(stats, "y")
    partial, parts = gradient(stats, s, d, (student_head, other[0]), n_dp * CORES)
    summed = lax.psum_scatter(partial, "y", scatter_dimension=0, tiled=True)

    totals = jnp.sum(exchange(parts[:, None], ("dp", "core")), axis=(0, 1))
    counted = totals[1]
    loss = totals[0] / counted
    factor = loss_scale * token_mask.astype(F32) / counted
    hidden_grad = (factor[:, None] * summed.astype(F32)).astype(BF)
    return hidden_grad, loss


def solution(mesh):
    dp, vocab = mesh.devices.shape
    grid = Mesh(mesh.devices.reshape(dp, vocab // CORES, CORES), ("dp", "y", "core"))
    every = ("dp", "y", "core")
    return jax.shard_map(
        body,
        mesh=grid,
        in_specs=(
            P(every, None),
            P(every, None),
            P(every),
            P(every),
            P(None, ("y", "core")),
            P(None, ("y", "core")),
            P(),
        ),
        out_specs=(P(every, None), P()),
        check_vma=False,
    )
```

time: 173 us -> 164 us (0.948)
  matrix products: 13.4 us -> 0.5 us
  Pallas kernels: 0 us -> 10.1 us
  waiting for transfers between devices: 58.5 us -> 52 us
    ppermute x3, waiting for transfers between devices: 20.1 us -> 6.63 us  [ring_gather(): r = lax.ppermute(r, axis, right)]
    dot_general x5 -> x2, matrix products: 13.4 us -> 0.5 us  [dot(): lax.dot_general(a, b, (((ca,), (cb,)), ((), ())), preferred_element_type=...]
    pallas_call x0 -> x3, Pallas kernels: none -> 10.1 us  [the longest x1 7.24 us: logits(): pl.pallas_call(logits_kernel, grid=(STEPS,), in_specs=[pl.BlockSpec((n_y,...]
    dynamic_update_slice x8 -> x9, local copies, waits for them, and re-layouts: 0.17 us -> 6.41 us  [put(): lax.dynamic_update_slice(out, block[None], (lax.rem(owner, n), row, 0))]
    all_to_all x2, waiting for transfers between devices: 19.7 us -> 24.3 us  [exchange(): return lax.all_to_all(x, axis, split_axis=0, concat_axis=0, tiled=True)]
    reduce_scatter x1, waiting for transfers between devices: 16.2 us -> 19.4 us  [body(): summed = lax.psum_scatter(partial, 'y', scatter_dimension=0, tiled=True)]
    concatenate x1 -> x0, local copies, waits for them, and re-layouts: 3.11 us -> none  [body(): jnp.concatenate([student_head, lax.ppermute(student_head, 'core', swap)],...]
where the time goes in v3:
time: 164 us; the launch traced here: 163 us
  starting transfers between devices  55.1 us (34%)
  waiting for transfers between devices  52 us (32%)
  between operations  17.2 us (10%)
  blocking collectives  14.5 us (9%)
  Pallas kernels  10.1 us (6%)
  local copies, waits for them, and re-layouts  8.51 us (5%)
  other arithmetic  5.1 us (3%)
    all_to_all x2, waiting for transfers between devices, exchange(): return lax.all_to_all(x, axis, split_axis=0, concat_axis=0, tiled=True)  24.3 us
    all_to_all x2, starting transfers between devices, exchange(): return lax.all_to_all(x, axis, split_axis=0, concat_axis=0, tiled=True)  21.8 us
    reduce_scatter x1, waiting for transfers between devices, body(): summed = lax.psum_scatter(partial, 'y', scatter_dimension=0, tiled=True)  19.4 us
    all_to_all x1, blocking collectives, exchange(): return lax.all_to_all(x, axis, split_axis=0, concat_axis=0, tiled=True)  14.5 us
    ppermute x3, starting transfers between devices, ring_gather(): l = lax.ppermute(l, axis, left)  13.5 us
    ppermute x3, starting transfers between devices, ring_gather(): r = lax.ppermute(r, axis, right)  8.33 us
    pallas_call x1, Pallas kernels, logits(): pl.pallas_call(logits_kernel, grid=(STEPS,), in_specs=[pl.BlockSpec((n_y,...  7.24 us
    ppermute x3, waiting for transfers between devices, ring_gather(): r = lax.ppermute(r, axis, right)  6.63 us
  transfers between devices with their start and end apart: 14, of which 8 were waited for; matrix products, arithmetic and copies ran while one was open for 8% of the time, Pallas kernels for 0%

profile of v3, /device:TPU:6, one launch (start us, length us, event | category | flops | bytes accessed | tf_op | source)
XLA Modules:
  0.0 163.3 jit_solution(15764861187240236202)
XLA Ops:
  7.2 0.0 all-gather.3.cloned.1.call-start
  7.2 0.7 all-gather.3.cloned.1.call-update
  7.9 0.0 reduce-scatter.2.cloned.1.call-start
  8.0 0.7 fusion.8
  8.6 0.2 convert_reduce_fusion
  8.8 0.7 convert_element_type.56
  9.5 0.1 tile.10
  9.6 0.1 broadcast_in_dim.113
  9.6 1.0 pad_maximum_fusion
  10.6 80.0 %while.22 = (s32[]{:T(128)}, s32[32]{0:T(128)S(1)}, bf16[8,32,4096]{2,1,0:T(8,128)(2,1)}, bf16[4096,256]{1,0:T(8,128)(2,1)}, bf16[4096,256]{1,0:T(8,128)(2,1)}, ...) while((s32[]{:T(128)}, s32[32]{0:T(128)S(1)}, ...), condition=%wide.region_2.3_spmd.clone, body=%wide.region_1.2_spmd.clone.sunk | while | flops 34484352 | bytes 59386968 | solution.py:220
  10.6 0.3 convolution_convert_fusion.4
  10.9 0.0 copy-start
  10.9 1.0 reshape.98
  11.9 13.4 %all-to-all-start = ((bf16[32,2,4224]{2,1,0:T(2,128)(2,1)}), bf16[32,2,4224]{2,1,0:T(2,128)(2,1)S(1)}, u32[]{:S(2)}, u32[]{:S(2)}) async-start(bf16[32,2,4224]{2,1,0:T(2,128)(2,1)} %reshape.98), calls=%async_computation | async-start | bytes 1081344 | tf_op jit(solution)/shard_map/while/body/all_to_all | solution.py:22
  25.4 17.1 %all-to-all-done = bf16[32,2,4224]{2,1,0:T(2,128)(2,1)S(1)} async-done(((bf16[32,2,4224]{2,1,0:T(2,128)(2,1)}), bf16[32,2,4224]{2,1,0:T(2,128)(2,1)S(1)}, u32[]{:S(2)}, u32[]{:S(2)}) %all-to-all-start) | async-done | bytes 540704 | tf_op jit(solution)/shard_map/while/body/all_to_all | solution.py:22
  42.5 0.2 reshape.99
  42.7 0.1 fusion.16
  42.9 0.2 convolution_convert_fusion.5
  43.1 3.5 %collective-permute-start = (bf16[32,4096]{1,0:T(8,128)(2,1)S(1)}, bf16[32,4096]{1,0:T(8,128)(2,1)S(1)}, u32[]{:S(2)}, u32[]{:S(2)}) collective-permute-start(bf16[32,4096]{1,0:T(8,128)(2,1)S(1)} %convolution_convert_fusion.5), channel_id=1, source_target_pairs={{0,2},{2,4},{4,6},{6,8},{8,10},{10,12},{12,14},{14,0},{1,3},{3,5},... | collective-permute-start | bytes 786440 | tf_op jit(solution)/shard_map/while/body/ppermute | solution.py:38
  46.6 3.8 %collective-permute-start.1 = (bf16[32,4096]{1,0:T(8,128)(2,1)S(1)}, bf16[32,4096]{1,0:T(8,128)(2,1)S(1)}, u32[]{:S(2)}, u32[]{:S(2)}) collective-permute-start(bf16[32,4096]{1,0:T(8,128)(2,1)S(1)} %convolution_convert_fusion.5), channel_id=1, source_target_pairs={{0,14},{2,0},{4,2},{6,4},{8,6},{10,8},{12,10},{14,12},{1,15},{3,1}... | collective-permute-start | bytes 786440 | tf_op jit(solution)/shard_map/while/body/ppermute | solution.py:39
  50.4 0.0 copy-done
  50.4 1.9 %collective-permute-start.4 = (bf16[4096,256]{1,0:T(8,128)(2,1)S(1)}, bf16[4096,256]{1,0:T(8,128)(2,1)S(1)}, u32[]{:S(2)}, u32[]{:S(2)}) collective-permute-start(bf16[4096,256]{1,0:T(8,128)(2,1)S(1)} %copy-done), channel_id=1, source_target_pairs={{0,1},{1,0},{2,3},{3,2},{4,5},{5,4},{6,7},{7,6},{8,9},{9,8},{10,11... | collective-permute-start | bytes 6291464 | tf_op jit(solution)/shard_map/while/body/ppermute | solution.py:213
  52.3 2.4 %collective-permute-start.5 = (bf16[4096,256]{1,0:T(8,128)(2,1)}, bf16[4096,256]{1,0:T(8,128)(2,1)S(1)}, u32[]{:S(2)}, u32[]{:S(2)}) collective-permute-start(bf16[4096,256]{1,0:T(8,128)(2,1)} %get-tuple-element.379), channel_id=1, source_target_pairs={{0,1},{1,0},{2,3},{3,2},{4,5},{5,4},{6,7},{7,6},{8,9},{9,8},{10,11... | collective-permute-start | bytes 6291464 | tf_op jit(solution)/shard_map/while/body/ppermute | solution.py:213
  54.8 0.7 bitcast_dynamic-update-slice_fusion.18
  55.5 0.1 slice_reduce_fusion.2
  55.6 3.8 %collective-permute-done = bf16[32,4096]{1,0:T(8,128)(2,1)S(1)} collective-permute-done((bf16[32,4096]{1,0:T(8,128)(2,1)S(1)}, bf16[32,4096]{1,0:T(8,128)(2,1)S(1)}, u32[]{:S(2)}, u32[]{:S(2)}) %collective-permute-start) | collective-permute-done | bytes 262176 | tf_op jit(solution)/shard_map/while/body/ppermute | solution.py:38
  59.4 2.1 %collective-permute-start.2 = (bf16[32,4096]{1,0:T(8,128)(2,1)S(1)}, bf16[32,4096]{1,0:T(8,128)(2,1)S(1)}, u32[]{:S(2)}, u32[]{:S(2)}) collective-permute-start(bf16[32,4096]{1,0:T(8,128)(2,1)S(1)} %collective-permute-done), channel_id=1, source_target_pairs={{0,2},{2,4},{4,6},{6,8},{8,10},{10,12},{12,14},{14,0},{1,3},{3,5},... | collective-permute-start | bytes 786440 | tf_op jit(solution)/shard_map/while/body/ppermute | solution.py:38
  61.5 0.0 collective-permute-done.1
  61.5 5.0 %collective-permute-start.3 = (bf16[32,4096]{1,0:T(8,128)(2,1)S(1)}, bf16[32,4096]{1,0:T(8,128)(2,1)S(1)}, u32[]{:S(2)}, u32[]{:S(2)}) collective-permute-start(bf16[32,4096]{1,0:T(8,128)(2,1)S(1)} %collective-permute-done.1), channel_id=1, source_target_pairs={{0,14},{2,0},{4,2},{6,4},{8,6},{10,8},{12,10},{14,12},{1,15},{3,1}... | collective-permute-start | bytes 786440 | tf_op jit(solution)/shard_map/while/body/ppermute | solution.py:39
  66.5 0.7 bitcast_dynamic-update-slice_fusion.19
  67.2 0.7 bitcast_dynamic-update-slice_fusion.20
  67.9 1.1 collective-permute-done.2
  69.1 0.7 bitcast_dynamic-update-slice_fusion.21
  69.8 0.6 collective-permute-done.3
  70.4 0.0 collective-permute-done.4
  70.4 0.0 collective-permute-done.5
  70.4 2.8 %collective-permute-start.6 = (bf16[32,4096]{1,0:T(8,128)(2,1)S(1)}, bf16[32,4096]{1,0:T(8,128)(2,1)S(1)}, u32[]{:S(2)}, u32[]{:S(2)}) collective-permute-start(bf16[32,4096]{1,0:T(8,128)(2,1)S(1)} %collective-permute-done.2), channel_id=1, source_target_pairs={{0,2},{2,4},{4,6},{6,8},{8,10},{10,12},{12,14},{14,0},{1,3},{3,5},... | collective-permute-start | bytes 786440 | tf_op jit(solution)/shard_map/while/body/ppermute | solution.py:38
  73.1 4.8 %collective-permute-start.7 = (bf16[32,4096]{1,0:T(8,128)(2,1)S(1)}, bf16[32,4096]{1,0:T(8,128)(2,1)S(1)}, u32[]{:S(2)}, u32[]{:S(2)}) collective-permute-start(bf16[32,4096]{1,0:T(8,128)(2,1)S(1)} %collective-permute-done.3), channel_id=1, source_target_pairs={{0,14},{2,0},{4,2},{6,4},{8,6},{10,8},{12,10},{14,12},{1,15},{3,1}... | collective-permute-start | bytes 786440 | tf_op jit(solution)/shard_map/while/body/ppermute | solution.py:39
  77.9 0.7 bitcast_dynamic-update-slice_fusion.22
  78.7 1.7 %collective-permute-done.6 = bf16[32,4096]{1,0:T(8,128)(2,1)S(1)} collective-permute-done((bf16[32,4096]{1,0:T(8,128)(2,1)S(1)}, bf16[32,4096]{1,0:T(8,128)(2,1)S(1)}, u32[]{:S(2)}, u32[]{:S(2)}) %collective-permute-start.6) | collective-permute-done | bytes 262176 | tf_op jit(solution)/shard_map/while/body/ppermute | solution.py:38
  80.3 1.9 %collective-permute-start.8 = (bf16[16,4096]{1,0:T(8,128)(2,1)S(1)}, bf16[16,4096]{1,0:T(8,128)(2,1)S(1)}, u32[]{:S(2)}, u32[]{:S(2)}) collective-permute-start(bf16[16,4096]{1,0:T(8,128)(2,1)S(1)} %slice.88), channel_id=1, source_target_pairs={{0,2},{2,4},{4,6},{6,8},{8,10},{10,12},{12,14},{14,0},{1,3},{3,5},... | collective-permute-start | bytes 393224 | tf_op jit(solution)/shard_map/while/body/ppermute | solution.py:44
  82.3 0.0 collective-permute-done.7
  82.3 5.1 %collective-permute-start.9 = (bf16[16,4096]{1,0:T(8,128)(2,1)S(1)}, bf16[16,4096]{1,0:T(8,128)(2,1)S(1)}, u32[]{:S(2)}, u32[]{:S(2)}) collective-permute-start(bf16[16,4096]{1,0:T(8,128)(2,1)S(1)} %slice.89), channel_id=1, source_target_pairs={{0,14},{2,0},{4,2},{6,4},{8,6},{10,8},{12,10},{14,12},{1,15},{3,1}... | collective-permute-start | bytes 393224 | tf_op jit(solution)/shard_map/while/body/ppermute | solution.py:45
  87.4 0.7 bitcast_dynamic-update-slice_fusion.23
  88.2 0.7 bitcast_dynamic-update-slice_fusion.24
  88.9 0.0 collective-permute-done.8
  88.9 0.7 bitcast_dynamic-update-slice_fusion.25
  89.5 0.4 collective-permute-done.9
  89.9 0.7 bitcast_dynamic-update-slice_fusion.26
  90.6 0.0 copy-done.2
  90.6 0.0 copy-done.4
  90.6 0.0 copy-start.3
  90.6 7.2 %logits.1 = (f32[256,512]{1,0:T(8,128)S(1)}, f32[256,512]{1,0:T(8,128)S(1)}, f32[8,8,256]{2,1,0:T(8,128)S(1)}) custom-call(bf16[8,32,4096]{2,1,0:T(8,128)(2,1)} %bitcast.45, bf16[8,32,4096]{2,1,0:T(8,128)(2,1)} %get-tuple-element.256.xt_ref, bf16[4096,256]{1,0:T(8,128)(2,1)} %get-tuple-element.452, bf16[4096,256]{1,0:T(8,128)(2,1)} %get-tuple-element.257.ws1_ref.w1_ref, ...), custom_call_target="tpu_custom_call" | custom-call | flops 2147483648 | bytes 12582912 | tf_op jit(solution)/shard_map/logits/pallas_call | solution.py:107
  97.9 14.5 %all_to_all.24.stats_ref = f32[8,8,256]{2,1,0:T(8,128)S(1)} all-to-all(f32[8,8,256]{2,1,0:T(8,128)S(1)} %get-tuple-element.259), channel_id=1, replica_groups=mesh['dp'=32,'y'=8,'core'=2] {'y'}, dimensions={0} | all-to-all | bytes 131072 | tf_op jit(solution)/shard_map/all_to_all | solution.py:22
  112.4 0.0 copy-done.1
  112.4 2.9 %gradient.1 = (bf16[256,4096]{1,0:T(8,128)(2,1)}, f32[64,128]{1,0:T(8,128)}) custom-call(f32[8,8,256]{2,1,0:T(8,128)S(1)} %all_to_all.24.stats_ref, f32[256,512]{1,0:T(8,128)S(1)} %get-tuple-element.260.s_ref, f32[256,512]{1,0:T(8,128)S(1)} %get-tuple-element.261.d_ref, bf16[4096,256]{1,0:T(8,128)(2,1)S(1)} %copy-done.1, bf16[4096,256]{1,0:T(8,128)(2,1)S(1)} %copy-done.3), custom_call_target="tpu_custom_call" | custom-call | flops 1073741824 | bytes 7340032 | tf_op jit(solution)/shard_map/gradient/pallas_call | solution.py:166
  115.3 0.0 reduce-scatter.2.cloned.1.call-update
  115.3 8.4 %all-to-all-start.2 = ((f32[64,1,128]{2,1,0:T(1,128)}), f32[64,1,128]{2,1,0:T(1,128)S(1)}, u32[]{:S(2)}, u32[]{:S(2)}) async-start(f32[64,1,128]{2,1,0:T(1,128)} %bitcast.2), calls=%async_computation.2 | async-start | bytes 65536 | tf_op jit(solution)/shard_map/all_to_all | solution.py:22
  124.3 7.2 %all-to-all-done.2 = f32[64,1,128]{2,1,0:T(1,128)S(1)} async-done(((f32[64,1,128]{2,1,0:T(1,128)}), f32[64,1,128]{2,1,0:T(1,128)S(1)}, u32[]{:S(2)}, u32[]{:S(2)}) %all-to-all-start.2) | async-done | bytes 32800 | tf_op jit(solution)/shard_map/all_to_all | solution.py:22
  131.5 0.1 reduce_sum.19
  131.6 0.6 fusion.9
  133.5 0.7 multiply_divide_fusion
  134.2 19.4 %reduce-scatter.2.cloned.1.call-done = bf16[32,4096]{1,0:T(8,128)(2,1)} async-done(((bf16[256,4096]{1,0:T(8,128)(2,1)}), bf16[32,4096]{1,0:T(8,128)(2,1)}) %reduce-scatter.2.cloned.1.call-update) | async-done | bytes 262160 | tf_op jit(solution)/shard_map/reduce_scatter | solution.py:231
  153.6 1.8 %multiply_convert_fusion = bf16[32,4096]{1,0:T(8,128)(2,1)} fusion(bf16[32,4096]{1,0:T(8,128)(2,1)} %reduce-scatter.2.cloned.1.call-done, f32[32]{0:T(128)S(1)} %multiply_divide_fusion), kind=kLoop, calls=%fused_computation.20 | loop fusion | flops 393216 | bytes 524416 | tf_op jit(solution)/shard_map/convert_element_type | solution.py:237
  (13 shorter events, 0.1 us)
Async XLA Ops:
  7.2 83.4 %all-gather.3.cloned.1.call-start = ((), (), s32[]{:S(2)}) async-start(), calls=%async_computation.5 | async-start | bytes 2359296 | tf_op jit(solution)/shard_map/all_gather | solution.py:217
  7.9 145.7 %reduce-scatter.2.cloned.1.call-start = ((), (), s32[]{:S(2)}) async-start(), calls=%async_computation.4 | async-start | bytes 2359296 | tf_op jit(solution)/shard_map/reduce_scatter | solution.py:231
  10.9 39.5 %copy-start = (bf16[4096,256]{1,0:T(8,128)(2,1)S(1)}, bf16[4096,256]{1,0:T(8,128)(2,1)}, u32[]{:S(2)}) copy-start(bf16[4096,256]{1,0:T(8,128)(2,1)} %get-tuple-element.378) | copy-start | bytes 6291460 | tf_op jit(solution)/shard_map/while
  11.9 30.6 %all-to-all-start = ((bf16[32,2,4224]{2,1,0:T(2,128)(2,1)}), bf16[32,2,4224]{2,1,0:T(2,128)(2,1)S(1)}, u32[]{:S(2)}, u32[]{:S(2)}) async-start(bf16[32,2,4224]{2,1,0:T(2,128)(2,1)} %reshape.98), calls=%async_computation | async-start | bytes 1081344 | tf_op jit(solution)/shard_map/while/body/all_to_all | solution.py:22
  43.1 16.3 %collective-permute-start = (bf16[32,4096]{1,0:T(8,128)(2,1)S(1)}, bf16[32,4096]{1,0:T(8,128)(2,1)S(1)}, u32[]{:S(2)}, u32[]{:S(2)}) collective-permute-start(bf16[32,4096]{1,0:T(8,128)(2,1)S(1)} %convolution_convert_fusion.5), channel_id=1, source_target_pairs={{0,2},{2,4},{4,6},{6,8},{8,10},{10,12},{12,14},{14,0},{1,3},{3,5},... | collective-permute-start | bytes 786440 | tf_op jit(solution)/shard_map/while/body/ppermute | solution.py:38
  46.6 14.9 %collective-permute-start.1 = (bf16[32,4096]{1,0:T(8,128)(2,1)S(1)}, bf16[32,4096]{1,0:T(8,128)(2,1)S(1)}, u32[]{:S(2)}, u32[]{:S(2)}) collective-permute-start(bf16[32,4096]{1,0:T(8,128)(2,1)S(1)} %convolution_convert_fusion.5), channel_id=1, source_target_pairs={{0,14},{2,0},{4,2},{6,4},{8,6},{10,8},{12,10},{14,12},{1,15},{3,1}... | collective-permute-start | bytes 786440 | tf_op jit(solution)/shard_map/while/body/ppermute | solution.py:39
  50.4 19.9 %collective-permute-start.4 = (bf16[4096,256]{1,0:T(8,128)(2,1)S(1)}, bf16[4096,256]{1,0:T(8,128)(2,1)S(1)}, u32[]{:S(2)}, u32[]{:S(2)}) collective-permute-start(bf16[4096,256]{1,0:T(8,128)(2,1)S(1)} %copy-done), channel_id=1, source_target_pairs={{0,1},{1,0},{2,3},{3,2},{4,5},{5,4},{6,7},{7,6},{8,9},{9,8},{10,11... | collective-permute-start | bytes 6291464 | tf_op jit(solution)/shard_map/while/body/ppermute | solution.py:213
  52.3 18.0 %collective-permute-start.5 = (bf16[4096,256]{1,0:T(8,128)(2,1)}, bf16[4096,256]{1,0:T(8,128)(2,1)S(1)}, u32[]{:S(2)}, u32[]{:S(2)}) collective-permute-start(bf16[4096,256]{1,0:T(8,128)(2,1)} %get-tuple-element.379), channel_id=1, source_target_pairs={{0,1},{1,0},{2,3},{3,2},{4,5},{5,4},{6,7},{7,6},{8,9},{9,8},{10,11... | collective-permute-start | bytes 6291464 | tf_op jit(solution)/shard_map/while/body/ppermute | solution.py:213
  59.4 9.7 %collective-permute-start.2 = (bf16[32,4096]{1,0:T(8,128)(2,1)S(1)}, bf16[32,4096]{1,0:T(8,128)(2,1)S(1)}, u32[]{:S(2)}, u32[]{:S(2)}) collective-permute-start(bf16[32,4096]{1,0:T(8,128)(2,1)S(1)} %collective-permute-done), channel_id=1, source_target_pairs={{0,2},{2,4},{4,6},{6,8},{8,10},{10,12},{12,14},{14,0},{1,3},{3,5},... | collective-permute-start | bytes 786440 | tf_op jit(solution)/shard_map/while/body/ppermute | solution.py:38
  61.5 8.8 %collective-permute-start.3 = (bf16[32,4096]{1,0:T(8,128)(2,1)S(1)}, bf16[32,4096]{1,0:T(8,128)(2,1)S(1)}, u32[]{:S(2)}, u32[]{:S(2)}) collective-permute-start(bf16[32,4096]{1,0:T(8,128)(2,1)S(1)} %collective-permute-done.1), channel_id=1, source_target_pairs={{0,14},{2,0},{4,2},{6,4},{8,6},{10,8},{12,10},{14,12},{1,15},{3,1}... | collective-permute-start | bytes 786440 | tf_op jit(solution)/shard_map/while/body/ppermute | solution.py:39
  70.4 20.2 %copy-start.2 = (bf16[4096,256]{1,0:T(8,128)(2,1)}, bf16[4096,256]{1,0:T(8,128)(2,1)S(1)}, u32[]{:S(2)}) copy-start(bf16[4096,256]{1,0:T(8,128)(2,1)S(1)} %collective-permute-done.4) | copy-start | bytes 6291460 | tf_op jit(solution)/shard_map/while
  70.4 20.2 %copy-start.4 = (bf16[4096,256]{1,0:T(8,128)(2,1)}, bf16[4096,256]{1,0:T(8,128)(2,1)S(1)}, u32[]{:S(2)}) copy-start(bf16[4096,256]{1,0:T(8,128)(2,1)S(1)} %collective-permute-done.5) | copy-start | bytes 6291460 | tf_op jit(solution)/shard_map/while
  70.4 10.0 %collective-permute-start.6 = (bf16[32,4096]{1,0:T(8,128)(2,1)S(1)}, bf16[32,4096]{1,0:T(8,128)(2,1)S(1)}, u32[]{:S(2)}, u32[]{:S(2)}) collective-permute-start(bf16[32,4096]{1,0:T(8,128)(2,1)S(1)} %collective-permute-done.2), channel_id=1, source_target_pairs={{0,2},{2,4},{4,6},{6,8},{8,10},{10,12},{12,14},{14,0},{1,3},{3,5},... | collective-permute-start | bytes 786440 | tf_op jit(solution)/shard_map/while/body/ppermute | solution.py:38
  73.1 9.1 %collective-permute-start.7 = (bf16[32,4096]{1,0:T(8,128)(2,1)S(1)}, bf16[32,4096]{1,0:T(8,128)(2,1)S(1)}, u32[]{:S(2)}, u32[]{:S(2)}) collective-permute-start(bf16[32,4096]{1,0:T(8,128)(2,1)S(1)} %collective-permute-done.3), channel_id=1, source_target_pairs={{0,14},{2,0},{4,2},{6,4},{8,6},{10,8},{12,10},{14,12},{1,15},{3,1}... | collective-permute-start | bytes 786440 | tf_op jit(solution)/shard_map/while/body/ppermute | solution.py:39
  80.3 8.5 %collective-permute-start.8 = (bf16[16,4096]{1,0:T(8,128)(2,1)S(1)}, bf16[16,4096]{1,0:T(8,128)(2,1)S(1)}, u32[]{:S(2)}, u32[]{:S(2)}) collective-permute-start(bf16[16,4096]{1,0:T(8,128)(2,1)S(1)} %slice.88), channel_id=1, source_target_pairs={{0,2},{2,4},{4,6},{6,8},{8,10},{10,12},{12,14},{14,0},{1,3},{3,5},... | collective-permute-start | bytes 393224 | tf_op jit(solution)/shard_map/while/body/ppermute | solution.py:44
  82.3 7.6 %collective-permute-start.9 = (bf16[16,4096]{1,0:T(8,128)(2,1)S(1)}, bf16[16,4096]{1,0:T(8,128)(2,1)S(1)}, u32[]{:S(2)}, u32[]{:S(2)}) collective-permute-start(bf16[16,4096]{1,0:T(8,128)(2,1)S(1)} %slice.89), channel_id=1, source_target_pairs={{0,14},{2,0},{4,2},{6,4},{8,6},{10,8},{12,10},{14,12},{1,15},{3,1}... | collective-permute-start | bytes 393224 | tf_op jit(solution)/shard_map/while/body/ppermute | solution.py:45
  90.6 21.8 %copy-start.1 = (bf16[4096,256]{1,0:T(8,128)(2,1)S(1)}, bf16[4096,256]{1,0:T(8,128)(2,1)}, u32[]{:S(2)}) copy-start(bf16[4096,256]{1,0:T(8,128)(2,1)} %get-tuple-element.452) | copy-start | bytes 6291460
  90.6 21.8 %copy-start.3 = (bf16[4096,256]{1,0:T(8,128)(2,1)S(1)}, bf16[4096,256]{1,0:T(8,128)(2,1)}, u32[]{:S(2)}) copy-start(bf16[4096,256]{1,0:T(8,128)(2,1)} %get-tuple-element.257.ws1_ref.w1_ref) | copy-start | bytes 6291460
  115.3 18.2 %copy-start.5 = (s32[32]{0:T(128)S(1)}, s32[32]{0:T(128)}, u32[]{:S(2)}) copy-start(s32[32]{0:T(128)} %param.12) | copy-start | bytes 388
  115.3 16.2 %all-to-all-start.2 = ((f32[64,1,128]{2,1,0:T(1,128)}), f32[64,1,128]{2,1,0:T(1,128)S(1)}, u32[]{:S(2)}, u32[]{:S(2)}) async-start(f32[64,1,128]{2,1,0:T(1,128)} %bitcast.2), calls=%async_computation.2 | async-start | bytes 65536 | tf_op jit(solution)/shard_map/all_to_all | solution.py:22
Sparse Core Ops, SparseCore 0:
  10.1 51.1 all-gather.2
  115.4 38.1 reduce-scatter.1

commit v4 on v3

--- a/solution.py
+++ b/solution.py
@@ -10,6 +10,7 @@
 CORES = 2
 STATS = 8
 STEPS = 4
+LOGITS_VMEM = 32 * 1024 * 1024
 GRADIENT_STEPS = 2
 VMEM_LIMIT = 16 * 1024 * 1024
 
@@ -56,78 +57,81 @@
     )()
 
 
-def logits_kernel(xs_ref, xt_ref, ws0_ref, ws1_ref, wt0_ref, wt1_ref, mask_ref, s_ref, d_ref, stats_ref):
-    step = pl.program_id(0)
-    rows, block = s_ref.shape[0], ws0_ref.shape[1]
-    xs = xs_ref[...].reshape(rows, xs_ref.shape[2])
-    xt = xt_ref[...].reshape(rows, xt_ref.shape[2])
-
-    @pl.when(step == 0)
-    def _():
-        s_ref[...] = jnp.zeros_like(s_ref)
-        d_ref[...] = jnp.zeros_like(d_ref)
-
-    s_ref[:, :block] += dot(xs, ws0_ref[...], 1, 0)
-    s_ref[:, block:] += dot(xs, ws1_ref[...], 1, 0)
-    d_ref[:, :block] += dot(xt, wt0_ref[...], 1, 0)
-    d_ref[:, block:] += dot(xt, wt1_ref[...], 1, 0)
-
-    @pl.when(step == pl.num_programs(0) - 1)
-    def _():
-        s, t = s_ref[...], d_ref[...]
-        d = s - t
-        d_ref[...] = d
-        s_top = jnp.max(s, axis=1, keepdims=True)
-        t_top = jnp.max(t, axis=1, keepdims=True)
-        e = jnp.exp(s - s_top)
-        columns = (
-            s_top,
-            t_top,
-            jnp.sum(e, axis=1, keepdims=True),
-            jnp.sum(jnp.exp(t - t_top), axis=1, keepdims=True),
-            jnp.sum(e * d, axis=1, keepdims=True),
-        )
-        lane = lax.broadcasted_iota(jnp.int32, (rows, 128), 1)
-        table = jnp.zeros((rows, 128), F32)
-        for j, column in enumerate(columns):
-            table = jnp.where(lane == j, column, table)
-        table = table.T[:STATS]
-        line = lax.broadcasted_iota(jnp.int32, (STATS, rows), 0)
-        table = jnp.where(line == len(columns), mask_ref[...], table)
-        stats_ref[...] = jnp.broadcast_to(table[None], stats_ref.shape)
+def logits_kernel(xs, xt, ws0, ws1, wt0, wt1, mask_ref, s_ref, d_ref, stats_ref, *scratch):
+    *held, sems = scratch
+    n_y, tok, width = xs.shape
+    rows, block = n_y * tok, ws0.shape[1]
+    depth = width // STEPS
+
+    def copies(side, k):
+        part = pl.ds(k * depth, depth)
+        for j, ref in enumerate(((xs, ws0, ws1), (xt, wt0, wt1))[side]):
+            at = (slice(None), slice(None), part) if j == 0 else (part, slice(None))
+            yield pltpu.make_async_copy(ref.at[at], held[3 * side + j].at[at], sems.at[3 * side + j, k])
+
+    for side in range(2):
+        for k in range(STEPS):
+            for copy in copies(side, k):
+                copy.start()
+
+    def product(side, out_ref):
+        x, w0, w1 = held[3 * side : 3 * side + 3]
+        for k in range(STEPS):
+            for copy in copies(side, k):
+                copy.wait()
+            part = pl.ds(k * depth, depth)
+            rows_in = x[:, :, part].reshape(rows, depth)
+            p0, p1 = dot(rows_in, w0[part, :], 1, 0), dot(rows_in, w1[part, :], 1, 0)
+            if k == 0:
+                out_ref[:, :block] = p0
+                out_ref[:, block:] = p1
+            else:
+                out_ref[:, :block] += p0
+                out_ref[:, block:] += p1
+
+    product(0, s_ref)
+    s = s_ref[...]
+    s_top = jnp.max(s, axis=1, keepdims=True)
+    s_sum = jnp.sum(jnp.exp(s - s_top), axis=1, keepdims=True)
+    product(1, d_ref)
+    s, t = s_ref[...], d_ref[...]
+    d = s - t
+    d_ref[...] = d
+    t_top = jnp.max(t, axis=1, keepdims=True)
+    t_sum = jnp.sum(jnp.exp(t - t_top), axis=1, keepdims=True)
+    cross = jnp.sum(jnp.exp(s - s_top) * d, axis=1, keepdims=True)
+    columns = (s_top, t_top, s_sum, t_sum, cross)
+    lane = lax.broadcasted_iota(jnp.int32, (rows, 128), 1)
+    table = jnp.zeros((rows, 128), F32)
+    for j, column in enumerate(columns):
+        table = jnp.where(lane == j, column, table)
+    table = table.T[:STATS]
+    line = lax.broadcasted_iota(jnp.int32, (STATS, rows), 0)
+    table = jnp.where(line == len(columns), mask_ref[...], table)
+    stats_ref[...] = jnp.broadcast_to(table[None], stats_ref.shape)
 
 
 def logits(student_rows, teacher_rows, heads, mask):
     n_y, tok, width = student_rows.shape
-    rows = n_y * tok
-    block = heads[0].shape[1]
-    depth = width // STEPS
-    head = pl.BlockSpec((depth, block), lambda k: (k, 0))
-    whole = pl.BlockSpec((rows, CORES * block), lambda k: (0, 0))
+    rows, block = n_y * tok, heads[0].shape[1]
+    far, near = pl.BlockSpec(memory_space=pltpu.HBM), pl.BlockSpec(memory_space=pltpu.VMEM)
+    side = [pltpu.VMEM(student_rows.shape, BF), pltpu.VMEM((width, block), BF), pltpu.VMEM((width, block), BF)]
     return pl.pallas_call(
         logits_kernel,
-        grid=(STEPS,),
-        in_specs=[
-            pl.BlockSpec((n_y, tok, depth), lambda k: (0, 0, k)),
-            pl.BlockSpec((n_y, tok, depth), lambda k: (0, 0, k)),
-            head,
-            head,
-            head,
-            head,
-            pl.BlockSpec((1, rows), lambda k: (0, 0)),
-        ],
-        out_specs=[whole, whole, pl.BlockSpec((n_y, STATS, rows), lambda k: (0, 0, 0))],
+        in_specs=[far] * 6 + [near],
+        out_specs=[near] * 3,
         out_shape=[
             jax.ShapeDtypeStruct((rows, CORES * block), F32),
             jax.ShapeDtypeStruct((rows, CORES * block), F32),
             jax.ShapeDtypeStruct((n_y, STATS, rows), F32),
         ],
-        compiler_params=pltpu.CompilerParams(vmem_limit_bytes=VMEM_LIMIT),
+        scratch_shapes=side + side + [pltpu.SemaphoreType.DMA((6, STEPS))],
+        compiler_params=pltpu.CompilerParams(vmem_limit_bytes=LOGITS_VMEM),
         cost_estimate=pl.CostEstimate(
             flops=8 * rows * width * block, bytes_accessed=12 * 2**20, transcendentals=2**18
         ),
         name="logits",
-    )(student_rows, teacher_rows, *heads, mask)
+    )(*(pltpu.with_memory_space_constraint(x, pltpu.HBM) for x in (student_rows, teacher_rows, *heads)), mask)
 
 
 def gradient_kernel(stats_ref, s_ref, d_ref, w0_ref, w1_ref, out_ref, parts_ref, grad_ref):
@@ -222,9 +226,6 @@
     mine = jnp.arange(rows, dtype=jnp.int32) // tok == lax.axis_index("y")
     mask = jnp.where(mine, jnp.tile(token_mask.astype(F32), n_y), 0.0)[None]
 
-    student_rows, teacher_rows, teacher_head = (
-        pltpu.with_memory_space_constraint(x, pltpu.HBM) for x in (student_rows, teacher_rows, teacher_head)
-    )
     s, d, stats = logits(student_rows, teacher_rows, (student_head, other[0], teacher_head, other[1]), mask)
     stats = exchange(stats, "y")
     partial, parts = gradient(stats, s, d, (student_head, other[0]), n_dp * CORES)

time: 164 us -> 163 us (level)
  no operation moved by 1% of the time
where the time goes in v4:
time: 163 us; the launch traced here: 162 us
  starting transfers between devices  55.1 us (34%)
  waiting for transfers between devices  52 us (32%)
  between operations  17.2 us (11%)
  blocking collectives  14.5 us (9%)
  local copies, waits for them, and re-layouts  8.51 us (5%)
  Pallas kernels  8.5 us (5%)
  other arithmetic  5.1 us (3%)
    all_to_all x2, waiting for transfers between devices, exchange(): return lax.all_to_all(x, axis, split_axis=0, concat_axis=0, tiled=True)  24.3 us
    all_to_all x2, starting transfers between devices, exchange(): return lax.all_to_all(x, axis, split_axis=0, concat_axis=0, tiled=True)  21.8 us
    reduce_scatter x1, waiting for transfers between devices, body(): summed = lax.psum_scatter(partial, 'y', scatter_dimension=0, tiled=True)  19.4 us
    all_to_all x1, blocking collectives, exchange(): return lax.all_to_all(x, axis, split_axis=0, concat_axis=0, tiled=True)  14.5 us
    ppermute x3, starting transfers between devices, ring_gather(): l = lax.ppermute(l, axis, left)  13.5 us
    ppermute x3, starting transfers between devices, ring_gather(): r = lax.ppermute(r, axis, right)  8.33 us
    ppermute x3, waiting for transfers between devices, ring_gather(): r = lax.ppermute(r, axis, right)  6.63 us
    dynamic_update_slice x9, local copies, waits for them, and re-layouts, put(): lax.dynamic_update_slice(out, block[None], (lax.rem(owner, n), row, 0))  6.41 us
  transfers between devices with their start and end apart: 14, of which 8 were waited for; matrix products, arithmetic and copies ran while one was open for 8% of the time, Pallas kernels for 0%

profile of v4, /device:TPU:6, one launch (start us, length us, event | category | flops | bytes accessed | tf_op | source)
XLA Modules:
  0.0 161.7 jit_solution(13318099687818418569)
XLA Ops:
  7.2 0.0 all-gather.3.cloned.1.call-start
  7.2 0.7 all-gather.3.cloned.1.call-update
  7.9 0.0 reduce-scatter.2.cloned.1.call-start
  8.0 0.7 fusion.8
  8.6 0.2 convert_reduce_fusion
  8.8 0.7 convert_element_type.56
  9.5 0.1 tile.10
  9.6 0.1 broadcast_in_dim.113
  9.6 1.0 pad_maximum_fusion
  10.6 80.0 %while.22 = (s32[]{:T(128)}, s32[32]{0:T(128)S(1)}, bf16[8,32,4096]{2,1,0:T(8,128)(2,1)}, bf16[4096,256]{1,0:T(8,128)(2,1)}, bf16[4096,256]{1,0:T(8,128)(2,1)}, ...) while((s32[]{:T(128)}, s32[32]{0:T(128)S(1)}, ...), condition=%wide.region_2.3_spmd.clone, body=%wide.region_1.2_spmd.clone.sunk | while | flops 34484352 | bytes 59386968 | solution.py:224
  10.6 0.3 convolution_convert_fusion.4
  10.9 0.0 copy-start
  10.9 1.0 reshape.98
  11.9 13.4 %all-to-all-start = ((bf16[32,2,4224]{2,1,0:T(2,128)(2,1)}), bf16[32,2,4224]{2,1,0:T(2,128)(2,1)S(1)}, u32[]{:S(2)}, u32[]{:S(2)}) async-start(bf16[32,2,4224]{2,1,0:T(2,128)(2,1)} %reshape.98), calls=%async_computation | async-start | bytes 1081344 | tf_op jit(solution)/shard_map/while/body/all_to_all | solution.py:23
  25.4 17.1 %all-to-all-done = bf16[32,2,4224]{2,1,0:T(2,128)(2,1)S(1)} async-done(((bf16[32,2,4224]{2,1,0:T(2,128)(2,1)}), bf16[32,2,4224]{2,1,0:T(2,128)(2,1)S(1)}, u32[]{:S(2)}, u32[]{:S(2)}) %all-to-all-start) | async-done | bytes 540704 | tf_op jit(solution)/shard_map/while/body/all_to_all | solution.py:23
  42.5 0.2 reshape.99
  42.7 0.1 fusion.16
  42.9 0.2 convolution_convert_fusion.5
  43.1 3.5 %collective-permute-start = (bf16[32,4096]{1,0:T(8,128)(2,1)S(1)}, bf16[32,4096]{1,0:T(8,128)(2,1)S(1)}, u32[]{:S(2)}, u32[]{:S(2)}) collective-permute-start(bf16[32,4096]{1,0:T(8,128)(2,1)S(1)} %convolution_convert_fusion.5), channel_id=1, source_target_pairs={{0,2},{2,4},{4,6},{6,8},{8,10},{10,12},{12,14},{14,0},{1,3},{3,5},... | collective-permute-start | bytes 786440 | tf_op jit(solution)/shard_map/while/body/ppermute | solution.py:39
  46.6 3.8 %collective-permute-start.1 = (bf16[32,4096]{1,0:T(8,128)(2,1)S(1)}, bf16[32,4096]{1,0:T(8,128)(2,1)S(1)}, u32[]{:S(2)}, u32[]{:S(2)}) collective-permute-start(bf16[32,4096]{1,0:T(8,128)(2,1)S(1)} %convolution_convert_fusion.5), channel_id=1, source_target_pairs={{0,14},{2,0},{4,2},{6,4},{8,6},{10,8},{12,10},{14,12},{1,15},{3,1}... | collective-permute-start | bytes 786440 | tf_op jit(solution)/shard_map/while/body/ppermute | solution.py:40
  50.4 0.0 copy-done
  50.4 1.9 %collective-permute-start.4 = (bf16[4096,256]{1,0:T(8,128)(2,1)S(1)}, bf16[4096,256]{1,0:T(8,128)(2,1)S(1)}, u32[]{:S(2)}, u32[]{:S(2)}) collective-permute-start(bf16[4096,256]{1,0:T(8,128)(2,1)S(1)} %copy-done), channel_id=1, source_target_pairs={{0,1},{1,0},{2,3},{3,2},{4,5},{5,4},{6,7},{7,6},{8,9},{9,8},{10,11... | collective-permute-start | bytes 6291464 | tf_op jit(solution)/shard_map/while/body/ppermute | solution.py:217
  52.3 2.4 %collective-permute-start.5 = (bf16[4096,256]{1,0:T(8,128)(2,1)}, bf16[4096,256]{1,0:T(8,128)(2,1)S(1)}, u32[]{:S(2)}, u32[]{:S(2)}) collective-permute-start(bf16[4096,256]{1,0:T(8,128)(2,1)} %get-tuple-element.379), channel_id=1, source_target_pairs={{0,1},{1,0},{2,3},{3,2},{4,5},{5,4},{6,7},{7,6},{8,9},{9,8},{10,11... | collective-permute-start | bytes 6291464 | tf_op jit(solution)/shard_map/while/body/ppermute | solution.py:217
  54.8 0.7 bitcast_dynamic-update-slice_fusion.18
  55.5 0.1 slice_reduce_fusion.2
  55.6 3.8 %collective-permute-done = bf16[32,4096]{1,0:T(8,128)(2,1)S(1)} collective-permute-done((bf16[32,4096]{1,0:T(8,128)(2,1)S(1)}, bf16[32,4096]{1,0:T(8,128)(2,1)S(1)}, u32[]{:S(2)}, u32[]{:S(2)}) %collective-permute-start) | collective-permute-done | bytes 262176 | tf_op jit(solution)/shard_map/while/body/ppermute | solution.py:39
  59.4 2.1 %collective-permute-start.2 = (bf16[32,4096]{1,0:T(8,128)(2,1)S(1)}, bf16[32,4096]{1,0:T(8,128)(2,1)S(1)}, u32[]{:S(2)}, u32[]{:S(2)}) collective-permute-start(bf16[32,4096]{1,0:T(8,128)(2,1)S(1)} %collective-permute-done), channel_id=1, source_target_pairs={{0,2},{2,4},{4,6},{6,8},{8,10},{10,12},{12,14},{14,0},{1,3},{3,5},... | collective-permute-start | bytes 786440 | tf_op jit(solution)/shard_map/while/body/ppermute | solution.py:39
  61.5 0.0 collective-permute-done.1
  61.5 5.0 %collective-permute-start.3 = (bf16[32,4096]{1,0:T(8,128)(2,1)S(1)}, bf16[32,4096]{1,0:T(8,128)(2,1)S(1)}, u32[]{:S(2)}, u32[]{:S(2)}) collective-permute-start(bf16[32,4096]{1,0:T(8,128)(2,1)S(1)} %collective-permute-done.1), channel_id=1, source_target_pairs={{0,14},{2,0},{4,2},{6,4},{8,6},{10,8},{12,10},{14,12},{1,15},{3,1}... | collective-permute-start | bytes 786440 | tf_op jit(solution)/shard_map/while/body/ppermute | solution.py:40
  66.5 0.7 bitcast_dynamic-update-slice_fusion.19
  67.2 0.7 bitcast_dynamic-update-slice_fusion.20
  67.9 1.1 collective-permute-done.2
  69.1 0.7 bitcast_dynamic-update-slice_fusion.21
  69.8 0.6 collective-permute-done.3
  70.4 0.0 collective-permute-done.4
  70.4 0.0 collective-permute-done.5
  70.4 2.8 %collective-permute-start.6 = (bf16[32,4096]{1,0:T(8,128)(2,1)S(1)}, bf16[32,4096]{1,0:T(8,128)(2,1)S(1)}, u32[]{:S(2)}, u32[]{:S(2)}) collective-permute-start(bf16[32,4096]{1,0:T(8,128)(2,1)S(1)} %collective-permute-done.2), channel_id=1, source_target_pairs={{0,2},{2,4},{4,6},{6,8},{8,10},{10,12},{12,14},{14,0},{1,3},{3,5},... | collective-permute-start | bytes 786440 | tf_op jit(solution)/shard_map/while/body/ppermute | solution.py:39
  73.1 4.8 %collective-permute-start.7 = (bf16[32,4096]{1,0:T(8,128)(2,1)S(1)}, bf16[32,4096]{1,0:T(8,128)(2,1)S(1)}, u32[]{:S(2)}, u32[]{:S(2)}) collective-permute-start(bf16[32,4096]{1,0:T(8,128)(2,1)S(1)} %collective-permute-done.3), channel_id=1, source_target_pairs={{0,14},{2,0},{4,2},{6,4},{8,6},{10,8},{12,10},{14,12},{1,15},{3,1}... | collective-permute-start | bytes 786440 | tf_op jit(solution)/shard_map/while/body/ppermute | solution.py:40
  77.9 0.7 bitcast_dynamic-update-slice_fusion.22
  78.7 1.7 %collective-permute-done.6 = bf16[32,4096]{1,0:T(8,128)(2,1)S(1)} collective-permute-done((bf16[32,4096]{1,0:T(8,128)(2,1)S(1)}, bf16[32,4096]{1,0:T(8,128)(2,1)S(1)}, u32[]{:S(2)}, u32[]{:S(2)}) %collective-permute-start.6) | collective-permute-done | bytes 262176 | tf_op jit(solution)/shard_map/while/body/ppermute | solution.py:39
  80.3 1.9 %collective-permute-start.8 = (bf16[16,4096]{1,0:T(8,128)(2,1)S(1)}, bf16[16,4096]{1,0:T(8,128)(2,1)S(1)}, u32[]{:S(2)}, u32[]{:S(2)}) collective-permute-start(bf16[16,4096]{1,0:T(8,128)(2,1)S(1)} %slice.88), channel_id=1, source_target_pairs={{0,2},{2,4},{4,6},{6,8},{8,10},{10,12},{12,14},{14,0},{1,3},{3,5},... | collective-permute-start | bytes 393224 | tf_op jit(solution)/shard_map/while/body/ppermute | solution.py:45
  82.3 0.0 collective-permute-done.7
  82.3 5.1 %collective-permute-start.9 = (bf16[16,4096]{1,0:T(8,128)(2,1)S(1)}, bf16[16,4096]{1,0:T(8,128)(2,1)S(1)}, u32[]{:S(2)}, u32[]{:S(2)}) collective-permute-start(bf16[16,4096]{1,0:T(8,128)(2,1)S(1)} %slice.89), channel_id=1, source_target_pairs={{0,14},{2,0},{4,2},{6,4},{8,6},{10,8},{12,10},{14,12},{1,15},{3,1}... | collective-permute-start | bytes 393224 | tf_op jit(solution)/shard_map/while/body/ppermute | solution.py:46
  87.4 0.7 bitcast_dynamic-update-slice_fusion.23
  88.2 0.7 bitcast_dynamic-update-slice_fusion.24
  88.9 0.0 collective-permute-done.8
  88.9 0.7 bitcast_dynamic-update-slice_fusion.25
  89.5 0.4 collective-permute-done.9
  89.9 0.7 bitcast_dynamic-update-slice_fusion.26
  90.6 0.0 copy-done.2
  90.6 0.0 copy-done.4
  90.6 0.0 copy-start.3
  90.6 5.6 %logits.1 = (f32[256,512]{1,0:T(8,128)S(1)}, f32[256,512]{1,0:T(8,128)S(1)}, f32[8,8,256]{2,1,0:T(8,128)S(1)}) custom-call(bf16[8,32,4096]{2,1,0:T(8,128)(2,1)} %bitcast.45, bf16[8,32,4096]{2,1,0:T(8,128)(2,1)} %get-tuple-element.256.xt, bf16[4096,256]{1,0:T(8,128)(2,1)} %get-tuple-element.452, bf16[4096,256]{1,0:T(8,128)(2,1)} %get-tuple-element.257.ws1.w1_ref, ...), custom_call_target="tpu_custom_call" | custom-call | flops 2147483648 | bytes 12582912 | tf_op jit(solution)/shard_map/logits/pallas_call | solution.py:119
  96.2 14.5 %all_to_all.24.stats_ref = f32[8,8,256]{2,1,0:T(8,128)S(1)} all-to-all(f32[8,8,256]{2,1,0:T(8,128)S(1)} %get-tuple-element.259), channel_id=1, replica_groups=mesh['dp'=32,'y'=8,'core'=2] {'y'}, dimensions={0} | all-to-all | bytes 131072 | tf_op jit(solution)/shard_map/all_to_all | solution.py:23
  110.8 0.0 copy-done.1
  110.8 2.9 %gradient.1 = (bf16[256,4096]{1,0:T(8,128)(2,1)}, f32[64,128]{1,0:T(8,128)}) custom-call(f32[8,8,256]{2,1,0:T(8,128)S(1)} %all_to_all.24.stats_ref, f32[256,512]{1,0:T(8,128)S(1)} %get-tuple-element.260.s_ref, f32[256,512]{1,0:T(8,128)S(1)} %get-tuple-element.261.d_ref, bf16[4096,256]{1,0:T(8,128)(2,1)S(1)} %copy-done.1, bf16[4096,256]{1,0:T(8,128)(2,1)S(1)} %copy-done.3), custom_call_target="tpu_custom_call" | custom-call | flops 1073741824 | bytes 7340032 | tf_op jit(solution)/shard_map/gradient/pallas_call | solution.py:170
  113.6 0.0 reduce-scatter.2.cloned.1.call-update
  113.7 8.4 %all-to-all-start.2 = ((f32[64,1,128]{2,1,0:T(1,128)}), f32[64,1,128]{2,1,0:T(1,128)S(1)}, u32[]{:S(2)}, u32[]{:S(2)}) async-start(f32[64,1,128]{2,1,0:T(1,128)} %bitcast.2), calls=%async_computation.2 | async-start | bytes 65536 | tf_op jit(solution)/shard_map/all_to_all | solution.py:23
  122.7 7.2 %all-to-all-done.2 = f32[64,1,128]{2,1,0:T(1,128)S(1)} async-done(((f32[64,1,128]{2,1,0:T(1,128)}), f32[64,1,128]{2,1,0:T(1,128)S(1)}, u32[]{:S(2)}, u32[]{:S(2)}) %all-to-all-start.2) | async-done | bytes 32800 | tf_op jit(solution)/shard_map/all_to_all | solution.py:23
  129.8 0.1 reduce_sum.19
  129.9 0.6 fusion.9
  131.9 0.7 multiply_divide_fusion
  132.5 19.4 %reduce-scatter.2.cloned.1.call-done = bf16[32,4096]{1,0:T(8,128)(2,1)} async-done(((bf16[256,4096]{1,0:T(8,128)(2,1)}), bf16[32,4096]{1,0:T(8,128)(2,1)}) %reduce-scatter.2.cloned.1.call-update) | async-done | bytes 262160 | tf_op jit(solution)/shard_map/reduce_scatter | solution.py:232
  152.0 1.8 %multiply_convert_fusion = bf16[32,4096]{1,0:T(8,128)(2,1)} fusion(bf16[32,4096]{1,0:T(8,128)(2,1)} %reduce-scatter.2.cloned.1.call-done, f32[32]{0:T(128)S(1)} %multiply_divide_fusion), kind=kLoop, calls=%fused_computation.20 | loop fusion | flops 393216 | bytes 524416 | tf_op jit(solution)/shard_map/convert_element_type | solution.py:238
  (13 shorter events, 0.1 us)
Async XLA Ops:
  7.2 83.4 %all-gather.3.cloned.1.call-start = ((), (), s32[]{:S(2)}) async-start(), calls=%async_computation.5 | async-start | bytes 2359296 | tf_op jit(solution)/shard_map/all_gather | solution.py:221
  7.9 144.1 %reduce-scatter.2.cloned.1.call-start = ((), (), s32[]{:S(2)}) async-start(), calls=%async_computation.4 | async-start | bytes 2359296 | tf_op jit(solution)/shard_map/reduce_scatter | solution.py:232
  10.9 39.5 %copy-start = (bf16[4096,256]{1,0:T(8,128)(2,1)S(1)}, bf16[4096,256]{1,0:T(8,128)(2,1)}, u32[]{:S(2)}) copy-start(bf16[4096,256]{1,0:T(8,128)(2,1)} %get-tuple-element.378) | copy-start | bytes 6291460 | tf_op jit(solution)/shard_map/while
  11.9 30.6 %all-to-all-start = ((bf16[32,2,4224]{2,1,0:T(2,128)(2,1)}), bf16[32,2,4224]{2,1,0:T(2,128)(2,1)S(1)}, u32[]{:S(2)}, u32[]{:S(2)}) async-start(bf16[32,2,4224]{2,1,0:T(2,128)(2,1)} %reshape.98), calls=%async_computation | async-start | bytes 1081344 | tf_op jit(solution)/shard_map/while/body/all_to_all | solution.py:23
  43.1 16.3 %collective-permute-start = (bf16[32,4096]{1,0:T(8,128)(2,1)S(1)}, bf16[32,4096]{1,0:T(8,128)(2,1)S(1)}, u32[]{:S(2)}, u32[]{:S(2)}) collective-permute-start(bf16[32,4096]{1,0:T(8,128)(2,1)S(1)} %convolution_convert_fusion.5), channel_id=1, source_target_pairs={{0,2},{2,4},{4,6},{6,8},{8,10},{10,12},{12,14},{14,0},{1,3},{3,5},... | collective-permute-start | bytes 786440 | tf_op jit(solution)/shard_map/while/body/ppermute | solution.py:39
  46.6 14.9 %collective-permute-start.1 = (bf16[32,4096]{1,0:T(8,128)(2,1)S(1)}, bf16[32,4096]{1,0:T(8,128)(2,1)S(1)}, u32[]{:S(2)}, u32[]{:S(2)}) collective-permute-start(bf16[32,4096]{1,0:T(8,128)(2,1)S(1)} %convolution_convert_fusion.5), channel_id=1, source_target_pairs={{0,14},{2,0},{4,2},{6,4},{8,6},{10,8},{12,10},{14,12},{1,15},{3,1}... | collective-permute-start | bytes 786440 | tf_op jit(solution)/shard_map/while/body/ppermute | solution.py:40
  50.4 19.9 %collective-permute-start.4 = (bf16[4096,256]{1,0:T(8,128)(2,1)S(1)}, bf16[4096,256]{1,0:T(8,128)(2,1)S(1)}, u32[]{:S(2)}, u32[]{:S(2)}) collective-permute-start(bf16[4096,256]{1,0:T(8,128)(2,1)S(1)} %copy-done), channel_id=1, source_target_pairs={{0,1},{1,0},{2,3},{3,2},{4,5},{5,4},{6,7},{7,6},{8,9},{9,8},{10,11... | collective-permute-start | bytes 6291464 | tf_op jit(solution)/shard_map/while/body/ppermute | solution.py:217
  52.3 18.0 %collective-permute-start.5 = (bf16[4096,256]{1,0:T(8,128)(2,1)}, bf16[4096,256]{1,0:T(8,128)(2,1)S(1)}, u32[]{:S(2)}, u32[]{:S(2)}) collective-permute-start(bf16[4096,256]{1,0:T(8,128)(2,1)} %get-tuple-element.379), channel_id=1, source_target_pairs={{0,1},{1,0},{2,3},{3,2},{4,5},{5,4},{6,7},{7,6},{8,9},{9,8},{10,11... | collective-permute-start | bytes 6291464 | tf_op jit(solution)/shard_map/while/body/ppermute | solution.py:217
  59.4 9.7 %collective-permute-start.2 = (bf16[32,4096]{1,0:T(8,128)(2,1)S(1)}, bf16[32,4096]{1,0:T(8,128)(2,1)S(1)}, u32[]{:S(2)}, u32[]{:S(2)}) collective-permute-start(bf16[32,4096]{1,0:T(8,128)(2,1)S(1)} %collective-permute-done), channel_id=1, source_target_pairs={{0,2},{2,4},{4,6},{6,8},{8,10},{10,12},{12,14},{14,0},{1,3},{3,5},... | collective-permute-start | bytes 786440 | tf_op jit(solution)/shard_map/while/body/ppermute | solution.py:39
  61.5 8.8 %collective-permute-start.3 = (bf16[32,4096]{1,0:T(8,128)(2,1)S(1)}, bf16[32,4096]{1,0:T(8,128)(2,1)S(1)}, u32[]{:S(2)}, u32[]{:S(2)}) collective-permute-start(bf16[32,4096]{1,0:T(8,128)(2,1)S(1)} %collective-permute-done.1), channel_id=1, source_target_pairs={{0,14},{2,0},{4,2},{6,4},{8,6},{10,8},{12,10},{14,12},{1,15},{3,1}... | collective-permute-start | bytes 786440 | tf_op jit(solution)/shard_map/while/body/ppermute | solution.py:40
  70.4 20.2 %copy-start.2 = (bf16[4096,256]{1,0:T(8,128)(2,1)}, bf16[4096,256]{1,0:T(8,128)(2,1)S(1)}, u32[]{:S(2)}) copy-start(bf16[4096,256]{1,0:T(8,128)(2,1)S(1)} %collective-permute-done.4) | copy-start | bytes 6291460 | tf_op jit(solution)/shard_map/while
  70.4 20.2 %copy-start.4 = (bf16[4096,256]{1,0:T(8,128)(2,1)}, bf16[4096,256]{1,0:T(8,128)(2,1)S(1)}, u32[]{:S(2)}) copy-start(bf16[4096,256]{1,0:T(8,128)(2,1)S(1)} %collective-permute-done.5) | copy-start | bytes 6291460 | tf_op jit(solution)/shard_map/while
  70.4 10.0 %collective-permute-start.6 = (bf16[32,4096]{1,0:T(8,128)(2,1)S(1)}, bf16[32,4096]{1,0:T(8,128)(2,1)S(1)}, u32[]{:S(2)}, u32[]{:S(2)}) collective-permute-start(bf16[32,4096]{1,0:T(8,128)(2,1)S(1)} %collective-permute-done.2), channel_id=1, source_target_pairs={{0,2},{2,4},{4,6},{6,8},{8,10},{10,12},{12,14},{14,0},{1,3},{3,5},... | collective-permute-start | bytes 786440 | tf_op jit(solution)/shard_map/while/body/ppermute | solution.py:39
  73.1 9.1 %collective-permute-start.7 = (bf16[32,4096]{1,0:T(8,128)(2,1)S(1)}, bf16[32,4096]{1,0:T(8,128)(2,1)S(1)}, u32[]{:S(2)}, u32[]{:S(2)}) collective-permute-start(bf16[32,4096]{1,0:T(8,128)(2,1)S(1)} %collective-permute-done.3), channel_id=1, source_target_pairs={{0,14},{2,0},{4,2},{6,4},{8,6},{10,8},{12,10},{14,12},{1,15},{3,1}... | collective-permute-start | bytes 786440 | tf_op jit(solution)/shard_map/while/body/ppermute | solution.py:40
  80.3 8.5 %collective-permute-start.8 = (bf16[16,4096]{1,0:T(8,128)(2,1)S(1)}, bf16[16,4096]{1,0:T(8,128)(2,1)S(1)}, u32[]{:S(2)}, u32[]{:S(2)}) collective-permute-start(bf16[16,4096]{1,0:T(8,128)(2,1)S(1)} %slice.88), channel_id=1, source_target_pairs={{0,2},{2,4},{4,6},{6,8},{8,10},{10,12},{12,14},{14,0},{1,3},{3,5},... | collective-permute-start | bytes 393224 | tf_op jit(solution)/shard_map/while/body/ppermute | solution.py:45
  82.3 7.6 %collective-permute-start.9 = (bf16[16,4096]{1,0:T(8,128)(2,1)S(1)}, bf16[16,4096]{1,0:T(8,128)(2,1)S(1)}, u32[]{:S(2)}, u32[]{:S(2)}) collective-permute-start(bf16[16,4096]{1,0:T(8,128)(2,1)S(1)} %slice.89), channel_id=1, source_target_pairs={{0,14},{2,0},{4,2},{6,4},{8,6},{10,8},{12,10},{14,12},{1,15},{3,1}... | collective-permute-start | bytes 393224 | tf_op jit(solution)/shard_map/while/body/ppermute | solution.py:46
  90.6 20.2 %copy-start.1 = (bf16[4096,256]{1,0:T(8,128)(2,1)S(1)}, bf16[4096,256]{1,0:T(8,128)(2,1)}, u32[]{:S(2)}) copy-start(bf16[4096,256]{1,0:T(8,128)(2,1)} %get-tuple-element.452) | copy-start | bytes 6291460
  90.6 20.2 %copy-start.3 = (bf16[4096,256]{1,0:T(8,128)(2,1)S(1)}, bf16[4096,256]{1,0:T(8,128)(2,1)}, u32[]{:S(2)}) copy-start(bf16[4096,256]{1,0:T(8,128)(2,1)} %get-tuple-element.257.ws1.w1_ref) | copy-start | bytes 6291460
  113.6 18.2 %copy-start.5 = (s32[32]{0:T(128)S(1)}, s32[32]{0:T(128)}, u32[]{:S(2)}) copy-start(s32[32]{0:T(128)} %param.12) | copy-start | bytes 388
  113.7 16.2 %all-to-all-start.2 = ((f32[64,1,128]{2,1,0:T(1,128)}), f32[64,1,128]{2,1,0:T(1,128)S(1)}, u32[]{:S(2)}, u32[]{:S(2)}) async-start(f32[64,1,128]{2,1,0:T(1,128)} %bitcast.2), calls=%async_computation.2 | async-start | bytes 65536 | tf_op jit(solution)/shard_map/all_to_all | solution.py:23
Sparse Core Ops, SparseCore 0:
  10.1 51.1 all-gather.2
  113.8 38.1 reduce-scatter.1

commit v5 on v4

--- a/solution.py
+++ b/solution.py
@@ -10,7 +10,7 @@
 CORES = 2
 STATS = 8
 STEPS = 4
-LOGITS_VMEM = 32 * 1024 * 1024
+LOGITS_VMEM = 24 * 1024 * 1024
 GRADIENT_STEPS = 2
 VMEM_LIMIT = 16 * 1024 * 1024
 
@@ -48,16 +48,17 @@
     return put(out, l, me + n // 2, half), beside
 
 
-def buffers(*shapes):
+def buffers(near, *far):
     return pl.pallas_call(
         lambda *refs: None,
-        out_specs=[pl.BlockSpec(memory_space=pl.ANY) for _ in shapes],
-        out_shape=[pltpu.HBM(shape, BF) for shape in shapes],
+        out_specs=[pl.BlockSpec(memory_space=pltpu.VMEM)] + [pl.BlockSpec(memory_space=pl.ANY)] * len(far),
+        out_shape=[pltpu.VMEM(near, BF)] + [pltpu.HBM(shape, BF) for shape in far],
+        compiler_params=pltpu.CompilerParams(vmem_limit_bytes=VMEM_LIMIT),
         name="buffers",
     )()
 
 
-def logits_kernel(xs, xt, ws0, ws1, wt0, wt1, mask_ref, s_ref, d_ref, stats_ref, *scratch):
+def logits_kernel(me_ref, xs, xt, ws0, ws1, wt0, wt1, mask_ref, s_ref, d_ref, stats_ref, *scratch):
     *held, sems = scratch
     n_y, tok, width = xs.shape
     rows, block = n_y * tok, ws0.shape[1]
@@ -107,18 +108,20 @@
         table = jnp.where(lane == j, column, table)
     table = table.T[:STATS]
     line = lax.broadcasted_iota(jnp.int32, (STATS, rows), 0)
-    table = jnp.where(line == len(columns), mask_ref[...], table)
+    mask = jnp.concatenate([mask_ref[...].astype(F32)] * n_y, axis=1)
+    mine = lax.div(lax.broadcasted_iota(jnp.int32, (1, rows), 1), tok) == me_ref[0]
+    table = jnp.where(line == len(columns), jnp.where(mine, mask, 0.0), table)
     stats_ref[...] = jnp.broadcast_to(table[None], stats_ref.shape)
 
 
-def logits(student_rows, teacher_rows, heads, mask):
+def logits(me, student_rows, teacher_rows, heads, mask):
     n_y, tok, width = student_rows.shape
     rows, block = n_y * tok, heads[0].shape[1]
     far, near = pl.BlockSpec(memory_space=pltpu.HBM), pl.BlockSpec(memory_space=pltpu.VMEM)
     side = [pltpu.VMEM(student_rows.shape, BF), pltpu.VMEM((width, block), BF), pltpu.VMEM((width, block), BF)]
     return pl.pallas_call(
         logits_kernel,
-        in_specs=[far] * 6 + [near],
+        in_specs=[pl.BlockSpec(memory_space=pltpu.SMEM)] + [far] * 6 + [near],
         out_specs=[near] * 3,
         out_shape=[
             jax.ShapeDtypeStruct((rows, CORES * block), F32),
@@ -131,7 +134,7 @@
             flops=8 * rows * width * block, bytes_accessed=12 * 2**20, transcendentals=2**18
         ),
         name="logits",
-    )(*(pltpu.with_memory_space_constraint(x, pltpu.HBM) for x in (student_rows, teacher_rows, *heads)), mask)
+    )(me, pltpu.with_memory_space_constraint(student_rows, pltpu.HBM), teacher_rows, *(pltpu.with_memory_space_constraint(x, pltpu.HBM) for x in heads), mask)
 
 
 def gradient_kernel(stats_ref, s_ref, d_ref, w0_ref, w1_ref, out_ref, parts_ref, grad_ref):
@@ -223,10 +226,10 @@
     empty = buffers((n_y, tok, width), student_head.shape, teacher_head.shape)
     _, teacher_rows, *other = lax.fori_loop(0, once, teacher_turn, (position, *empty))
 
-    mine = jnp.arange(rows, dtype=jnp.int32) // tok == lax.axis_index("y")
-    mask = jnp.where(mine, jnp.tile(token_mask.astype(F32), n_y), 0.0)[None]
-
-    s, d, stats = logits(student_rows, teacher_rows, (student_head, other[0], teacher_head, other[1]), mask)
+    me = lax.axis_index("y")[None]
+    s, d, stats = logits(
+        me, student_rows, teacher_rows, (student_head, other[0], teacher_head, other[1]), token_mask[None]
+    )
     stats = exchange(stats, "y")
     partial, parts = gradient(stats, s, d, (student_head, other[0]), n_dp * CORES)
     summed = lax.psum_scatter(partial, "y", scatter_dimension=0, tiled=True)

time: 163 us -> 161 us (0.988)
  waiting for transfers between devices: 52 us -> 58.5 us
  local copies, waits for them, and re-layouts: 8.51 us -> 2.22 us
    dynamic_update_slice x9, local copies, waits for them, and re-layouts: 6.41 us -> 0.19 us  [put(): lax.dynamic_update_slice(out, block[None], (lax.rem(owner, n), row, 0))]
    ppermute x3, waiting for transfers between devices: 6.63 us -> 9.64 us  [ring_gather(): r = lax.ppermute(r, axis, right)]
  transfers between devices with their start and end apart: 14 -> 14, of which waited for: 8 -> 10; matrix products, arithmetic and copies ran while one was open for 8% -> 3% of each run, Pallas kernels for 0% -> 0%
where the time goes in v5:
time: 161 us
  waiting for transfers between devices  58.5 us (36%)
  starting transfers between devices  54.3 us (34%)
  between operations  17.3 us (11%)
  blocking collectives  14.9 us (9%)
  Pallas kernels  8.21 us (5%)
  other arithmetic  4.43 us (3%)
  local copies, waits for them, and re-layouts  2.22 us (1%)
    all_to_all x2, waiting for transfers between devices, exchange(): return lax.all_to_all(x, axis, split_axis=0, concat_axis=0, tiled=True)  24.3 us
    all_to_all x2, starting transfers between devices, exchange(): return lax.all_to_all(x, axis, split_axis=0, concat_axis=0, tiled=True)  21.2 us
    reduce_scatter x1, waiting for transfers between devices, body(): summed = lax.psum_scatter(partial, 'y', scatter_dimension=0, tiled=True)  19.4 us
    all_to_all x1, blocking collectives, exchange(): return lax.all_to_all(x, axis, split_axis=0, concat_axis=0, tiled=True)  14.9 us
    ppermute x3, starting transfers between devices, ring_gather(): l = lax.ppermute(l, axis, left)  13.7 us
    ppermute x3, waiting for transfers between devices, ring_gather(): r = lax.ppermute(r, axis, right)  9.64 us
    ppermute x3, starting transfers between devices, ring_gather(): r = lax.ppermute(r, axis, right)  8.14 us
    pallas_call x1, Pallas kernels, logits(): pl.pallas_call(logits_kernel, in_specs=[pl.BlockSpec(memory_space=pltpu.S...  5.38 us
  transfers between devices with their start and end apart: 14, of which 10 were waited for; matrix products, arithmetic and copies ran while one was open for 3% of the time, Pallas kernels for 0%

profile of v5, /device:TPU:6, one launch (start us, length us, event | category | flops | bytes accessed | tf_op | source)
XLA Modules:
  0.0 160.5 jit_solution(9481111974652028003)
XLA Ops:
  7.2 0.0 all-gather.3.cloned.1.call-start
  7.2 0.7 all-gather.3.cloned.1.call-update
  7.9 0.0 reduce-scatter.2.cloned.1.call-start
  8.0 0.7 fusion.8
  8.6 0.2 convert_reduce_fusion
  8.8 0.1 broadcast_in_dim.115
  8.9 1.0 pad_maximum_fusion
  9.9 0.0 copy-start
  9.9 80.0 %while.22 = (s32[]{:T(128)}, s32[32]{0:T(128)S(1)}, bf16[8,32,4096]{2,1,0:T(8,128)(2,1)S(1)}, bf16[4096,256]{1,0:T(8,128)(2,1)}, bf16[4096,256]{1,0:T(8,128)(2,1...) while((s32[]{:T(128)}, s32[32]{0:T(128)S(1)}, ...), condition=%wide.region_2.3_spmd.clone, body=%wide.region_1.2_spmd.clone.sunk | while | flops 34484352 | bytes 50998332 | solution.py:227
  9.9 0.3 convolution_convert_fusion.4
  10.2 1.0 reshape.50
  11.2 13.4 %all-to-all-start = ((bf16[32,2,4224]{2,1,0:T(2,128)(2,1)}), bf16[32,2,4224]{2,1,0:T(2,128)(2,1)S(1)}, u32[]{:S(2)}, u32[]{:S(2)}) async-start(bf16[32,2,4224]{2,1,0:T(2,128)(2,1)} %reshape.50), calls=%async_computation | async-start | bytes 1081344 | tf_op jit(solution)/shard_map/while/body/all_to_all | solution.py:23
  24.7 17.1 %all-to-all-done = bf16[32,2,4224]{2,1,0:T(2,128)(2,1)S(1)} async-done(((bf16[32,2,4224]{2,1,0:T(2,128)(2,1)}), bf16[32,2,4224]{2,1,0:T(2,128)(2,1)S(1)}, u32[]{:S(2)}, u32[]{:S(2)}) %all-to-all-start) | async-done | bytes 540704 | tf_op jit(solution)/shard_map/while/body/all_to_all | solution.py:23
  41.8 0.2 reshape.51
  42.0 0.1 fusion.16
  42.1 0.2 convolution_convert_fusion.5
  42.3 3.5 %collective-permute-start = (bf16[32,4096]{1,0:T(8,128)(2,1)S(1)}, bf16[32,4096]{1,0:T(8,128)(2,1)S(1)}, u32[]{:S(2)}, u32[]{:S(2)}) collective-permute-start(bf16[32,4096]{1,0:T(8,128)(2,1)S(1)} %convolution_convert_fusion.5), channel_id=1, source_target_pairs={{0,2},{2,4},{4,6},{6,8},{8,10},{10,12},{12,14},{14,0},{1,3},{3,5},... | collective-permute-start | bytes 786440 | tf_op jit(solution)/shard_map/while/body/ppermute | solution.py:39
  45.8 3.8 %collective-permute-start.1 = (bf16[32,4096]{1,0:T(8,128)(2,1)S(1)}, bf16[32,4096]{1,0:T(8,128)(2,1)S(1)}, u32[]{:S(2)}, u32[]{:S(2)}) collective-permute-start(bf16[32,4096]{1,0:T(8,128)(2,1)S(1)} %convolution_convert_fusion.5), channel_id=1, source_target_pairs={{0,14},{2,0},{4,2},{6,4},{8,6},{10,8},{12,10},{14,12},{1,15},{3,1}... | collective-permute-start | bytes 786440 | tf_op jit(solution)/shard_map/while/body/ppermute | solution.py:40
  49.7 1.9 %collective-permute-start.4 = (bf16[4096,256]{1,0:T(8,128)(2,1)}, bf16[4096,256]{1,0:T(8,128)(2,1)S(1)}, u32[]{:S(2)}, u32[]{:S(2)}) collective-permute-start(bf16[4096,256]{1,0:T(8,128)(2,1)} %get-tuple-element.378), channel_id=1, source_target_pairs={{0,1},{1,0},{2,3},{3,2},{4,5},{5,4},{6,7},{7,6},{8,9},{9,8},{10,11... | collective-permute-start | bytes 6291464 | tf_op jit(solution)/shard_map/while/body/ppermute | solution.py:220
  51.6 2.4 %collective-permute-start.5 = (bf16[4096,256]{1,0:T(8,128)(2,1)}, bf16[4096,256]{1,0:T(8,128)(2,1)S(1)}, u32[]{:S(2)}, u32[]{:S(2)}) collective-permute-start(bf16[4096,256]{1,0:T(8,128)(2,1)} %get-tuple-element.379), channel_id=1, source_target_pairs={{0,1},{1,0},{2,3},{3,2},{4,5},{5,4},{6,7},{7,6},{8,9},{9,8},{10,11... | collective-permute-start | bytes 6291464 | tf_op jit(solution)/shard_map/while/body/ppermute | solution.py:220
  54.0 0.1 slice_reduce_fusion.2
  54.1 4.8 %collective-permute-done = bf16[32,4096]{1,0:T(8,128)(2,1)S(1)} collective-permute-done((bf16[32,4096]{1,0:T(8,128)(2,1)S(1)}, bf16[32,4096]{1,0:T(8,128)(2,1)S(1)}, u32[]{:S(2)}, u32[]{:S(2)}) %collective-permute-start) | collective-permute-done | bytes 262176 | tf_op jit(solution)/shard_map/while/body/ppermute | solution.py:39
  59.0 2.1 %collective-permute-start.2 = (bf16[32,4096]{1,0:T(8,128)(2,1)S(1)}, bf16[32,4096]{1,0:T(8,128)(2,1)S(1)}, u32[]{:S(2)}, u32[]{:S(2)}) collective-permute-start(bf16[32,4096]{1,0:T(8,128)(2,1)S(1)} %collective-permute-done), channel_id=1, source_target_pairs={{0,2},{2,4},{4,6},{6,8},{8,10},{10,12},{12,14},{14,0},{1,3},{3,5},... | collective-permute-start | bytes 786440 | tf_op jit(solution)/shard_map/while/body/ppermute | solution.py:39
  61.1 0.0 collective-permute-done.1
  61.1 4.9 %collective-permute-start.3 = (bf16[32,4096]{1,0:T(8,128)(2,1)S(1)}, bf16[32,4096]{1,0:T(8,128)(2,1)S(1)}, u32[]{:S(2)}, u32[]{:S(2)}) collective-permute-start(bf16[32,4096]{1,0:T(8,128)(2,1)S(1)} %collective-permute-done.1), channel_id=1, source_target_pairs={{0,14},{2,0},{4,2},{6,4},{8,6},{10,8},{12,10},{14,12},{1,15},{3,1}... | collective-permute-start | bytes 786440 | tf_op jit(solution)/shard_map/while/body/ppermute | solution.py:40
  66.1 2.4 %collective-permute-done.2 = bf16[32,4096]{1,0:T(8,128)(2,1)S(1)} collective-permute-done((bf16[32,4096]{1,0:T(8,128)(2,1)S(1)}, bf16[32,4096]{1,0:T(8,128)(2,1)S(1)}, u32[]{:S(2)}, u32[]{:S(2)}) %collective-permute-start.2) | collective-permute-done | bytes 262176 | tf_op jit(solution)/shard_map/while/body/ppermute | solution.py:39
  68.6 1.4 collective-permute-done.3
  69.9 0.0 collective-permute-done.4
  69.9 0.0 copy-start.2
  69.9 0.0 collective-permute-done.5
  69.9 0.0 copy-start.4
  69.9 2.5 %collective-permute-start.6 = (bf16[32,4096]{1,0:T(8,128)(2,1)S(1)}, bf16[32,4096]{1,0:T(8,128)(2,1)S(1)}, u32[]{:S(2)}, u32[]{:S(2)}) collective-permute-start(bf16[32,4096]{1,0:T(8,128)(2,1)S(1)} %collective-permute-done.2), channel_id=1, source_target_pairs={{0,2},{2,4},{4,6},{6,8},{8,10},{10,12},{12,14},{14,0},{1,3},{3,5},... | collective-permute-start | bytes 786440 | tf_op jit(solution)/shard_map/while/body/ppermute | solution.py:39
  72.5 5.0 %collective-permute-start.7 = (bf16[32,4096]{1,0:T(8,128)(2,1)S(1)}, bf16[32,4096]{1,0:T(8,128)(2,1)S(1)}, u32[]{:S(2)}, u32[]{:S(2)}) collective-permute-start(bf16[32,4096]{1,0:T(8,128)(2,1)S(1)} %collective-permute-done.3), channel_id=1, source_target_pairs={{0,14},{2,0},{4,2},{6,4},{8,6},{10,8},{12,10},{14,12},{1,15},{3,1}... | collective-permute-start | bytes 786440 | tf_op jit(solution)/shard_map/while/body/ppermute | solution.py:40
  77.5 2.4 %collective-permute-done.6 = bf16[32,4096]{1,0:T(8,128)(2,1)S(1)} collective-permute-done((bf16[32,4096]{1,0:T(8,128)(2,1)S(1)}, bf16[32,4096]{1,0:T(8,128)(2,1)S(1)}, u32[]{:S(2)}, u32[]{:S(2)}) %collective-permute-start.6) | collective-permute-done | bytes 262176 | tf_op jit(solution)/shard_map/while/body/ppermute | solution.py:39
  79.9 1.9 %collective-permute-start.8 = (bf16[16,4096]{1,0:T(8,128)(2,1)S(1)}, bf16[16,4096]{1,0:T(8,128)(2,1)S(1)}, u32[]{:S(2)}, u32[]{:S(2)}) collective-permute-start(bf16[16,4096]{1,0:T(8,128)(2,1)S(1)} %slice.88), channel_id=1, source_target_pairs={{0,2},{2,4},{4,6},{6,8},{8,10},{10,12},{12,14},{14,0},{1,3},{3,5},... | collective-permute-start | bytes 393224 | tf_op jit(solution)/shard_map/while/body/ppermute | solution.py:45
  81.8 0.2 collective-permute-done.7
  82.1 4.9 %collective-permute-start.9 = (bf16[16,4096]{1,0:T(8,128)(2,1)S(1)}, bf16[16,4096]{1,0:T(8,128)(2,1)S(1)}, u32[]{:S(2)}, u32[]{:S(2)}) collective-permute-start(bf16[16,4096]{1,0:T(8,128)(2,1)S(1)} %slice.89), channel_id=1, source_target_pairs={{0,14},{2,0},{4,2},{6,4},{8,6},{10,8},{12,10},{14,12},{1,15},{3,1}... | collective-permute-start | bytes 393224 | tf_op jit(solution)/shard_map/while/body/ppermute | solution.py:46
  87.1 0.9 collective-permute-done.8
  88.0 1.8 %collective-permute-done.9 = bf16[16,4096]{1,0:T(8,128)(2,1)S(1)} collective-permute-done((bf16[16,4096]{1,0:T(8,128)(2,1)S(1)}, bf16[16,4096]{1,0:T(8,128)(2,1)S(1)}, u32[]{:S(2)}, u32[]{:S(2)}) %collective-permute-start.9) | collective-permute-done | bytes 131104 | tf_op jit(solution)/shard_map/while/body/ppermute | solution.py:46
  89.9 0.0 copy-done.2
  89.9 0.0 copy-done.4
  89.9 0.0 all-gather.3.cloned.1.call-done
  89.9 0.0 copy-done
  89.9 0.0 copy-start.1
  89.9 0.0 copy-start.3
  89.9 5.4 %logits.1 = (f32[256,512]{1,0:T(8,128)S(1)}, f32[256,512]{1,0:T(8,128)S(1)}, f32[8,8,256]{2,1,0:T(8,128)S(1)}) custom-call(s32[1]{0:T(128)} %bitcast.me_ref, bf16[8,32,4096]{2,1,0:T(8,128)(2,1)} %bitcast.48, bf16[8,32,4096]{2,1,0:T(8,128)(2,1)S(1)} %get-tuple-element.256.xt, bf16[4096,256]{1,0:T(8,128)(2,1)} %get-tuple-element.452, ...), custom_call_target="tpu_custom_call" | custom-call | flops 2147483648 | bytes 12582912 | tf_op jit(solution)/shard_map/logits/pallas_call | solution.py:122
  95.3 14.9 %all_to_all.24.stats_ref = f32[8,8,256]{2,1,0:T(8,128)S(1)} all-to-all(f32[8,8,256]{2,1,0:T(8,128)S(1)} %get-tuple-element.259), channel_id=1, replica_groups=mesh['dp'=32,'y'=8,'core'=2] {'y'}, dimensions={0} | all-to-all | bytes 131072 | tf_op jit(solution)/shard_map/all_to_all | solution.py:23
  110.2 0.0 copy-done.1
  110.2 0.0 copy-done.3
  110.2 2.8 %gradient.1 = (bf16[256,4096]{1,0:T(8,128)(2,1)}, f32[64,128]{1,0:T(8,128)}) custom-call(f32[8,8,256]{2,1,0:T(8,128)S(1)} %all_to_all.24.stats_ref, f32[256,512]{1,0:T(8,128)S(1)} %get-tuple-element.260.s_ref, f32[256,512]{1,0:T(8,128)S(1)} %get-tuple-element.261.d_ref, bf16[4096,256]{1,0:T(8,128)(2,1)S(1)} %copy-done.1, bf16[4096,256]{1,0:T(8,128)(2,1)S(1)} %copy-done.3), custom_call_target="tpu_custom_call" | custom-call | flops 1073741824 | bytes 7340032 | tf_op jit(solution)/shard_map/gradient/pallas_call | solution.py:173
  113.0 0.0 reduce-scatter.2.cloned.1.call-update
  113.0 7.8 %all-to-all-start.2 = ((f32[64,1,128]{2,1,0:T(1,128)}), f32[64,1,128]{2,1,0:T(1,128)S(1)}, u32[]{:S(2)}, u32[]{:S(2)}) async-start(f32[64,1,128]{2,1,0:T(1,128)} %bitcast.4), calls=%async_computation.2 | async-start | bytes 65536 | tf_op jit(solution)/shard_map/all_to_all | solution.py:23
  121.5 7.2 %all-to-all-done.2 = f32[64,1,128]{2,1,0:T(1,128)S(1)} async-done(((f32[64,1,128]{2,1,0:T(1,128)}), f32[64,1,128]{2,1,0:T(1,128)S(1)}, u32[]{:S(2)}, u32[]{:S(2)}) %all-to-all-start.2) | async-done | bytes 32800 | tf_op jit(solution)/shard_map/all_to_all | solution.py:23
  128.7 0.1 reduce_sum.19
  128.7 0.6 fusion.9
  130.7 0.7 multiply_divide_fusion
  131.3 19.4 %reduce-scatter.2.cloned.1.call-done = bf16[32,4096]{1,0:T(8,128)(2,1)} async-done(((bf16[256,4096]{1,0:T(8,128)(2,1)}), bf16[32,4096]{1,0:T(8,128)(2,1)}) %reduce-scatter.2.cloned.1.call-update) | async-done | bytes 262160 | tf_op jit(solution)/shard_map/reduce_scatter | solution.py:235
  150.8 1.8 %multiply_convert_fusion = bf16[32,4096]{1,0:T(8,128)(2,1)} fusion(bf16[32,4096]{1,0:T(8,128)(2,1)} %reduce-scatter.2.cloned.1.call-done, f32[32]{0:T(128)S(1)} %multiply_divide_fusion), kind=kLoop, calls=%fused_computation.20 | loop fusion | flops 393216 | bytes 524416 | tf_op jit(solution)/shard_map/convert_element_type | solution.py:241
  (13 shorter events, 0.2 us)
Async XLA Ops:
  7.2 82.7 %all-gather.3.cloned.1.call-start = ((), (), s32[]{:S(2)}) async-start(), calls=%async_computation.5 | async-start | bytes 2359296 | tf_op jit(solution)/shard_map/all_gather | solution.py:224
  7.9 142.9 %reduce-scatter.2.cloned.1.call-start = ((), (), s32[]{:S(2)}) async-start(), calls=%async_computation.4 | async-start | bytes 2359296 | tf_op jit(solution)/shard_map/reduce_scatter | solution.py:235
  9.9 80.0 %copy-start = (s32[32]{0:T(128)S(1)}, s32[32]{0:T(128)}, u32[]{:S(2)}) copy-start(s32[32]{0:T(128)} %param.12) | copy-start | bytes 388
  11.2 30.6 %all-to-all-start = ((bf16[32,2,4224]{2,1,0:T(2,128)(2,1)}), bf16[32,2,4224]{2,1,0:T(2,128)(2,1)S(1)}, u32[]{:S(2)}, u32[]{:S(2)}) async-start(bf16[32,2,4224]{2,1,0:T(2,128)(2,1)} %reshape.50), calls=%async_computation | async-start | bytes 1081344 | tf_op jit(solution)/shard_map/while/body/all_to_all | solution.py:23
  42.3 16.6 %collective-permute-start = (bf16[32,4096]{1,0:T(8,128)(2,1)S(1)}, bf16[32,4096]{1,0:T(8,128)(2,1)S(1)}, u32[]{:S(2)}, u32[]{:S(2)}) collective-permute-start(bf16[32,4096]{1,0:T(8,128)(2,1)S(1)} %convolution_convert_fusion.5), channel_id=1, source_target_pairs={{0,2},{2,4},{4,6},{6,8},{8,10},{10,12},{12,14},{14,0},{1,3},{3,5},... | collective-permute-start | bytes 786440 | tf_op jit(solution)/shard_map/while/body/ppermute | solution.py:39
  45.8 15.3 %collective-permute-start.1 = (bf16[32,4096]{1,0:T(8,128)(2,1)S(1)}, bf16[32,4096]{1,0:T(8,128)(2,1)S(1)}, u32[]{:S(2)}, u32[]{:S(2)}) collective-permute-start(bf16[32,4096]{1,0:T(8,128)(2,1)S(1)} %convolution_convert_fusion.5), channel_id=1, source_target_pairs={{0,14},{2,0},{4,2},{6,4},{8,6},{10,8},{12,10},{14,12},{1,15},{3,1}... | collective-permute-start | bytes 786440 | tf_op jit(solution)/shard_map/while/body/ppermute | solution.py:40
  49.7 20.3 %collective-permute-start.4 = (bf16[4096,256]{1,0:T(8,128)(2,1)}, bf16[4096,256]{1,0:T(8,128)(2,1)S(1)}, u32[]{:S(2)}, u32[]{:S(2)}) collective-permute-start(bf16[4096,256]{1,0:T(8,128)(2,1)} %get-tuple-element.378), channel_id=1, source_target_pairs={{0,1},{1,0},{2,3},{3,2},{4,5},{5,4},{6,7},{7,6},{8,9},{9,8},{10,11... | collective-permute-start | bytes 6291464 | tf_op jit(solution)/shard_map/while/body/ppermute | solution.py:220
  51.6 18.3 %collective-permute-start.5 = (bf16[4096,256]{1,0:T(8,128)(2,1)}, bf16[4096,256]{1,0:T(8,128)(2,1)S(1)}, u32[]{:S(2)}, u32[]{:S(2)}) collective-permute-start(bf16[4096,256]{1,0:T(8,128)(2,1)} %get-tuple-element.379), channel_id=1, source_target_pairs={{0,1},{1,0},{2,3},{3,2},{4,5},{5,4},{6,7},{7,6},{8,9},{9,8},{10,11... | collective-permute-start | bytes 6291464 | tf_op jit(solution)/shard_map/while/body/ppermute | solution.py:220
  59.0 9.6 %collective-permute-start.2 = (bf16[32,4096]{1,0:T(8,128)(2,1)S(1)}, bf16[32,4096]{1,0:T(8,128)(2,1)S(1)}, u32[]{:S(2)}, u32[]{:S(2)}) collective-permute-start(bf16[32,4096]{1,0:T(8,128)(2,1)S(1)} %collective-permute-done), channel_id=1, source_target_pairs={{0,2},{2,4},{4,6},{6,8},{8,10},{10,12},{12,14},{14,0},{1,3},{3,5},... | collective-permute-start | bytes 786440 | tf_op jit(solution)/shard_map/while/body/ppermute | solution.py:39
  61.1 8.8 %collective-permute-start.3 = (bf16[32,4096]{1,0:T(8,128)(2,1)S(1)}, bf16[32,4096]{1,0:T(8,128)(2,1)S(1)}, u32[]{:S(2)}, u32[]{:S(2)}) collective-permute-start(bf16[32,4096]{1,0:T(8,128)(2,1)S(1)} %collective-permute-done.1), channel_id=1, source_target_pairs={{0,14},{2,0},{4,2},{6,4},{8,6},{10,8},{12,10},{14,12},{1,15},{3,1}... | collective-permute-start | bytes 786440 | tf_op jit(solution)/shard_map/while/body/ppermute | solution.py:40
  69.9 19.9 %copy-start.2 = (bf16[4096,256]{1,0:T(8,128)(2,1)}, bf16[4096,256]{1,0:T(8,128)(2,1)S(1)}, u32[]{:S(2)}) copy-start(bf16[4096,256]{1,0:T(8,128)(2,1)S(1)} %collective-permute-done.4) | copy-start | bytes 6291460 | tf_op jit(solution)/shard_map/while
  69.9 19.9 %copy-start.4 = (bf16[4096,256]{1,0:T(8,128)(2,1)}, bf16[4096,256]{1,0:T(8,128)(2,1)S(1)}, u32[]{:S(2)}) copy-start(bf16[4096,256]{1,0:T(8,128)(2,1)S(1)} %collective-permute-done.5) | copy-start | bytes 6291460 | tf_op jit(solution)/shard_map/while
  69.9 10.0 %collective-permute-start.6 = (bf16[32,4096]{1,0:T(8,128)(2,1)S(1)}, bf16[32,4096]{1,0:T(8,128)(2,1)S(1)}, u32[]{:S(2)}, u32[]{:S(2)}) collective-permute-start(bf16[32,4096]{1,0:T(8,128)(2,1)S(1)} %collective-permute-done.2), channel_id=1, source_target_pairs={{0,2},{2,4},{4,6},{6,8},{8,10},{10,12},{12,14},{14,0},{1,3},{3,5},... | collective-permute-start | bytes 786440 | tf_op jit(solution)/shard_map/while/body/ppermute | solution.py:39
  72.5 9.6 %collective-permute-start.7 = (bf16[32,4096]{1,0:T(8,128)(2,1)S(1)}, bf16[32,4096]{1,0:T(8,128)(2,1)S(1)}, u32[]{:S(2)}, u32[]{:S(2)}) collective-permute-start(bf16[32,4096]{1,0:T(8,128)(2,1)S(1)} %collective-permute-done.3), channel_id=1, source_target_pairs={{0,14},{2,0},{4,2},{6,4},{8,6},{10,8},{12,10},{14,12},{1,15},{3,1}... | collective-permute-start | bytes 786440 | tf_op jit(solution)/shard_map/while/body/ppermute | solution.py:40
  79.9 8.1 %collective-permute-start.8 = (bf16[16,4096]{1,0:T(8,128)(2,1)S(1)}, bf16[16,4096]{1,0:T(8,128)(2,1)S(1)}, u32[]{:S(2)}, u32[]{:S(2)}) collective-permute-start(bf16[16,4096]{1,0:T(8,128)(2,1)S(1)} %slice.88), channel_id=1, source_target_pairs={{0,2},{2,4},{4,6},{6,8},{8,10},{10,12},{12,14},{14,0},{1,3},{3,5},... | collective-permute-start | bytes 393224 | tf_op jit(solution)/shard_map/while/body/ppermute | solution.py:45
  82.1 7.7 %collective-permute-start.9 = (bf16[16,4096]{1,0:T(8,128)(2,1)S(1)}, bf16[16,4096]{1,0:T(8,128)(2,1)S(1)}, u32[]{:S(2)}, u32[]{:S(2)}) collective-permute-start(bf16[16,4096]{1,0:T(8,128)(2,1)S(1)} %slice.89), channel_id=1, source_target_pairs={{0,14},{2,0},{4,2},{6,4},{8,6},{10,8},{12,10},{14,12},{1,15},{3,1}... | collective-permute-start | bytes 393224 | tf_op jit(solution)/shard_map/while/body/ppermute | solution.py:46
  89.9 20.3 %copy-start.1 = (bf16[4096,256]{1,0:T(8,128)(2,1)S(1)}, bf16[4096,256]{1,0:T(8,128)(2,1)}, u32[]{:S(2)}) copy-start(bf16[4096,256]{1,0:T(8,128)(2,1)} %get-tuple-element.452) | copy-start | bytes 6291460
  89.9 20.3 %copy-start.3 = (bf16[4096,256]{1,0:T(8,128)(2,1)S(1)}, bf16[4096,256]{1,0:T(8,128)(2,1)}, u32[]{:S(2)}) copy-start(bf16[4096,256]{1,0:T(8,128)(2,1)} %get-tuple-element.257.ws1.w1_ref) | copy-start | bytes 6291460
  113.0 15.6 %all-to-all-start.2 = ((f32[64,1,128]{2,1,0:T(1,128)}), f32[64,1,128]{2,1,0:T(1,128)S(1)}, u32[]{:S(2)}, u32[]{:S(2)}) async-start(f32[64,1,128]{2,1,0:T(1,128)} %bitcast.4), calls=%async_computation.2 | async-start | bytes 65536 | tf_op jit(solution)/shard_map/all_to_all | solution.py:23
Sparse Core Ops, SparseCore 0:
  10.1 51.2 all-gather.2
  113.2 37.5 reduce-scatter.1

commit v6 on v5

--- a/solution.py
+++ b/solution.py
@@ -28,10 +28,10 @@
     me = lax.axis_index(axis)
     right = [(i, (i + 1) % n) for i in range(n)]
     left = [(i, (i - 1) % n) for i in range(n)]
-    half = x.shape[0] // 2
-
-    def put(out, block, owner, row=0):
-        return lax.dynamic_update_slice(out, block[None], (lax.rem(owner, n), row, 0))
+    share = x.shape[1] * 5 // 8 // 128 * 128
+
+    def put(out, block, owner, column=0):
+        return lax.dynamic_update_slice(out, block[None], (lax.rem(owner, n), 0, column))
 
     out = put(out, x, me)
     r = l = x
@@ -42,10 +42,10 @@
         out = put(out, l, me + k)
         if k == 2:
             r, l, beside = lax.optimization_barrier((r, l, beside))
-    r = lax.ppermute(r[:half], axis, right)
-    l = lax.ppermute(l[half:], axis, left)
+    r = lax.ppermute(r[:, :share], axis, right)
+    l = lax.ppermute(l[:, share:], axis, left)
     out = put(out, r, me + n // 2)
-    return put(out, l, me + n // 2, half), beside
+    return put(out, l, me + n // 2, share), beside
 
 
 def buffers(near, *far):
@@ -60,6 +60,7 @@
 
 def logits_kernel(me_ref, xs, xt, ws0, ws1, wt0, wt1, mask_ref, s_ref, d_ref, stats_ref, *scratch):
     *held, sems = scratch
+    held.insert(3, xt)
     n_y, tok, width = xs.shape
     rows, block = n_y * tok, ws0.shape[1]
     depth = width // STEPS
@@ -67,6 +68,8 @@
     def copies(side, k):
         part = pl.ds(k * depth, depth)
         for j, ref in enumerate(((xs, ws0, ws1), (xt, wt0, wt1))[side]):
+            if ref is xt:
+                continue
             at = (slice(None), slice(None), part) if j == 0 else (part, slice(None))
             yield pltpu.make_async_copy(ref.at[at], held[3 * side + j].at[at], sems.at[3 * side + j, k])
 
@@ -121,14 +124,14 @@
     side = [pltpu.VMEM(student_rows.shape, BF), pltpu.VMEM((width, block), BF), pltpu.VMEM((width, block), BF)]
     return pl.pallas_call(
         logits_kernel,
-        in_specs=[pl.BlockSpec(memory_space=pltpu.SMEM)] + [far] * 6 + [near],
+        in_specs=[pl.BlockSpec(memory_space=pltpu.SMEM), far, near] + [far] * 4 + [near],
         out_specs=[near] * 3,
         out_shape=[
             jax.ShapeDtypeStruct((rows, CORES * block), F32),
             jax.ShapeDtypeStruct((rows, CORES * block), F32),
             jax.ShapeDtypeStruct((n_y, STATS, rows), F32),
         ],
-        scratch_shapes=side + side + [pltpu.SemaphoreType.DMA((6, STEPS))],
+        scratch_shapes=side + side[1:] + [pltpu.SemaphoreType.DMA((6, STEPS))],
         compiler_params=pltpu.CompilerParams(vmem_limit_bytes=LOGITS_VMEM),
         cost_estimate=pl.CostEstimate(
             flops=8 * rows * width * block, bytes_accessed=12 * 2**20, transcendentals=2**18

time: 161 us -> 161 us (level)
  no operation moved by 1% of the time
where the time goes in v6:
time: 161 us; the launch traced here: 160 us
  waiting for transfers between devices  58.4 us (36%)
  starting transfers between devices  54.3 us (34%)
  between operations  17.2 us (11%)
  blocking collectives  14.9 us (9%)
  Pallas kernels  8.2 us (5%)
  other arithmetic  4.43 us (3%)
  local copies, waits for them, and re-layouts  2.22 us (1%)
    all_to_all x2, waiting for transfers between devices, exchange(): return lax.all_to_all(x, axis, split_axis=0, concat_axis=0, tiled=True)  24.3 us
    all_to_all x2, starting transfers between devices, exchange(): return lax.all_to_all(x, axis, split_axis=0, concat_axis=0, tiled=True)  21.2 us
    reduce_scatter x1, waiting for transfers between devices, body(): summed = lax.psum_scatter(partial, 'y', scatter_dimension=0, tiled=True)  19.8 us
    all_to_all x1, blocking collectives, exchange(): return lax.all_to_all(x, axis, split_axis=0, concat_axis=0, tiled=True)  14.9 us
    ppermute x3, starting transfers between devices, ring_gather(): l = lax.ppermute(l, axis, left)  13.7 us
    ppermute x3, waiting for transfers between devices, ring_gather(): r = lax.ppermute(r, axis, right)  9.64 us
    ppermute x3, starting transfers between devices, ring_gather(): r = lax.ppermute(r, axis, right)  8.14 us
    pallas_call x1, Pallas kernels, logits(): pl.pallas_call(logits_kernel, in_specs=[pl.BlockSpec(memory_space=pltpu.S...  5.37 us
  transfers between devices with their start and end apart: 14, of which 10 were waited for; matrix products, arithmetic and copies ran while one was open for 3% of the time, Pallas kernels for 0%

profile of v6, /device:TPU:6, one launch (start us, length us, event | category | flops | bytes accessed | tf_op | source)
XLA Modules:
  0.0 160.4 jit_solution(4357422149912385065)
XLA Ops:
  7.2 0.0 all-gather.3.cloned.1.call-start
  7.2 0.7 all-gather.3.cloned.1.call-update
  7.9 0.0 reduce-scatter.2.cloned.1.call-start
  8.0 0.7 fusion.8
  8.6 0.2 convert_reduce_fusion
  8.8 0.1 broadcast_in_dim.115
  8.9 1.0 pad_maximum_fusion
  9.9 0.0 copy-start
  9.9 79.6 %while.22 = (s32[]{:T(128)}, s32[32]{0:T(128)S(1)}, bf16[8,32,4096]{2,1,0:T(8,128)(2,1)S(1)}, bf16[4096,256]{1,0:T(8,128)(2,1)}, bf16[4096,256]{1,0:T(8,128)(2,1...) while((s32[]{:T(128)}, s32[32]{0:T(128)S(1)}, ...), condition=%wide.region_2.3_spmd.clone, body=%wide.region_1.2_spmd.clone.sunk | while | flops 34484352 | bytes 50998332 | solution.py:230
  9.9 0.3 convolution_convert_fusion.4
  10.2 1.0 reshape.50
  11.2 13.4 %all-to-all-start = ((bf16[32,2,4224]{2,1,0:T(2,128)(2,1)}), bf16[32,2,4224]{2,1,0:T(2,128)(2,1)S(1)}, u32[]{:S(2)}, u32[]{:S(2)}) async-start(bf16[32,2,4224]{2,1,0:T(2,128)(2,1)} %reshape.50), calls=%async_computation | async-start | bytes 1081344 | tf_op jit(solution)/shard_map/while/body/all_to_all | solution.py:23
  24.7 17.1 %all-to-all-done = bf16[32,2,4224]{2,1,0:T(2,128)(2,1)S(1)} async-done(((bf16[32,2,4224]{2,1,0:T(2,128)(2,1)}), bf16[32,2,4224]{2,1,0:T(2,128)(2,1)S(1)}, u32[]{:S(2)}, u32[]{:S(2)}) %all-to-all-start) | async-done | bytes 540704 | tf_op jit(solution)/shard_map/while/body/all_to_all | solution.py:23
  41.8 0.2 reshape.51
  42.0 0.1 fusion.16
  42.1 0.2 convolution_convert_fusion.5
  42.3 3.5 %collective-permute-start = (bf16[32,4096]{1,0:T(8,128)(2,1)S(1)}, bf16[32,4096]{1,0:T(8,128)(2,1)S(1)}, u32[]{:S(2)}, u32[]{:S(2)}) collective-permute-start(bf16[32,4096]{1,0:T(8,128)(2,1)S(1)} %convolution_convert_fusion.5), channel_id=1, source_target_pairs={{0,2},{2,4},{4,6},{6,8},{8,10},{10,12},{12,14},{14,0},{1,3},{3,5},... | collective-permute-start | bytes 786440 | tf_op jit(solution)/shard_map/while/body/ppermute | solution.py:39
  45.8 3.8 %collective-permute-start.1 = (bf16[32,4096]{1,0:T(8,128)(2,1)S(1)}, bf16[32,4096]{1,0:T(8,128)(2,1)S(1)}, u32[]{:S(2)}, u32[]{:S(2)}) collective-permute-start(bf16[32,4096]{1,0:T(8,128)(2,1)S(1)} %convolution_convert_fusion.5), channel_id=1, source_target_pairs={{0,14},{2,0},{4,2},{6,4},{8,6},{10,8},{12,10},{14,12},{1,15},{3,1}... | collective-permute-start | bytes 786440 | tf_op jit(solution)/shard_map/while/body/ppermute | solution.py:40
  49.7 1.9 %collective-permute-start.4 = (bf16[4096,256]{1,0:T(8,128)(2,1)}, bf16[4096,256]{1,0:T(8,128)(2,1)S(1)}, u32[]{:S(2)}, u32[]{:S(2)}) collective-permute-start(bf16[4096,256]{1,0:T(8,128)(2,1)} %get-tuple-element.378), channel_id=1, source_target_pairs={{0,1},{1,0},{2,3},{3,2},{4,5},{5,4},{6,7},{7,6},{8,9},{9,8},{10,11... | collective-permute-start | bytes 6291464 | tf_op jit(solution)/shard_map/while/body/ppermute | solution.py:223
  51.6 2.4 %collective-permute-start.5 = (bf16[4096,256]{1,0:T(8,128)(2,1)}, bf16[4096,256]{1,0:T(8,128)(2,1)S(1)}, u32[]{:S(2)}, u32[]{:S(2)}) collective-permute-start(bf16[4096,256]{1,0:T(8,128)(2,1)} %get-tuple-element.379), channel_id=1, source_target_pairs={{0,1},{1,0},{2,3},{3,2},{4,5},{5,4},{6,7},{7,6},{8,9},{9,8},{10,11... | collective-permute-start | bytes 6291464 | tf_op jit(solution)/shard_map/while/body/ppermute | solution.py:223
  54.0 0.1 slice_reduce_fusion.2
  54.1 4.8 %collective-permute-done = bf16[32,4096]{1,0:T(8,128)(2,1)S(1)} collective-permute-done((bf16[32,4096]{1,0:T(8,128)(2,1)S(1)}, bf16[32,4096]{1,0:T(8,128)(2,1)S(1)}, u32[]{:S(2)}, u32[]{:S(2)}) %collective-permute-start) | collective-permute-done | bytes 262176 | tf_op jit(solution)/shard_map/while/body/ppermute | solution.py:39
  59.0 2.1 %collective-permute-start.2 = (bf16[32,4096]{1,0:T(8,128)(2,1)S(1)}, bf16[32,4096]{1,0:T(8,128)(2,1)S(1)}, u32[]{:S(2)}, u32[]{:S(2)}) collective-permute-start(bf16[32,4096]{1,0:T(8,128)(2,1)S(1)} %collective-permute-done), channel_id=1, source_target_pairs={{0,2},{2,4},{4,6},{6,8},{8,10},{10,12},{12,14},{14,0},{1,3},{3,5},... | collective-permute-start | bytes 786440 | tf_op jit(solution)/shard_map/while/body/ppermute | solution.py:39
  61.1 0.0 collective-permute-done.1
  61.1 4.9 %collective-permute-start.3 = (bf16[32,4096]{1,0:T(8,128)(2,1)S(1)}, bf16[32,4096]{1,0:T(8,128)(2,1)S(1)}, u32[]{:S(2)}, u32[]{:S(2)}) collective-permute-start(bf16[32,4096]{1,0:T(8,128)(2,1)S(1)} %collective-permute-done.1), channel_id=1, source_target_pairs={{0,14},{2,0},{4,2},{6,4},{8,6},{10,8},{12,10},{14,12},{1,15},{3,1}... | collective-permute-start | bytes 786440 | tf_op jit(solution)/shard_map/while/body/ppermute | solution.py:40
  66.1 2.4 %collective-permute-done.2 = bf16[32,4096]{1,0:T(8,128)(2,1)S(1)} collective-permute-done((bf16[32,4096]{1,0:T(8,128)(2,1)S(1)}, bf16[32,4096]{1,0:T(8,128)(2,1)S(1)}, u32[]{:S(2)}, u32[]{:S(2)}) %collective-permute-start.2) | collective-permute-done | bytes 262176 | tf_op jit(solution)/shard_map/while/body/ppermute | solution.py:39
  68.6 1.4 collective-permute-done.3
  69.9 0.0 collective-permute-done.4
  69.9 0.0 copy-start.2
  69.9 0.0 collective-permute-done.5
  69.9 0.0 copy-start.4
  69.9 2.5 %collective-permute-start.6 = (bf16[32,4096]{1,0:T(8,128)(2,1)S(1)}, bf16[32,4096]{1,0:T(8,128)(2,1)S(1)}, u32[]{:S(2)}, u32[]{:S(2)}) collective-permute-start(bf16[32,4096]{1,0:T(8,128)(2,1)S(1)} %collective-permute-done.2), channel_id=1, source_target_pairs={{0,2},{2,4},{4,6},{6,8},{8,10},{10,12},{12,14},{14,0},{1,3},{3,5},... | collective-permute-start | bytes 786440 | tf_op jit(solution)/shard_map/while/body/ppermute | solution.py:39
  72.5 5.0 %collective-permute-start.7 = (bf16[32,4096]{1,0:T(8,128)(2,1)S(1)}, bf16[32,4096]{1,0:T(8,128)(2,1)S(1)}, u32[]{:S(2)}, u32[]{:S(2)}) collective-permute-start(bf16[32,4096]{1,0:T(8,128)(2,1)S(1)} %collective-permute-done.3), channel_id=1, source_target_pairs={{0,14},{2,0},{4,2},{6,4},{8,6},{10,8},{12,10},{14,12},{1,15},{3,1}... | collective-permute-start | bytes 786440 | tf_op jit(solution)/shard_map/while/body/ppermute | solution.py:40
  77.5 2.4 %collective-permute-done.6 = bf16[32,4096]{1,0:T(8,128)(2,1)S(1)} collective-permute-done((bf16[32,4096]{1,0:T(8,128)(2,1)S(1)}, bf16[32,4096]{1,0:T(8,128)(2,1)S(1)}, u32[]{:S(2)}, u32[]{:S(2)}) %collective-permute-start.6) | collective-permute-done | bytes 262176 | tf_op jit(solution)/shard_map/while/body/ppermute | solution.py:39
  79.9 1.9 %collective-permute-start.8 = (bf16[32,2560]{1,0:T(8,128)(2,1)S(1)}, bf16[32,2560]{1,0:T(8,128)(2,1)S(1)}, u32[]{:S(2)}, u32[]{:S(2)}) collective-permute-start(bf16[32,2560]{1,0:T(8,128)(2,1)S(1)} %slice.88), channel_id=1, source_target_pairs={{0,2},{2,4},{4,6},{6,8},{8,10},{10,12},{12,14},{14,0},{1,3},{3,5},... | collective-permute-start | bytes 491528 | tf_op jit(solution)/shard_map/while/body/ppermute | solution.py:45
  81.8 0.2 collective-permute-done.7
  82.1 4.9 %collective-permute-start.9 = (bf16[32,1536]{1,0:T(8,128)(2,1)S(1)}, bf16[32,1536]{1,0:T(8,128)(2,1)S(1)}, u32[]{:S(2)}, u32[]{:S(2)}) collective-permute-start(bf16[32,1536]{1,0:T(8,128)(2,1)S(1)} %slice.89), channel_id=1, source_target_pairs={{0,14},{2,0},{4,2},{6,4},{8,6},{10,8},{12,10},{14,12},{1,15},{3,1}... | collective-permute-start | bytes 294920 | tf_op jit(solution)/shard_map/while/body/ppermute | solution.py:46
  87.1 1.3 collective-permute-done.8
  88.3 1.1 collective-permute-done.9
  89.5 0.0 copy-done.2
  89.5 0.0 copy-done.4
  89.5 0.0 all-gather.3.cloned.1.call-done
  89.6 0.0 copy-done
  89.6 0.0 copy-start.1
  89.6 0.0 copy-start.3
  89.6 5.4 %logits.1 = (f32[256,512]{1,0:T(8,128)S(1)}, f32[256,512]{1,0:T(8,128)S(1)}, f32[8,8,256]{2,1,0:T(8,128)S(1)}) custom-call(s32[1]{0:T(128)} %bitcast.me_ref, bf16[8,32,4096]{2,1,0:T(8,128)(2,1)} %bitcast.48, bf16[8,32,4096]{2,1,0:T(8,128)(2,1)S(1)} %get-tuple-element.256.xt, bf16[4096,256]{1,0:T(8,128)(2,1)} %get-tuple-element.452, ...), custom_call_target="tpu_custom_call" | custom-call | flops 2147483648 | bytes 12582912 | tf_op jit(solution)/shard_map/logits/pallas_call | solution.py:125
  95.0 14.9 %all_to_all.24.stats_ref = f32[8,8,256]{2,1,0:T(8,128)S(1)} all-to-all(f32[8,8,256]{2,1,0:T(8,128)S(1)} %get-tuple-element.259), channel_id=1, replica_groups=mesh['dp'=32,'y'=8,'core'=2] {'y'}, dimensions={0} | all-to-all | bytes 131072 | tf_op jit(solution)/shard_map/all_to_all | solution.py:23
  109.8 0.0 copy-done.1
  109.8 0.0 copy-done.3
  109.8 2.8 %gradient.1 = (bf16[256,4096]{1,0:T(8,128)(2,1)}, f32[64,128]{1,0:T(8,128)}) custom-call(f32[8,8,256]{2,1,0:T(8,128)S(1)} %all_to_all.24.stats_ref, f32[256,512]{1,0:T(8,128)S(1)} %get-tuple-element.260.s_ref, f32[256,512]{1,0:T(8,128)S(1)} %get-tuple-element.261.d_ref, bf16[4096,256]{1,0:T(8,128)(2,1)S(1)} %copy-done.1, bf16[4096,256]{1,0:T(8,128)(2,1)S(1)} %copy-done.3), custom_call_target="tpu_custom_call" | custom-call | flops 1073741824 | bytes 7340032 | tf_op jit(solution)/shard_map/gradient/pallas_call | solution.py:176
  112.7 0.0 reduce-scatter.2.cloned.1.call-update
  112.7 7.8 %all-to-all-start.2 = ((f32[64,1,128]{2,1,0:T(1,128)}), f32[64,1,128]{2,1,0:T(1,128)S(1)}, u32[]{:S(2)}, u32[]{:S(2)}) async-start(f32[64,1,128]{2,1,0:T(1,128)} %bitcast.4), calls=%async_computation.2 | async-start | bytes 65536 | tf_op jit(solution)/shard_map/all_to_all | solution.py:23
  121.1 7.2 %all-to-all-done.2 = f32[64,1,128]{2,1,0:T(1,128)S(1)} async-done(((f32[64,1,128]{2,1,0:T(1,128)}), f32[64,1,128]{2,1,0:T(1,128)S(1)}, u32[]{:S(2)}, u32[]{:S(2)}) %all-to-all-start.2) | async-done | bytes 32800 | tf_op jit(solution)/shard_map/all_to_all | solution.py:23
  128.3 0.1 reduce_sum.19
  128.4 0.6 fusion.9
  130.3 0.7 multiply_divide_fusion
  131.0 19.8 %reduce-scatter.2.cloned.1.call-done = bf16[32,4096]{1,0:T(8,128)(2,1)} async-done(((bf16[256,4096]{1,0:T(8,128)(2,1)}), bf16[32,4096]{1,0:T(8,128)(2,1)}) %reduce-scatter.2.cloned.1.call-update) | async-done | bytes 262160 | tf_op jit(solution)/shard_map/reduce_scatter | solution.py:238
  150.7 1.8 %multiply_convert_fusion = bf16[32,4096]{1,0:T(8,128)(2,1)} fusion(bf16[32,4096]{1,0:T(8,128)(2,1)} %reduce-scatter.2.cloned.1.call-done, f32[32]{0:T(128)S(1)} %multiply_divide_fusion), kind=kLoop, calls=%fused_computation.20 | loop fusion | flops 393216 | bytes 524416 | tf_op jit(solution)/shard_map/convert_element_type | solution.py:244
  (13 shorter events, 0.2 us)
Async XLA Ops:
  7.2 82.4 %all-gather.3.cloned.1.call-start = ((), (), s32[]{:S(2)}) async-start(), calls=%async_computation.5 | async-start | bytes 2359296 | tf_op jit(solution)/shard_map/all_gather | solution.py:227
  7.9 142.8 %reduce-scatter.2.cloned.1.call-start = ((), (), s32[]{:S(2)}) async-start(), calls=%async_computation.4 | async-start | bytes 2359296 | tf_op jit(solution)/shard_map/reduce_scatter | solution.py:238
  9.9 79.7 %copy-start = (s32[32]{0:T(128)S(1)}, s32[32]{0:T(128)}, u32[]{:S(2)}) copy-start(s32[32]{0:T(128)} %param.12) | copy-start | bytes 388
  11.2 30.6 %all-to-all-start = ((bf16[32,2,4224]{2,1,0:T(2,128)(2,1)}), bf16[32,2,4224]{2,1,0:T(2,128)(2,1)S(1)}, u32[]{:S(2)}, u32[]{:S(2)}) async-start(bf16[32,2,4224]{2,1,0:T(2,128)(2,1)} %reshape.50), calls=%async_computation | async-start | bytes 1081344 | tf_op jit(solution)/shard_map/while/body/all_to_all | solution.py:23
  42.3 16.6 %collective-permute-start = (bf16[32,4096]{1,0:T(8,128)(2,1)S(1)}, bf16[32,4096]{1,0:T(8,128)(2,1)S(1)}, u32[]{:S(2)}, u32[]{:S(2)}) collective-permute-start(bf16[32,4096]{1,0:T(8,128)(2,1)S(1)} %convolution_convert_fusion.5), channel_id=1, source_target_pairs={{0,2},{2,4},{4,6},{6,8},{8,10},{10,12},{12,14},{14,0},{1,3},{3,5},... | collective-permute-start | bytes 786440 | tf_op jit(solution)/shard_map/while/body/ppermute | solution.py:39
  45.8 15.3 %collective-permute-start.1 = (bf16[32,4096]{1,0:T(8,128)(2,1)S(1)}, bf16[32,4096]{1,0:T(8,128)(2,1)S(1)}, u32[]{:S(2)}, u32[]{:S(2)}) collective-permute-start(bf16[32,4096]{1,0:T(8,128)(2,1)S(1)} %convolution_convert_fusion.5), channel_id=1, source_target_pairs={{0,14},{2,0},{4,2},{6,4},{8,6},{10,8},{12,10},{14,12},{1,15},{3,1}... | collective-permute-start | bytes 786440 | tf_op jit(solution)/shard_map/while/body/ppermute | solution.py:40
  49.7 20.3 %collective-permute-start.4 = (bf16[4096,256]{1,0:T(8,128)(2,1)}, bf16[4096,256]{1,0:T(8,128)(2,1)S(1)}, u32[]{:S(2)}, u32[]{:S(2)}) collective-permute-start(bf16[4096,256]{1,0:T(8,128)(2,1)} %get-tuple-element.378), channel_id=1, source_target_pairs={{0,1},{1,0},{2,3},{3,2},{4,5},{5,4},{6,7},{7,6},{8,9},{9,8},{10,11... | collective-permute-start | bytes 6291464 | tf_op jit(solution)/shard_map/while/body/ppermute | solution.py:223
  51.6 18.3 %collective-permute-start.5 = (bf16[4096,256]{1,0:T(8,128)(2,1)}, bf16[4096,256]{1,0:T(8,128)(2,1)S(1)}, u32[]{:S(2)}, u32[]{:S(2)}) collective-permute-start(bf16[4096,256]{1,0:T(8,128)(2,1)} %get-tuple-element.379), channel_id=1, source_target_pairs={{0,1},{1,0},{2,3},{3,2},{4,5},{5,4},{6,7},{7,6},{8,9},{9,8},{10,11... | collective-permute-start | bytes 6291464 | tf_op jit(solution)/shard_map/while/body/ppermute | solution.py:223
  59.0 9.6 %collective-permute-start.2 = (bf16[32,4096]{1,0:T(8,128)(2,1)S(1)}, bf16[32,4096]{1,0:T(8,128)(2,1)S(1)}, u32[]{:S(2)}, u32[]{:S(2)}) collective-permute-start(bf16[32,4096]{1,0:T(8,128)(2,1)S(1)} %collective-permute-done), channel_id=1, source_target_pairs={{0,2},{2,4},{4,6},{6,8},{8,10},{10,12},{12,14},{14,0},{1,3},{3,5},... | collective-permute-start | bytes 786440 | tf_op jit(solution)/shard_map/while/body/ppermute | solution.py:39
  61.1 8.8 %collective-permute-start.3 = (bf16[32,4096]{1,0:T(8,128)(2,1)S(1)}, bf16[32,4096]{1,0:T(8,128)(2,1)S(1)}, u32[]{:S(2)}, u32[]{:S(2)}) collective-permute-start(bf16[32,4096]{1,0:T(8,128)(2,1)S(1)} %collective-permute-done.1), channel_id=1, source_target_pairs={{0,14},{2,0},{4,2},{6,4},{8,6},{10,8},{12,10},{14,12},{1,15},{3,1}... | collective-permute-start | bytes 786440 | tf_op jit(solution)/shard_map/while/body/ppermute | solution.py:40
  69.9 19.6 %copy-start.2 = (bf16[4096,256]{1,0:T(8,128)(2,1)}, bf16[4096,256]{1,0:T(8,128)(2,1)S(1)}, u32[]{:S(2)}) copy-start(bf16[4096,256]{1,0:T(8,128)(2,1)S(1)} %collective-permute-done.4) | copy-start | bytes 6291460 | tf_op jit(solution)/shard_map/while
  69.9 19.6 %copy-start.4 = (bf16[4096,256]{1,0:T(8,128)(2,1)}, bf16[4096,256]{1,0:T(8,128)(2,1)S(1)}, u32[]{:S(2)}) copy-start(bf16[4096,256]{1,0:T(8,128)(2,1)S(1)} %collective-permute-done.5) | copy-start | bytes 6291460 | tf_op jit(solution)/shard_map/while
  69.9 10.0 %collective-permute-start.6 = (bf16[32,4096]{1,0:T(8,128)(2,1)S(1)}, bf16[32,4096]{1,0:T(8,128)(2,1)S(1)}, u32[]{:S(2)}, u32[]{:S(2)}) collective-permute-start(bf16[32,4096]{1,0:T(8,128)(2,1)S(1)} %collective-permute-done.2), channel_id=1, source_target_pairs={{0,2},{2,4},{4,6},{6,8},{8,10},{10,12},{12,14},{14,0},{1,3},{3,5},... | collective-permute-start | bytes 786440 | tf_op jit(solution)/shard_map/while/body/ppermute | solution.py:39
  72.5 9.6 %collective-permute-start.7 = (bf16[32,4096]{1,0:T(8,128)(2,1)S(1)}, bf16[32,4096]{1,0:T(8,128)(2,1)S(1)}, u32[]{:S(2)}, u32[]{:S(2)}) collective-permute-start(bf16[32,4096]{1,0:T(8,128)(2,1)S(1)} %collective-permute-done.3), channel_id=1, source_target_pairs={{0,14},{2,0},{4,2},{6,4},{8,6},{10,8},{12,10},{14,12},{1,15},{3,1}... | collective-permute-start | bytes 786440 | tf_op jit(solution)/shard_map/while/body/ppermute | solution.py:40
  79.9 8.4 %collective-permute-start.8 = (bf16[32,2560]{1,0:T(8,128)(2,1)S(1)}, bf16[32,2560]{1,0:T(8,128)(2,1)S(1)}, u32[]{:S(2)}, u32[]{:S(2)}) collective-permute-start(bf16[32,2560]{1,0:T(8,128)(2,1)S(1)} %slice.88), channel_id=1, source_target_pairs={{0,2},{2,4},{4,6},{6,8},{8,10},{10,12},{12,14},{14,0},{1,3},{3,5},... | collective-permute-start | bytes 491528 | tf_op jit(solution)/shard_map/while/body/ppermute | solution.py:45
  82.1 7.4 %collective-permute-start.9 = (bf16[32,1536]{1,0:T(8,128)(2,1)S(1)}, bf16[32,1536]{1,0:T(8,128)(2,1)S(1)}, u32[]{:S(2)}, u32[]{:S(2)}) collective-permute-start(bf16[32,1536]{1,0:T(8,128)(2,1)S(1)} %slice.89), channel_id=1, source_target_pairs={{0,14},{2,0},{4,2},{6,4},{8,6},{10,8},{12,10},{14,12},{1,15},{3,1}... | collective-permute-start | bytes 294920 | tf_op jit(solution)/shard_map/while/body/ppermute | solution.py:46
  89.6 20.3 %copy-start.1 = (bf16[4096,256]{1,0:T(8,128)(2,1)S(1)}, bf16[4096,256]{1,0:T(8,128)(2,1)}, u32[]{:S(2)}) copy-start(bf16[4096,256]{1,0:T(8,128)(2,1)} %get-tuple-element.452) | copy-start | bytes 6291460
  89.6 20.3 %copy-start.3 = (bf16[4096,256]{1,0:T(8,128)(2,1)S(1)}, bf16[4096,256]{1,0:T(8,128)(2,1)}, u32[]{:S(2)}) copy-start(bf16[4096,256]{1,0:T(8,128)(2,1)} %get-tuple-element.257.ws1.w1_ref) | copy-start | bytes 6291460
  112.7 15.6 %all-to-all-start.2 = ((f32[64,1,128]{2,1,0:T(1,128)}), f32[64,1,128]{2,1,0:T(1,128)S(1)}, u32[]{:S(2)}, u32[]{:S(2)}) async-start(f32[64,1,128]{2,1,0:T(1,128)} %bitcast.4), calls=%async_computation.2 | async-start | bytes 65536 | tf_op jit(solution)/shard_map/all_to_all | solution.py:23
Sparse Core Ops, SparseCore 0:
  10.1 51.2 all-gather.2
  112.8 37.8 reduce-scatter.1

commit v7 on v6

--- a/solution.py
+++ b/solution.py
@@ -40,7 +40,7 @@
         l = lax.ppermute(l, axis, left)
         out = put(out, r, me + n - k)
         out = put(out, l, me + k)
-        if k == 2:
+        if k == 1:
             r, l, beside = lax.optimization_barrier((r, l, beside))
     r = lax.ppermute(r[:, :share], axis, right)
     l = lax.ppermute(l[:, share:], axis, left)
@@ -58,9 +58,9 @@
     )()
 
 
-def logits_kernel(me_ref, xs, xt, ws0, ws1, wt0, wt1, mask_ref, s_ref, d_ref, stats_ref, *scratch):
-    *held, sems = scratch
-    held.insert(3, xt)
+def logits_kernel(me_ref, xs, xt, ws0, ws1, wt0, wt1, mask_ref, s_ref, d_ref, stats_ref, ws0_out, ws1_out, *scratch):
+    xs_in, wt0_in, wt1_in, sems = scratch
+    held = [xs_in, ws0_out, ws1_out, xt, wt0_in, wt1_in]
     n_y, tok, width = xs.shape
     rows, block = n_y * tok, ws0.shape[1]
     depth = width // STEPS
@@ -125,13 +125,15 @@
     return pl.pallas_call(
         logits_kernel,
         in_specs=[pl.BlockSpec(memory_space=pltpu.SMEM), far, near] + [far] * 4 + [near],
-        out_specs=[near] * 3,
+        out_specs=[near] * 5,
         out_shape=[
             jax.ShapeDtypeStruct((rows, CORES * block), F32),
             jax.ShapeDtypeStruct((rows, CORES * block), F32),
             jax.ShapeDtypeStruct((n_y, STATS, rows), F32),
+            pltpu.VMEM((width, block), BF),
+            pltpu.VMEM((width, block), BF),
         ],
-        scratch_shapes=side + side[1:] + [pltpu.SemaphoreType.DMA((6, STEPS))],
+        scratch_shapes=side + [pltpu.SemaphoreType.DMA((6, STEPS))],
         compiler_params=pltpu.CompilerParams(vmem_limit_bytes=LOGITS_VMEM),
         cost_estimate=pl.CostEstimate(
             flops=8 * rows * width * block, bytes_accessed=12 * 2**20, transcendentals=2**18
@@ -215,12 +217,12 @@
         position, out, *_ = carry
         spread = (jnp.arange(n_dp * cap, dtype=jnp.int32)[:, None] == position[None, :]).astype(BF)
         send = dot(spread, payload, 1, 0).astype(BF)
+        heads, send = lax.optimization_barrier(((student_head, teacher_head), send))
+        other = [lax.ppermute(head, "core", swap) for head in heads]
         got = exchange(send.reshape(n_dp, cap, width + 128), "dp").reshape(n_dp * cap, width + 128)
         slots = got[:, width].astype(jnp.int32) - 1
         place = (index[:, None] == slots[None, :]).astype(BF)
         placed = dot(place, got[:, :width], 1, 0).astype(BF)
-        heads, placed = lax.optimization_barrier(((student_head, teacher_head), placed))
-        other = [lax.ppermute(head, "core", swap) for head in heads]
         out, other = ring_gather(placed, out, "y", other)
         return slots[:tok], out, *other
 
@@ -230,11 +232,11 @@
     _, teacher_rows, *other = lax.fori_loop(0, once, teacher_turn, (position, *empty))
 
     me = lax.axis_index("y")[None]
-    s, d, stats = logits(
+    s, d, stats, *near_heads = logits(
         me, student_rows, teacher_rows, (student_head, other[0], teacher_head, other[1]), token_mask[None]
     )
     stats = exchange(stats, "y")
-    partial, parts = gradient(stats, s, d, (student_head, other[0]), n_dp * CORES)
+    partial, parts = gradient(stats, s, d, near_heads, n_dp * CORES)
     summed = lax.psum_scatter(partial, "y", scatter_dimension=0, tiled=True)
 
     totals = jnp.sum(exchange(parts[:, None], ("dp", "core")), axis=(0, 1))

time: 161 us -> 161 us (level)
    ppermute x3, waiting for transfers between devices: 9.64 us -> 14.6 us  [ring_gather(): r = lax.ppermute(r, axis, right)]
    all_to_all x2, waiting for transfers between devices: 24.3 us -> 20 us  [exchange(): return lax.all_to_all(x, axis, split_axis=0, concat_axis=0, tiled=True)]
    ppermute x3, starting transfers between devices: 13.7 us -> 11 us  [ring_gather(): l = lax.ppermute(l, axis, left)]
    ppermute x3, starting transfers between devices: 8.14 us -> 10.4 us  [ring_gather(): r = lax.ppermute(r, axis, right)]
  transfers between devices with their start and end apart: 14 -> 14, of which waited for: 10 -> 9; matrix products, arithmetic and copies ran while one was open for 3% -> 3% of each run, Pallas kernels for 0% -> 0%
where the time goes in v7:
time: 161 us; the launch traced here: 160 us
  waiting for transfers between devices  56.9 us (35%)
  starting transfers between devices  55.5 us (34%)
  between operations  17.2 us (11%)
  blocking collectives  14.6 us (9%)
  Pallas kernels  8.11 us (5%)
  other arithmetic  4.43 us (3%)
  local copies, waits for them, and re-layouts  2.17 us (1%)
    all_to_all x2, starting transfers between devices, exchange(): return lax.all_to_all(x, axis, split_axis=0, concat_axis=0, tiled=True)  22.6 us
    all_to_all x2, waiting for transfers between devices, exchange(): return lax.all_to_all(x, axis, split_axis=0, concat_axis=0, tiled=True)  20 us
    reduce_scatter x1, waiting for transfers between devices, body(): summed = lax.psum_scatter(partial, 'y', scatter_dimension=0, tiled=True)  19.4 us
    all_to_all x1, blocking collectives, exchange(): return lax.all_to_all(x, axis, split_axis=0, concat_axis=0, tiled=True)  14.6 us
    ppermute x3, waiting for transfers between devices, ring_gather(): r = lax.ppermute(r, axis, right)  14.6 us
    ppermute x3, starting transfers between devices, ring_gather(): l = lax.ppermute(l, axis, left)  11 us
    ppermute x3, starting transfers between devices, ring_gather(): r = lax.ppermute(r, axis, right)  10.4 us
    pallas_call x1, Pallas kernels, logits(): pl.pallas_call(logits_kernel, in_specs=[pl.BlockSpec(memory_space=pltpu.S...  5.24 us
  transfers between devices with their start and end apart: 14, of which 9 were waited for; matrix products, arithmetic and copies ran while one was open for 3% of the time, Pallas kernels for 0%

profile of v7, /device:TPU:6, one launch (start us, length us, event | category | flops | bytes accessed | tf_op | source)
XLA Modules:
  0.0 159.7 jit_solution(3603667508826764984)
XLA Ops:
  7.2 0.0 all-gather.3.cloned.1.call-start
  7.2 0.7 all-gather.3.cloned.1.call-update
  7.9 0.0 reduce-scatter.2.cloned.1.call-start
  8.0 0.7 fusion.8
  8.6 0.2 convert_reduce_fusion
  8.8 0.1 broadcast_in_dim.115
  8.9 1.0 pad_maximum_fusion
  9.9 0.0 copy-start
  9.9 78.2 %while.22 = (s32[]{:T(128)}, s32[32]{0:T(128)S(1)}, bf16[8,32,4096]{2,1,0:T(8,128)(2,1)S(1)}, bf16[4096,256]{1,0:T(8,128)(2,1)}, bf16[4096,256]{1,0:T(8,128)(2,1...) while((s32[]{:T(128)}, s32[32]{0:T(128)S(1)}, ...), condition=%wide.region_2.3_spmd.clone, body=%wide.region_1.2_spmd.clone.sunk | while | flops 34484352 | bytes 33958916 | solution.py:232
  9.9 0.3 convolution_convert_fusion.3
  10.2 1.0 reshape.50
  11.2 13.4 %all-to-all-start = ((bf16[32,2,4224]{2,1,0:T(2,128)(2,1)}), bf16[32,2,4224]{2,1,0:T(2,128)(2,1)S(1)}, u32[]{:S(2)}, u32[]{:S(2)}) async-start(bf16[32,2,4224]{2,1,0:T(2,128)(2,1)} %reshape.50), calls=%async_computation | async-start | bytes 1081344 | tf_op jit(solution)/shard_map/while/body/all_to_all | solution.py:23
  24.6 1.9 %collective-permute-start.2 = (bf16[4096,256]{1,0:T(8,128)(2,1)}, bf16[4096,256]{1,0:T(8,128)(2,1)}, u32[]{:S(2)}, u32[]{:S(2)}) collective-permute-start(bf16[4096,256]{1,0:T(8,128)(2,1)} %get-tuple-element.388), channel_id=1, source_target_pairs={{0,1},{1,0},{2,3},{3,2},{4,5},{5,4},{6,7},{7,6},{8,9},{9,8},{10,11... | collective-permute-start | bytes 6291464 | tf_op jit(solution)/shard_map/while/body/ppermute | solution.py:221
  26.5 2.4 %collective-permute-start.3 = (bf16[4096,256]{1,0:T(8,128)(2,1)}, bf16[4096,256]{1,0:T(8,128)(2,1)}, u32[]{:S(2)}, u32[]{:S(2)}) collective-permute-start(bf16[4096,256]{1,0:T(8,128)(2,1)} %get-tuple-element.389), channel_id=1, source_target_pairs={{0,1},{1,0},{2,3},{3,2},{4,5},{5,4},{6,7},{7,6},{8,9},{9,8},{10,11... | collective-permute-start | bytes 6291464 | tf_op jit(solution)/shard_map/while/body/ppermute | solution.py:221
  29.0 12.8 %all-to-all-done = bf16[32,2,4224]{2,1,0:T(2,128)(2,1)S(1)} async-done(((bf16[32,2,4224]{2,1,0:T(2,128)(2,1)}), bf16[32,2,4224]{2,1,0:T(2,128)(2,1)S(1)}, u32[]{:S(2)}, u32[]{:S(2)}) %all-to-all-start) | async-done | bytes 540704 | tf_op jit(solution)/shard_map/while/body/all_to_all | solution.py:23
  41.8 0.2 reshape.51
  42.0 0.1 fusion.14
  42.1 0.2 bitcast_dynamic-update-slice_fusion.18
  42.3 3.5 %collective-permute-start = (bf16[32,4096]{1,0:T(8,128)(2,1)S(1)}, bf16[32,4096]{1,0:T(8,128)(2,1)S(1)}, u32[]{:S(2)}, u32[]{:S(2)}) collective-permute-start(bf16[32,4096]{1,0:T(8,128)(2,1)S(1)} %get-tuple-element.387), channel_id=1, source_target_pairs={{0,2},{2,4},{4,6},{6,8},{8,10},{10,12},{12,14},{14,0},{1,3},{3,5},... | collective-permute-start | bytes 786440 | tf_op jit(solution)/shard_map/while/body/ppermute | solution.py:39
  45.9 3.8 %collective-permute-start.1 = (bf16[32,4096]{1,0:T(8,128)(2,1)S(1)}, bf16[32,4096]{1,0:T(8,128)(2,1)S(1)}, u32[]{:S(2)}, u32[]{:S(2)}) collective-permute-start(bf16[32,4096]{1,0:T(8,128)(2,1)S(1)} %get-tuple-element.387), channel_id=1, source_target_pairs={{0,14},{2,0},{4,2},{6,4},{8,6},{10,8},{12,10},{14,12},{1,15},{3,1}... | collective-permute-start | bytes 786440 | tf_op jit(solution)/shard_map/while/body/ppermute | solution.py:40
  49.7 0.1 slice_reduce_fusion.2
  49.8 9.2 %collective-permute-done = bf16[32,4096]{1,0:T(8,128)(2,1)S(1)} collective-permute-done((bf16[32,4096]{1,0:T(8,128)(2,1)S(1)}, bf16[32,4096]{1,0:T(8,128)(2,1)S(1)}, u32[]{:S(2)}, u32[]{:S(2)}) %collective-permute-start) | collective-permute-done | bytes 262176 | tf_op jit(solution)/shard_map/while/body/ppermute | solution.py:39
  59.0 0.2 collective-permute-done.1
  59.2 0.0 collective-permute-done.2
  59.2 0.0 collective-permute-done.3
  59.2 4.4 %collective-permute-start.4 = (bf16[32,4096]{1,0:T(8,128)(2,1)S(1)}, bf16[32,4096]{1,0:T(8,128)(2,1)S(1)}, u32[]{:S(2)}, u32[]{:S(2)}) collective-permute-start(bf16[32,4096]{1,0:T(8,128)(2,1)S(1)} %collective-permute-done), channel_id=1, source_target_pairs={{0,2},{2,4},{4,6},{6,8},{8,10},{10,12},{12,14},{14,0},{1,3},{3,5},... | collective-permute-start | bytes 786440 | tf_op jit(solution)/shard_map/while/body/ppermute | solution.py:39
  63.6 2.6 %collective-permute-start.5 = (bf16[32,4096]{1,0:T(8,128)(2,1)S(1)}, bf16[32,4096]{1,0:T(8,128)(2,1)S(1)}, u32[]{:S(2)}, u32[]{:S(2)}) collective-permute-start(bf16[32,4096]{1,0:T(8,128)(2,1)S(1)} %collective-permute-done.1), channel_id=1, source_target_pairs={{0,14},{2,0},{4,2},{6,4},{8,6},{10,8},{12,10},{14,12},{1,15},{3,1}... | collective-permute-start | bytes 786440 | tf_op jit(solution)/shard_map/while/body/ppermute | solution.py:40
  66.3 3.0 %collective-permute-done.4 = bf16[32,4096]{1,0:T(8,128)(2,1)S(1)} collective-permute-done((bf16[32,4096]{1,0:T(8,128)(2,1)S(1)}, bf16[32,4096]{1,0:T(8,128)(2,1)S(1)}, u32[]{:S(2)}, u32[]{:S(2)}) %collective-permute-start.4) | collective-permute-done | bytes 262176 | tf_op jit(solution)/shard_map/while/body/ppermute | solution.py:39
  69.3 2.5 %collective-permute-start.6 = (bf16[32,4096]{1,0:T(8,128)(2,1)S(1)}, bf16[32,4096]{1,0:T(8,128)(2,1)S(1)}, u32[]{:S(2)}, u32[]{:S(2)}) collective-permute-start(bf16[32,4096]{1,0:T(8,128)(2,1)S(1)} %collective-permute-done.4), channel_id=1, source_target_pairs={{0,2},{2,4},{4,6},{6,8},{8,10},{10,12},{12,14},{14,0},{1,3},{3,5},... | collective-permute-start | bytes 786440 | tf_op jit(solution)/shard_map/while/body/ppermute | solution.py:39
  71.9 0.0 collective-permute-done.5
  71.9 4.5 %collective-permute-start.7 = (bf16[32,4096]{1,0:T(8,128)(2,1)S(1)}, bf16[32,4096]{1,0:T(8,128)(2,1)S(1)}, u32[]{:S(2)}, u32[]{:S(2)}) collective-permute-start(bf16[32,4096]{1,0:T(8,128)(2,1)S(1)} %collective-permute-done.5), channel_id=1, source_target_pairs={{0,14},{2,0},{4,2},{6,4},{8,6},{10,8},{12,10},{14,12},{1,15},{3,1}... | collective-permute-start | bytes 786440 | tf_op jit(solution)/shard_map/while/body/ppermute | solution.py:40
  76.5 2.3 %collective-permute-done.6 = bf16[32,4096]{1,0:T(8,128)(2,1)S(1)} collective-permute-done((bf16[32,4096]{1,0:T(8,128)(2,1)S(1)}, bf16[32,4096]{1,0:T(8,128)(2,1)S(1)}, u32[]{:S(2)}, u32[]{:S(2)}) %collective-permute-start.6) | collective-permute-done | bytes 262176 | tf_op jit(solution)/shard_map/while/body/ppermute | solution.py:39
  78.8 1.9 %collective-permute-start.8 = (bf16[32,2560]{1,0:T(8,128)(2,1)S(1)}, bf16[32,2560]{1,0:T(8,128)(2,1)S(1)}, u32[]{:S(2)}, u32[]{:S(2)}) collective-permute-start(bf16[32,2560]{1,0:T(8,128)(2,1)S(1)} %slice.90), channel_id=1, source_target_pairs={{0,2},{2,4},{4,6},{6,8},{8,10},{10,12},{12,14},{14,0},{1,3},{3,5},... | collective-permute-start | bytes 491528 | tf_op jit(solution)/shard_map/while/body/ppermute | solution.py:45
  80.7 0.0 collective-permute-done.7
  80.8 5.1 %collective-permute-start.9 = (bf16[32,1536]{1,0:T(8,128)(2,1)S(1)}, bf16[32,1536]{1,0:T(8,128)(2,1)S(1)}, u32[]{:S(2)}, u32[]{:S(2)}) collective-permute-start(bf16[32,1536]{1,0:T(8,128)(2,1)S(1)} %slice.91), channel_id=1, source_target_pairs={{0,14},{2,0},{4,2},{6,4},{8,6},{10,8},{12,10},{14,12},{1,15},{3,1}... | collective-permute-start | bytes 294920 | tf_op jit(solution)/shard_map/while/body/ppermute | solution.py:46
  86.0 1.3 collective-permute-done.8
  87.3 0.8 collective-permute-done.9
  88.1 0.0 all-gather.3.cloned.1.call-done
  88.1 0.0 copy-done
  88.2 5.2 %logits.1 = (f32[256,512]{1,0:T(8,128)S(1)}, f32[256,512]{1,0:T(8,128)S(1)}, f32[8,8,256]{2,1,0:T(8,128)S(1)}, bf16[4096,256]{1,0:T(8,128)(2,1)S(1)}, bf16[4096,256]{1,0:T(8,128)(2,1)S(1)}) custom-call(s32[1]{0:T(128)} %bitcast.me_ref, bf16[8,32,4096]{2,1,0:T(8,128)(2,1)} %bitcast.48, bf16[8,32,4096]{2,1,0:T(8,128)(2,1)S(1)} %get-tuple-element.258.xt, ...), custom_call_target="tpu_custom_call" | custom-call | flops 2147483648 | bytes 12582912 | tf_op jit(solution)/shard_map/logits/pallas_call | solution.py:125
  93.4 14.6 %all_to_all.24.stats_ref = f32[8,8,256]{2,1,0:T(8,128)S(1)} all-to-all(f32[8,8,256]{2,1,0:T(8,128)S(1)} %get-tuple-element.261), channel_id=1, replica_groups=mesh['dp'=32,'y'=8,'core'=2] {'y'}, dimensions={0} | all-to-all | bytes 131072 | tf_op jit(solution)/shard_map/all_to_all | solution.py:23
  108.0 2.9 %gradient.1 = (bf16[256,4096]{1,0:T(8,128)(2,1)}, f32[64,128]{1,0:T(8,128)}) custom-call(f32[8,8,256]{2,1,0:T(8,128)S(1)} %all_to_all.24.stats_ref, f32[256,512]{1,0:T(8,128)S(1)} %get-tuple-element.262.s_ref, f32[256,512]{1,0:T(8,128)S(1)} %get-tuple-element.263.d_ref, bf16[4096,256]{1,0:T(8,128)(2,1)S(1)} %get-tuple-element.264.w0_ref, ...), custom_call_target="tpu_custom_call" | custom-call | flops 1073741824 | bytes 7340032 | tf_op jit(solution)/shard_map/gradient/pallas_call | solution.py:178
  110.8 0.0 reduce-scatter.2.cloned.1.call-update
  110.9 9.2 %all-to-all-start.2 = ((f32[64,1,128]{2,1,0:T(1,128)}), f32[64,1,128]{2,1,0:T(1,128)S(1)}, u32[]{:S(2)}, u32[]{:S(2)}) async-start(f32[64,1,128]{2,1,0:T(1,128)} %bitcast.4), calls=%async_computation.2 | async-start | bytes 65536 | tf_op jit(solution)/shard_map/all_to_all | solution.py:23
  120.8 7.2 %all-to-all-done.2 = f32[64,1,128]{2,1,0:T(1,128)S(1)} async-done(((f32[64,1,128]{2,1,0:T(1,128)}), f32[64,1,128]{2,1,0:T(1,128)S(1)}, u32[]{:S(2)}, u32[]{:S(2)}) %all-to-all-start.2) | async-done | bytes 32800 | tf_op jit(solution)/shard_map/all_to_all | solution.py:23
  127.9 0.1 reduce_sum.19
  128.0 0.6 fusion.9
  129.9 0.7 multiply_divide_fusion
  130.6 19.4 %reduce-scatter.2.cloned.1.call-done = bf16[32,4096]{1,0:T(8,128)(2,1)} async-done(((bf16[256,4096]{1,0:T(8,128)(2,1)}), bf16[32,4096]{1,0:T(8,128)(2,1)}) %reduce-scatter.2.cloned.1.call-update) | async-done | bytes 262160 | tf_op jit(solution)/shard_map/reduce_scatter | solution.py:240
  149.9 1.8 %multiply_convert_fusion = bf16[32,4096]{1,0:T(8,128)(2,1)} fusion(bf16[32,4096]{1,0:T(8,128)(2,1)} %reduce-scatter.2.cloned.1.call-done, f32[32]{0:T(128)S(1)} %multiply_divide_fusion), kind=kLoop, calls=%fused_computation.20 | loop fusion | flops 393216 | bytes 524416 | tf_op jit(solution)/shard_map/convert_element_type | solution.py:246
  (12 shorter events, 0.2 us)
Async XLA Ops:
  7.2 81.0 %all-gather.3.cloned.1.call-start = ((), (), s32[]{:S(2)}) async-start(), calls=%async_computation.5 | async-start | bytes 2359296 | tf_op jit(solution)/shard_map/all_gather | solution.py:229
  7.9 142.0 %reduce-scatter.2.cloned.1.call-start = ((), (), s32[]{:S(2)}) async-start(), calls=%async_computation.4 | async-start | bytes 2359296 | tf_op jit(solution)/shard_map/reduce_scatter | solution.py:240
  9.9 78.3 %copy-start = (s32[32]{0:T(128)S(1)}, s32[32]{0:T(128)}, u32[]{:S(2)}) copy-start(s32[32]{0:T(128)} %param.12) | copy-start | bytes 388
  11.2 30.6 %all-to-all-start = ((bf16[32,2,4224]{2,1,0:T(2,128)(2,1)}), bf16[32,2,4224]{2,1,0:T(2,128)(2,1)S(1)}, u32[]{:S(2)}, u32[]{:S(2)}) async-start(bf16[32,2,4224]{2,1,0:T(2,128)(2,1)} %reshape.50), calls=%async_computation | async-start | bytes 1081344 | tf_op jit(solution)/shard_map/while/body/all_to_all | solution.py:23
  24.6 34.6 %collective-permute-start.2 = (bf16[4096,256]{1,0:T(8,128)(2,1)}, bf16[4096,256]{1,0:T(8,128)(2,1)}, u32[]{:S(2)}, u32[]{:S(2)}) collective-permute-start(bf16[4096,256]{1,0:T(8,128)(2,1)} %get-tuple-element.388), channel_id=1, source_target_pairs={{0,1},{1,0},{2,3},{3,2},{4,5},{5,4},{6,7},{7,6},{8,9},{9,8},{10,11... | collective-permute-start | bytes 6291464 | tf_op jit(solution)/shard_map/while/body/ppermute | solution.py:221
  26.5 32.7 %collective-permute-start.3 = (bf16[4096,256]{1,0:T(8,128)(2,1)}, bf16[4096,256]{1,0:T(8,128)(2,1)}, u32[]{:S(2)}, u32[]{:S(2)}) collective-permute-start(bf16[4096,256]{1,0:T(8,128)(2,1)} %get-tuple-element.389), channel_id=1, source_target_pairs={{0,1},{1,0},{2,3},{3,2},{4,5},{5,4},{6,7},{7,6},{8,9},{9,8},{10,11... | collective-permute-start | bytes 6291464 | tf_op jit(solution)/shard_map/while/body/ppermute | solution.py:221
  42.3 16.7 %collective-permute-start = (bf16[32,4096]{1,0:T(8,128)(2,1)S(1)}, bf16[32,4096]{1,0:T(8,128)(2,1)S(1)}, u32[]{:S(2)}, u32[]{:S(2)}) collective-permute-start(bf16[32,4096]{1,0:T(8,128)(2,1)S(1)} %get-tuple-element.387), channel_id=1, source_target_pairs={{0,2},{2,4},{4,6},{6,8},{8,10},{10,12},{12,14},{14,0},{1,3},{3,5},... | collective-permute-start | bytes 786440 | tf_op jit(solution)/shard_map/while/body/ppermute | solution.py:39
  45.9 13.3 %collective-permute-start.1 = (bf16[32,4096]{1,0:T(8,128)(2,1)S(1)}, bf16[32,4096]{1,0:T(8,128)(2,1)S(1)}, u32[]{:S(2)}, u32[]{:S(2)}) collective-permute-start(bf16[32,4096]{1,0:T(8,128)(2,1)S(1)} %get-tuple-element.387), channel_id=1, source_target_pairs={{0,14},{2,0},{4,2},{6,4},{8,6},{10,8},{12,10},{14,12},{1,15},{3,1}... | collective-permute-start | bytes 786440 | tf_op jit(solution)/shard_map/while/body/ppermute | solution.py:40
  59.2 10.1 %collective-permute-start.4 = (bf16[32,4096]{1,0:T(8,128)(2,1)S(1)}, bf16[32,4096]{1,0:T(8,128)(2,1)S(1)}, u32[]{:S(2)}, u32[]{:S(2)}) collective-permute-start(bf16[32,4096]{1,0:T(8,128)(2,1)S(1)} %collective-permute-done), channel_id=1, source_target_pairs={{0,2},{2,4},{4,6},{6,8},{8,10},{10,12},{12,14},{14,0},{1,3},{3,5},... | collective-permute-start | bytes 786440 | tf_op jit(solution)/shard_map/while/body/ppermute | solution.py:39
  63.6 8.3 %collective-permute-start.5 = (bf16[32,4096]{1,0:T(8,128)(2,1)S(1)}, bf16[32,4096]{1,0:T(8,128)(2,1)S(1)}, u32[]{:S(2)}, u32[]{:S(2)}) collective-permute-start(bf16[32,4096]{1,0:T(8,128)(2,1)S(1)} %collective-permute-done.1), channel_id=1, source_target_pairs={{0,14},{2,0},{4,2},{6,4},{8,6},{10,8},{12,10},{14,12},{1,15},{3,1}... | collective-permute-start | bytes 786440 | tf_op jit(solution)/shard_map/while/body/ppermute | solution.py:40
  69.3 9.5 %collective-permute-start.6 = (bf16[32,4096]{1,0:T(8,128)(2,1)S(1)}, bf16[32,4096]{1,0:T(8,128)(2,1)S(1)}, u32[]{:S(2)}, u32[]{:S(2)}) collective-permute-start(bf16[32,4096]{1,0:T(8,128)(2,1)S(1)} %collective-permute-done.4), channel_id=1, source_target_pairs={{0,2},{2,4},{4,6},{6,8},{8,10},{10,12},{12,14},{14,0},{1,3},{3,5},... | collective-permute-start | bytes 786440 | tf_op jit(solution)/shard_map/while/body/ppermute | solution.py:39
  71.9 8.9 %collective-permute-start.7 = (bf16[32,4096]{1,0:T(8,128)(2,1)S(1)}, bf16[32,4096]{1,0:T(8,128)(2,1)S(1)}, u32[]{:S(2)}, u32[]{:S(2)}) collective-permute-start(bf16[32,4096]{1,0:T(8,128)(2,1)S(1)} %collective-permute-done.5), channel_id=1, source_target_pairs={{0,14},{2,0},{4,2},{6,4},{8,6},{10,8},{12,10},{14,12},{1,15},{3,1}... | collective-permute-start | bytes 786440 | tf_op jit(solution)/shard_map/while/body/ppermute | solution.py:40
  78.8 8.4 %collective-permute-start.8 = (bf16[32,2560]{1,0:T(8,128)(2,1)S(1)}, bf16[32,2560]{1,0:T(8,128)(2,1)S(1)}, u32[]{:S(2)}, u32[]{:S(2)}) collective-permute-start(bf16[32,2560]{1,0:T(8,128)(2,1)S(1)} %slice.90), channel_id=1, source_target_pairs={{0,2},{2,4},{4,6},{6,8},{8,10},{10,12},{12,14},{14,0},{1,3},{3,5},... | collective-permute-start | bytes 491528 | tf_op jit(solution)/shard_map/while/body/ppermute | solution.py:45
  80.8 7.3 %collective-permute-start.9 = (bf16[32,1536]{1,0:T(8,128)(2,1)S(1)}, bf16[32,1536]{1,0:T(8,128)(2,1)S(1)}, u32[]{:S(2)}, u32[]{:S(2)}) collective-permute-start(bf16[32,1536]{1,0:T(8,128)(2,1)S(1)} %slice.91), channel_id=1, source_target_pairs={{0,14},{2,0},{4,2},{6,4},{8,6},{10,8},{12,10},{14,12},{1,15},{3,1}... | collective-permute-start | bytes 294920 | tf_op jit(solution)/shard_map/while/body/ppermute | solution.py:46
  110.9 17.0 %all-to-all-start.2 = ((f32[64,1,128]{2,1,0:T(1,128)}), f32[64,1,128]{2,1,0:T(1,128)S(1)}, u32[]{:S(2)}, u32[]{:S(2)}) async-start(f32[64,1,128]{2,1,0:T(1,128)} %bitcast.4), calls=%async_computation.2 | async-start | bytes 65536 | tf_op jit(solution)/shard_map/all_to_all | solution.py:23
Sparse Core Ops, SparseCore 0:
  10.1 51.2 all-gather.2
  111.0 38.8 reduce-scatter.1

commit v8 on v7

--- a/solution.py
+++ b/solution.py
@@ -28,7 +28,7 @@
     me = lax.axis_index(axis)
     right = [(i, (i + 1) % n) for i in range(n)]
     left = [(i, (i - 1) % n) for i in range(n)]
-    share = x.shape[1] * 5 // 8 // 128 * 128
+    share = x.shape[1] * 3 // 4 // 128 * 128
 
     def put(out, block, owner, column=0):
         return lax.dynamic_update_slice(out, block[None], (lax.rem(owner, n), 0, column))

time: 161 us -> 160 us (level)
  no operation moved by 1% of the time
where the time goes in v8:
time: 160 us; the launch traced here: 159 us
  waiting for transfers between devices  56.6 us (35%)
  starting transfers between devices  55.5 us (35%)
  between operations  17.2 us (11%)
  blocking collectives  14.5 us (9%)
  Pallas kernels  8.11 us (5%)
  other arithmetic  4.43 us (3%)
  local copies, waits for them, and re-layouts  2.17 us (1%)
    all_to_all x2, starting transfers between devices, exchange(): return lax.all_to_all(x, axis, split_axis=0, concat_axis=0, tiled=True)  22.6 us
    all_to_all x2, waiting for transfers between devices, exchange(): return lax.all_to_all(x, axis, split_axis=0, concat_axis=0, tiled=True)  20 us
    reduce_scatter x1, waiting for transfers between devices, body(): summed = lax.psum_scatter(partial, 'y', scatter_dimension=0, tiled=True)  19.4 us
    ppermute x3, waiting for transfers between devices, ring_gather(): r = lax.ppermute(r, axis, right)  14.6 us
    all_to_all x1, blocking collectives, exchange(): return lax.all_to_all(x, axis, split_axis=0, concat_axis=0, tiled=True)  14.5 us
    ppermute x3, starting transfers between devices, ring_gather(): l = lax.ppermute(l, axis, left)  11 us
    ppermute x3, starting transfers between devices, ring_gather(): r = lax.ppermute(r, axis, right)  10.4 us
    pallas_call x1, Pallas kernels, logits(): pl.pallas_call(logits_kernel, in_specs=[pl.BlockSpec(memory_space=pltpu.S...  5.24 us
  transfers between devices with their start and end apart: 14, of which 9 were waited for; matrix products, arithmetic and copies ran while one was open for 3% of the time, Pallas kernels for 0%

profile of v8, /device:TPU:6, one launch (start us, length us, event | category | flops | bytes accessed | tf_op | source)
XLA Modules:
  0.0 159.3 jit_solution(65324777413312280)
XLA Ops:
  7.2 0.0 all-gather.3.cloned.1.call-start
  7.2 0.7 all-gather.3.cloned.1.call-update
  7.9 0.0 reduce-scatter.2.cloned.1.call-start
  8.0 0.7 fusion.8
  8.6 0.2 convert_reduce_fusion
  8.8 0.1 broadcast_in_dim.115
  8.9 1.0 pad_maximum_fusion
  9.9 0.0 copy-start
  9.9 77.9 %while.22 = (s32[]{:T(128)}, s32[32]{0:T(128)S(1)}, bf16[8,32,4096]{2,1,0:T(8,128)(2,1)S(1)}, bf16[4096,256]{1,0:T(8,128)(2,1)}, bf16[4096,256]{1,0:T(8,128)(2,1...) while((s32[]{:T(128)}, s32[32]{0:T(128)S(1)}, ...), condition=%wide.region_2.3_spmd.clone, body=%wide.region_1.2_spmd.clone.sunk | while | flops 34484352 | bytes 33958916 | solution.py:232
  9.9 0.3 convolution_convert_fusion.3
  10.2 1.0 reshape.50
  11.2 13.4 %all-to-all-start = ((bf16[32,2,4224]{2,1,0:T(2,128)(2,1)}), bf16[32,2,4224]{2,1,0:T(2,128)(2,1)S(1)}, u32[]{:S(2)}, u32[]{:S(2)}) async-start(bf16[32,2,4224]{2,1,0:T(2,128)(2,1)} %reshape.50), calls=%async_computation | async-start | bytes 1081344 | tf_op jit(solution)/shard_map/while/body/all_to_all | solution.py:23
  24.6 1.9 %collective-permute-start.2 = (bf16[4096,256]{1,0:T(8,128)(2,1)}, bf16[4096,256]{1,0:T(8,128)(2,1)}, u32[]{:S(2)}, u32[]{:S(2)}) collective-permute-start(bf16[4096,256]{1,0:T(8,128)(2,1)} %get-tuple-element.388), channel_id=1, source_target_pairs={{0,1},{1,0},{2,3},{3,2},{4,5},{5,4},{6,7},{7,6},{8,9},{9,8},{10,11... | collective-permute-start | bytes 6291464 | tf_op jit(solution)/shard_map/while/body/ppermute | solution.py:221
  26.5 2.4 %collective-permute-start.3 = (bf16[4096,256]{1,0:T(8,128)(2,1)}, bf16[4096,256]{1,0:T(8,128)(2,1)}, u32[]{:S(2)}, u32[]{:S(2)}) collective-permute-start(bf16[4096,256]{1,0:T(8,128)(2,1)} %get-tuple-element.389), channel_id=1, source_target_pairs={{0,1},{1,0},{2,3},{3,2},{4,5},{5,4},{6,7},{7,6},{8,9},{9,8},{10,11... | collective-permute-start | bytes 6291464 | tf_op jit(solution)/shard_map/while/body/ppermute | solution.py:221
  29.0 12.8 %all-to-all-done = bf16[32,2,4224]{2,1,0:T(2,128)(2,1)S(1)} async-done(((bf16[32,2,4224]{2,1,0:T(2,128)(2,1)}), bf16[32,2,4224]{2,1,0:T(2,128)(2,1)S(1)}, u32[]{:S(2)}, u32[]{:S(2)}) %all-to-all-start) | async-done | bytes 540704 | tf_op jit(solution)/shard_map/while/body/all_to_all | solution.py:23
  41.8 0.2 reshape.51
  42.0 0.1 fusion.14
  42.1 0.2 bitcast_dynamic-update-slice_fusion.18
  42.3 3.5 %collective-permute-start = (bf16[32,4096]{1,0:T(8,128)(2,1)S(1)}, bf16[32,4096]{1,0:T(8,128)(2,1)S(1)}, u32[]{:S(2)}, u32[]{:S(2)}) collective-permute-start(bf16[32,4096]{1,0:T(8,128)(2,1)S(1)} %get-tuple-element.387), channel_id=1, source_target_pairs={{0,2},{2,4},{4,6},{6,8},{8,10},{10,12},{12,14},{14,0},{1,3},{3,5},... | collective-permute-start | bytes 786440 | tf_op jit(solution)/shard_map/while/body/ppermute | solution.py:39
  45.9 3.8 %collective-permute-start.1 = (bf16[32,4096]{1,0:T(8,128)(2,1)S(1)}, bf16[32,4096]{1,0:T(8,128)(2,1)S(1)}, u32[]{:S(2)}, u32[]{:S(2)}) collective-permute-start(bf16[32,4096]{1,0:T(8,128)(2,1)S(1)} %get-tuple-element.387), channel_id=1, source_target_pairs={{0,14},{2,0},{4,2},{6,4},{8,6},{10,8},{12,10},{14,12},{1,15},{3,1}... | collective-permute-start | bytes 786440 | tf_op jit(solution)/shard_map/while/body/ppermute | solution.py:40
  49.7 0.1 slice_reduce_fusion.2
  49.8 9.2 %collective-permute-done = bf16[32,4096]{1,0:T(8,128)(2,1)S(1)} collective-permute-done((bf16[32,4096]{1,0:T(8,128)(2,1)S(1)}, bf16[32,4096]{1,0:T(8,128)(2,1)S(1)}, u32[]{:S(2)}, u32[]{:S(2)}) %collective-permute-start) | collective-permute-done | bytes 262176 | tf_op jit(solution)/shard_map/while/body/ppermute | solution.py:39
  59.0 0.2 collective-permute-done.1
  59.2 0.0 collective-permute-done.2
  59.2 0.0 collective-permute-done.3
  59.2 4.4 %collective-permute-start.4 = (bf16[32,4096]{1,0:T(8,128)(2,1)S(1)}, bf16[32,4096]{1,0:T(8,128)(2,1)S(1)}, u32[]{:S(2)}, u32[]{:S(2)}) collective-permute-start(bf16[32,4096]{1,0:T(8,128)(2,1)S(1)} %collective-permute-done), channel_id=1, source_target_pairs={{0,2},{2,4},{4,6},{6,8},{8,10},{10,12},{12,14},{14,0},{1,3},{3,5},... | collective-permute-start | bytes 786440 | tf_op jit(solution)/shard_map/while/body/ppermute | solution.py:39
  63.6 2.6 %collective-permute-start.5 = (bf16[32,4096]{1,0:T(8,128)(2,1)S(1)}, bf16[32,4096]{1,0:T(8,128)(2,1)S(1)}, u32[]{:S(2)}, u32[]{:S(2)}) collective-permute-start(bf16[32,4096]{1,0:T(8,128)(2,1)S(1)} %collective-permute-done.1), channel_id=1, source_target_pairs={{0,14},{2,0},{4,2},{6,4},{8,6},{10,8},{12,10},{14,12},{1,15},{3,1}... | collective-permute-start | bytes 786440 | tf_op jit(solution)/shard_map/while/body/ppermute | solution.py:40
  66.3 3.0 %collective-permute-done.4 = bf16[32,4096]{1,0:T(8,128)(2,1)S(1)} collective-permute-done((bf16[32,4096]{1,0:T(8,128)(2,1)S(1)}, bf16[32,4096]{1,0:T(8,128)(2,1)S(1)}, u32[]{:S(2)}, u32[]{:S(2)}) %collective-permute-start.4) | collective-permute-done | bytes 262176 | tf_op jit(solution)/shard_map/while/body/ppermute | solution.py:39
  69.3 2.5 %collective-permute-start.6 = (bf16[32,4096]{1,0:T(8,128)(2,1)S(1)}, bf16[32,4096]{1,0:T(8,128)(2,1)S(1)}, u32[]{:S(2)}, u32[]{:S(2)}) collective-permute-start(bf16[32,4096]{1,0:T(8,128)(2,1)S(1)} %collective-permute-done.4), channel_id=1, source_target_pairs={{0,2},{2,4},{4,6},{6,8},{8,10},{10,12},{12,14},{14,0},{1,3},{3,5},... | collective-permute-start | bytes 786440 | tf_op jit(solution)/shard_map/while/body/ppermute | solution.py:39
  71.9 0.0 collective-permute-done.5
  71.9 4.5 %collective-permute-start.7 = (bf16[32,4096]{1,0:T(8,128)(2,1)S(1)}, bf16[32,4096]{1,0:T(8,128)(2,1)S(1)}, u32[]{:S(2)}, u32[]{:S(2)}) collective-permute-start(bf16[32,4096]{1,0:T(8,128)(2,1)S(1)} %collective-permute-done.5), channel_id=1, source_target_pairs={{0,14},{2,0},{4,2},{6,4},{8,6},{10,8},{12,10},{14,12},{1,15},{3,1}... | collective-permute-start | bytes 786440 | tf_op jit(solution)/shard_map/while/body/ppermute | solution.py:40
  76.5 2.3 %collective-permute-done.6 = bf16[32,4096]{1,0:T(8,128)(2,1)S(1)} collective-permute-done((bf16[32,4096]{1,0:T(8,128)(2,1)S(1)}, bf16[32,4096]{1,0:T(8,128)(2,1)S(1)}, u32[]{:S(2)}, u32[]{:S(2)}) %collective-permute-start.6) | collective-permute-done | bytes 262176 | tf_op jit(solution)/shard_map/while/body/ppermute | solution.py:39
  78.8 1.9 %collective-permute-start.8 = (bf16[32,3072]{1,0:T(8,128)(2,1)S(1)}, bf16[32,3072]{1,0:T(8,128)(2,1)S(1)}, u32[]{:S(2)}, u32[]{:S(2)}) collective-permute-start(bf16[32,3072]{1,0:T(8,128)(2,1)S(1)} %slice.90), channel_id=1, source_target_pairs={{0,2},{2,4},{4,6},{6,8},{8,10},{10,12},{12,14},{14,0},{1,3},{3,5},... | collective-permute-start | bytes 589832 | tf_op jit(solution)/shard_map/while/body/ppermute | solution.py:45
  80.7 0.0 collective-permute-done.7
  80.8 5.1 %collective-permute-start.9 = (bf16[32,1024]{1,0:T(8,128)(2,1)S(1)}, bf16[32,1024]{1,0:T(8,128)(2,1)S(1)}, u32[]{:S(2)}, u32[]{:S(2)}) collective-permute-start(bf16[32,1024]{1,0:T(8,128)(2,1)S(1)} %slice.91), channel_id=1, source_target_pairs={{0,14},{2,0},{4,2},{6,4},{8,6},{10,8},{12,10},{14,12},{1,15},{3,1}... | collective-permute-start | bytes 196616 | tf_op jit(solution)/shard_map/while/body/ppermute | solution.py:46
  86.0 1.6 %collective-permute-done.8 = bf16[32,3072]{1,0:T(8,128)(2,1)S(1)} collective-permute-done((bf16[32,3072]{1,0:T(8,128)(2,1)S(1)}, bf16[32,3072]{1,0:T(8,128)(2,1)S(1)}, u32[]{:S(2)}, u32[]{:S(2)}) %collective-permute-start.8) | collective-permute-done | bytes 196640 | tf_op jit(solution)/shard_map/while/body/ppermute | solution.py:45
  87.6 0.2 collective-permute-done.9
  87.8 0.0 all-gather.3.cloned.1.call-done
  87.8 0.0 copy-done
  87.8 5.2 %logits.1 = (f32[256,512]{1,0:T(8,128)S(1)}, f32[256,512]{1,0:T(8,128)S(1)}, f32[8,8,256]{2,1,0:T(8,128)S(1)}, bf16[4096,256]{1,0:T(8,128)(2,1)S(1)}, bf16[4096,256]{1,0:T(8,128)(2,1)S(1)}) custom-call(s32[1]{0:T(128)} %bitcast.me_ref, bf16[8,32,4096]{2,1,0:T(8,128)(2,1)} %bitcast.48, bf16[8,32,4096]{2,1,0:T(8,128)(2,1)S(1)} %get-tuple-element.258.xt, ...), custom_call_target="tpu_custom_call" | custom-call | flops 2147483648 | bytes 12582912 | tf_op jit(solution)/shard_map/logits/pallas_call | solution.py:125
  93.1 14.5 %all_to_all.24.stats_ref = f32[8,8,256]{2,1,0:T(8,128)S(1)} all-to-all(f32[8,8,256]{2,1,0:T(8,128)S(1)} %get-tuple-element.261), channel_id=1, replica_groups=mesh['dp'=32,'y'=8,'core'=2] {'y'}, dimensions={0} | all-to-all | bytes 131072 | tf_op jit(solution)/shard_map/all_to_all | solution.py:23
  107.6 2.9 %gradient.1 = (bf16[256,4096]{1,0:T(8,128)(2,1)}, f32[64,128]{1,0:T(8,128)}) custom-call(f32[8,8,256]{2,1,0:T(8,128)S(1)} %all_to_all.24.stats_ref, f32[256,512]{1,0:T(8,128)S(1)} %get-tuple-element.262.s_ref, f32[256,512]{1,0:T(8,128)S(1)} %get-tuple-element.263.d_ref, bf16[4096,256]{1,0:T(8,128)(2,1)S(1)} %get-tuple-element.264.w0_ref, ...), custom_call_target="tpu_custom_call" | custom-call | flops 1073741824 | bytes 7340032 | tf_op jit(solution)/shard_map/gradient/pallas_call | solution.py:178
  110.5 0.0 reduce-scatter.2.cloned.1.call-update
  110.5 9.2 %all-to-all-start.2 = ((f32[64,1,128]{2,1,0:T(1,128)}), f32[64,1,128]{2,1,0:T(1,128)S(1)}, u32[]{:S(2)}, u32[]{:S(2)}) async-start(f32[64,1,128]{2,1,0:T(1,128)} %bitcast.4), calls=%async_computation.2 | async-start | bytes 65536 | tf_op jit(solution)/shard_map/all_to_all | solution.py:23
  120.4 7.2 %all-to-all-done.2 = f32[64,1,128]{2,1,0:T(1,128)S(1)} async-done(((f32[64,1,128]{2,1,0:T(1,128)}), f32[64,1,128]{2,1,0:T(1,128)S(1)}, u32[]{:S(2)}, u32[]{:S(2)}) %all-to-all-start.2) | async-done | bytes 32800 | tf_op jit(solution)/shard_map/all_to_all | solution.py:23
  127.6 0.1 reduce_sum.19
  127.6 0.6 fusion.9
  129.6 0.7 multiply_divide_fusion
  130.2 19.4 %reduce-scatter.2.cloned.1.call-done = bf16[32,4096]{1,0:T(8,128)(2,1)} async-done(((bf16[256,4096]{1,0:T(8,128)(2,1)}), bf16[32,4096]{1,0:T(8,128)(2,1)}) %reduce-scatter.2.cloned.1.call-update) | async-done | bytes 262160 | tf_op jit(solution)/shard_map/reduce_scatter | solution.py:240
  149.6 1.8 %multiply_convert_fusion = bf16[32,4096]{1,0:T(8,128)(2,1)} fusion(bf16[32,4096]{1,0:T(8,128)(2,1)} %reduce-scatter.2.cloned.1.call-done, f32[32]{0:T(128)S(1)} %multiply_divide_fusion), kind=kLoop, calls=%fused_computation.20 | loop fusion | flops 393216 | bytes 524416 | tf_op jit(solution)/shard_map/convert_element_type | solution.py:246
  (12 shorter events, 0.2 us)
Async XLA Ops:
  7.2 80.7 %all-gather.3.cloned.1.call-start = ((), (), s32[]{:S(2)}) async-start(), calls=%async_computation.5 | async-start | bytes 2359296 | tf_op jit(solution)/shard_map/all_gather | solution.py:229
  7.9 141.7 %reduce-scatter.2.cloned.1.call-start = ((), (), s32[]{:S(2)}) async-start(), calls=%async_computation.4 | async-start | bytes 2359296 | tf_op jit(solution)/shard_map/reduce_scatter | solution.py:240
  9.9 78.0 %copy-start = (s32[32]{0:T(128)S(1)}, s32[32]{0:T(128)}, u32[]{:S(2)}) copy-start(s32[32]{0:T(128)} %param.12) | copy-start | bytes 388
  11.2 30.6 %all-to-all-start = ((bf16[32,2,4224]{2,1,0:T(2,128)(2,1)}), bf16[32,2,4224]{2,1,0:T(2,128)(2,1)S(1)}, u32[]{:S(2)}, u32[]{:S(2)}) async-start(bf16[32,2,4224]{2,1,0:T(2,128)(2,1)} %reshape.50), calls=%async_computation | async-start | bytes 1081344 | tf_op jit(solution)/shard_map/while/body/all_to_all | solution.py:23
  24.6 34.6 %collective-permute-start.2 = (bf16[4096,256]{1,0:T(8,128)(2,1)}, bf16[4096,256]{1,0:T(8,128)(2,1)}, u32[]{:S(2)}, u32[]{:S(2)}) collective-permute-start(bf16[4096,256]{1,0:T(8,128)(2,1)} %get-tuple-element.388), channel_id=1, source_target_pairs={{0,1},{1,0},{2,3},{3,2},{4,5},{5,4},{6,7},{7,6},{8,9},{9,8},{10,11... | collective-permute-start | bytes 6291464 | tf_op jit(solution)/shard_map/while/body/ppermute | solution.py:221
  26.5 32.7 %collective-permute-start.3 = (bf16[4096,256]{1,0:T(8,128)(2,1)}, bf16[4096,256]{1,0:T(8,128)(2,1)}, u32[]{:S(2)}, u32[]{:S(2)}) collective-permute-start(bf16[4096,256]{1,0:T(8,128)(2,1)} %get-tuple-element.389), channel_id=1, source_target_pairs={{0,1},{1,0},{2,3},{3,2},{4,5},{5,4},{6,7},{7,6},{8,9},{9,8},{10,11... | collective-permute-start | bytes 6291464 | tf_op jit(solution)/shard_map/while/body/ppermute | solution.py:221
  42.3 16.7 %collective-permute-start = (bf16[32,4096]{1,0:T(8,128)(2,1)S(1)}, bf16[32,4096]{1,0:T(8,128)(2,1)S(1)}, u32[]{:S(2)}, u32[]{:S(2)}) collective-permute-start(bf16[32,4096]{1,0:T(8,128)(2,1)S(1)} %get-tuple-element.387), channel_id=1, source_target_pairs={{0,2},{2,4},{4,6},{6,8},{8,10},{10,12},{12,14},{14,0},{1,3},{3,5},... | collective-permute-start | bytes 786440 | tf_op jit(solution)/shard_map/while/body/ppermute | solution.py:39
  45.9 13.3 %collective-permute-start.1 = (bf16[32,4096]{1,0:T(8,128)(2,1)S(1)}, bf16[32,4096]{1,0:T(8,128)(2,1)S(1)}, u32[]{:S(2)}, u32[]{:S(2)}) collective-permute-start(bf16[32,4096]{1,0:T(8,128)(2,1)S(1)} %get-tuple-element.387), channel_id=1, source_target_pairs={{0,14},{2,0},{4,2},{6,4},{8,6},{10,8},{12,10},{14,12},{1,15},{3,1}... | collective-permute-start | bytes 786440 | tf_op jit(solution)/shard_map/while/body/ppermute | solution.py:40
  59.2 10.1 %collective-permute-start.4 = (bf16[32,4096]{1,0:T(8,128)(2,1)S(1)}, bf16[32,4096]{1,0:T(8,128)(2,1)S(1)}, u32[]{:S(2)}, u32[]{:S(2)}) collective-permute-start(bf16[32,4096]{1,0:T(8,128)(2,1)S(1)} %collective-permute-done), channel_id=1, source_target_pairs={{0,2},{2,4},{4,6},{6,8},{8,10},{10,12},{12,14},{14,0},{1,3},{3,5},... | collective-permute-start | bytes 786440 | tf_op jit(solution)/shard_map/while/body/ppermute | solution.py:39
  63.6 8.3 %collective-permute-start.5 = (bf16[32,4096]{1,0:T(8,128)(2,1)S(1)}, bf16[32,4096]{1,0:T(8,128)(2,1)S(1)}, u32[]{:S(2)}, u32[]{:S(2)}) collective-permute-start(bf16[32,4096]{1,0:T(8,128)(2,1)S(1)} %collective-permute-done.1), channel_id=1, source_target_pairs={{0,14},{2,0},{4,2},{6,4},{8,6},{10,8},{12,10},{14,12},{1,15},{3,1}... | collective-permute-start | bytes 786440 | tf_op jit(solution)/shard_map/while/body/ppermute | solution.py:40
  69.3 9.5 %collective-permute-start.6 = (bf16[32,4096]{1,0:T(8,128)(2,1)S(1)}, bf16[32,4096]{1,0:T(8,128)(2,1)S(1)}, u32[]{:S(2)}, u32[]{:S(2)}) collective-permute-start(bf16[32,4096]{1,0:T(8,128)(2,1)S(1)} %collective-permute-done.4), channel_id=1, source_target_pairs={{0,2},{2,4},{4,6},{6,8},{8,10},{10,12},{12,14},{14,0},{1,3},{3,5},... | collective-permute-start | bytes 786440 | tf_op jit(solution)/shard_map/while/body/ppermute | solution.py:39
  71.9 8.9 %collective-permute-start.7 = (bf16[32,4096]{1,0:T(8,128)(2,1)S(1)}, bf16[32,4096]{1,0:T(8,128)(2,1)S(1)}, u32[]{:S(2)}, u32[]{:S(2)}) collective-permute-start(bf16[32,4096]{1,0:T(8,128)(2,1)S(1)} %collective-permute-done.5), channel_id=1, source_target_pairs={{0,14},{2,0},{4,2},{6,4},{8,6},{10,8},{12,10},{14,12},{1,15},{3,1}... | collective-permute-start | bytes 786440 | tf_op jit(solution)/shard_map/while/body/ppermute | solution.py:40
  78.8 8.8 %collective-permute-start.8 = (bf16[32,3072]{1,0:T(8,128)(2,1)S(1)}, bf16[32,3072]{1,0:T(8,128)(2,1)S(1)}, u32[]{:S(2)}, u32[]{:S(2)}) collective-permute-start(bf16[32,3072]{1,0:T(8,128)(2,1)S(1)} %slice.90), channel_id=1, source_target_pairs={{0,2},{2,4},{4,6},{6,8},{8,10},{10,12},{12,14},{14,0},{1,3},{3,5},... | collective-permute-start | bytes 589832 | tf_op jit(solution)/shard_map/while/body/ppermute | solution.py:45
  80.8 7.0 %collective-permute-start.9 = (bf16[32,1024]{1,0:T(8,128)(2,1)S(1)}, bf16[32,1024]{1,0:T(8,128)(2,1)S(1)}, u32[]{:S(2)}, u32[]{:S(2)}) collective-permute-start(bf16[32,1024]{1,0:T(8,128)(2,1)S(1)} %slice.91), channel_id=1, source_target_pairs={{0,14},{2,0},{4,2},{6,4},{8,6},{10,8},{12,10},{14,12},{1,15},{3,1}... | collective-permute-start | bytes 196616 | tf_op jit(solution)/shard_map/while/body/ppermute | solution.py:46
  110.5 17.0 %all-to-all-start.2 = ((f32[64,1,128]{2,1,0:T(1,128)}), f32[64,1,128]{2,1,0:T(1,128)S(1)}, u32[]{:S(2)}, u32[]{:S(2)}) async-start(f32[64,1,128]{2,1,0:T(1,128)} %bitcast.4), calls=%async_computation.2 | async-start | bytes 65536 | tf_op jit(solution)/shard_map/all_to_all | solution.py:23
Sparse Core Ops, SparseCore 0:
  10.1 51.2 all-gather.2
  110.6 38.8 reduce-scatter.1
